TPU v7x, 256 devices: a whole 4x4x8 slice. The times are simulated.
256 devices in a mesh: shell: 8 (over x, core), radial: 32 (over z, y).
Axes of the slice: x: 4, y: 4, z: 8, core: 2. Of those that a mesh axis runs over, the one named last changes fastest.
Arguments:
- density: float32 [32, 128, 4096], P('radial', 'shell'), may hold values from -6 to 6
- footprint: int32 [32, 128, 4096], P('radial', 'shell'), may hold values 0 or 1
- cycle_index: int32 [128], P('shell'), may hold values from 2944 to 3071, as said below
- order_values: int32 [64], replicated, may hold values from 0 to 2047, as said below
- block_lengths: int32 [32], replicated, may hold values from 1 to 128, 2048 in all
- legendre: bfloat16 [64, 2048, 128], P('shell'), may hold values from -0.0078125 to 0.0078125
- bessel: bfloat16 [32, 2048, 512], P('radial', None, 'shell'), may hold values from -2 to 2
Outputs:
- sfb: bfloat16 [4096, 512, 128], P('radial', 'shell')
Inputs may be any that keep to these rules, and one draw needn't show every extreme that they name: `order_values`: 64 different orders, 0 and 2047 among them. `cycle_index`: 128 different row numbers forming the contiguous band that ends at row 3071, in any order over the slots.
All inputs are finite; a program needn't handle non-finite values. No bound on the sum of `footprint` on one device may be relied on, other than what follows from the above.
Results may differ from a plain program's by a relative error of at most 0.0049.
The roundings to bfloat16 on the way count: a program that leaves them out, or rounds other values in their place, can miss the bound.
Values may be sent and summed in bfloat16 or wider, within the bound.
No kernel may reach another device: no remote copies, remote signals or barrier semaphores. Data moves between devices by JAX's collectives and lax.ppermute only.
A program may use at most 64 MiB of HBM per device.

v0:
```python
import math

import jax
import jax.numpy as jnp
from jax import lax
from jax.sharding import PartitionSpec as P

NSIDE = 1024


def phase_table(nphi, order_values):
    pixel = lax.iota(jnp.int32, nphi)
    turns = pixel[:, None] * 2 * order_values[None, :] % (2 * nphi)
    angle = turns.astype(jnp.float32) * (math.pi / nphi)
    return jnp.concatenate([jnp.cos(angle), -jnp.sin(angle)], axis=1)


def latitude_twist(cycle_index, order_values, nphi):
    parity = (cycle_index - NSIDE + 1) % 2
    turns = order_values[None, :] * (2 - parity)[:, None] % (2 * nphi)
    angle = turns.astype(jnp.float32) * (math.pi / nphi)
    return (jnp.cos(angle), jnp.sin(angle))


def block_slots(block_lengths, deg, capacity):
    starts = jnp.cumsum(block_lengths) - block_lengths
    offset = lax.iota(jnp.int32, capacity)
    rows = jnp.minimum(starts[:, None] + offset[None, :], deg - 1)
    valid = offset[None, :] < block_lengths[:, None]
    return (rows.reshape(-1), valid.reshape(-1))


def on_device(density, footprint, cycle_index, order_values, block_lengths, legendre, bessel):
    shell_dev, cycle_dev, nphi = density.shape
    orders = order_values.shape[0]
    ord_dev, deg, cycles = legendre.shape
    radial_count = lax.axis_size("radial")
    capacity = 2 * deg // radial_count
    pixels = (density * footprint.astype(jnp.float32)).reshape(shell_dev * cycle_dev, nphi)
    spectra = jnp.dot(pixels, phase_table(nphi, order_values), precision=lax.Precision.HIGHEST)
    spectra = spectra.reshape(shell_dev, cycle_dev, 2, orders)
    cos_t, sin_t = latitude_twist(cycle_index, order_values, nphi)
    real0 = spectra[:, :, 0, :]
    imag0 = spectra[:, :, 1, :]
    real = real0 * cos_t + imag0 * sin_t
    imag = imag0 * cos_t - real0 * sin_t
    four = jnp.stack([real, imag], axis=2).astype(jnp.bfloat16)
    rows, valid = block_slots(block_lengths, deg, capacity)
    radial_send = jnp.take(bessel, rows, axis=1)
    radial_rows = lax.all_to_all(radial_send, "radial", split_axis=1, concat_axis=0, tiled=True)
    by_order = lax.all_to_all(four, "shell", split_axis=3, concat_axis=1, tiled=True)
    harmonic = jnp.einsum("mlr,srcm->smcl", legendre, by_order, preferred_element_type=jnp.float32)
    my_orders = lax.dynamic_slice(order_values, (lax.axis_index("shell") * ord_dev,), (ord_dev,))
    degree = lax.iota(jnp.int32, deg)
    keep = (degree[None, :] >= my_orders[:, None]).astype(jnp.float32)
    harmonic = (harmonic * keep[None, :, None, :]).astype(jnp.bfloat16)
    slot_keep = valid.astype(jnp.bfloat16)
    every_order = lax.all_gather(harmonic, "shell", axis=1, tiled=True)
    send_wide = jnp.take(every_order, rows, axis=3) * slot_keep
    coeffs = lax.all_to_all(send_wide, "radial", split_axis=3, concat_axis=0, tiled=True)
    result = jnp.einsum("skn,smck->kncm", radial_rows, coeffs, preferred_element_type=jnp.float32)
    return result.reshape(capacity, radial_rows.shape[2], 2 * orders).astype(jnp.bfloat16)


def solution(mesh):
    return jax.shard_map(
        on_device,
        mesh=mesh,
        in_specs=(
            P("radial", "shell", None),
            P("radial", "shell", None),
            P("shell"),
            P(),
            P(),
            P("shell", None, None),
            P("radial", None, "shell"),
        ),
        out_specs=P("radial", "shell", None),
        check_vma=False,
    )
```

profile of v0, /device:TPU:1, one launch (start us, length us, event | category | flops | bytes accessed | tf_op | source)
XLA Modules:
  0.0 178.0 jit_solution(8600046202066091926)
XLA Ops:
  0.0 0.7 fusion.20
  0.7 4.8 %fusion.8 = (f32[4096,64]{0,1:T(8,128)S(1)}, f32[4096,64]{0,1:T(8,128)S(1)}) fusion(s32[64]{0:T(128)} %param.10, s32[4096]{0:T(1024)S(1)} %iota_multiply_fusion), kind=kLoop, calls=%fused_computation.22 | loop fusion | flops 3932160 | bytes 2113792 | tf_op jit(solution)/shard_map/cos | solution.py:15
  5.5 0.2 pad_maximum_fusion
  5.7 0.7 copy-done
  6.5 2.5 %convolution_bitcast_fusion = f32[1,16,2,64]{3,1,2,0:T(8,128)S(1)} fusion(f32[2,64,4096]{2,1,0:T(8,128)S(1)} %bitcast.63, f32[1,16,4096]{2,1,0:T(8,128)S(1)} %copy-done, s32[1,16,4096]{2,1,0:T(8,128)S(1)} %copy-done.1), kind=kOutput, calls=%fused_computation.13 | convolution fusion | flops 100794368 | bytes 2629632 | tf_op jit(solution)/shard_map/dot_general | solution.py:40
  9.1 0.1 add_convert_fusion
  9.3 0.7 reshape.376
  10.0 6.5 %all-to-all-start = ((bf16[8,2,128]{2,1,0:T(2,128)(2,1)}), bf16[8,2,128]{2,1,0:T(2,128)(2,1)S(1)}, u32[]{:S(2)}, u32[]{:S(2)}) async-start(bf16[8,2,128]{2,1,0:T(2,128)(2,1)} %reshape.376), calls=%async_computation | async-start | bytes 8192 | tf_op jit(solution)/shard_map/all_to_all | solution.py:51
  16.6 0.1 reduce
  17.1 0.3 copy.53
  17.4 12.1 %gather_fusion.1 = bf16[4096,64]{1,0:T(8,128)(2,1)S(1)} fusion(bf16[2048,64]{1,0:T(8,128)(2,1)S(1)} %bitcast.59, s32[4096]{0:T(1024)S(1)} %broadcast_clamp_fusion), kind=kCustom, calls=%fused_computation.1 | custom fusion | bytes 1064960 | tf_op jit(solution)/shard_map/jit(_take)/gather | solution.py:49
  29.5 2.1 %bitcast_select_fusion.1 = bf16[1,4096,64]{2,1,0:T(8,128)(2,1)S(1)} fusion(bf16[4096,64]{1,0:T(8,128)(2,1)S(1)} %gather_fusion.1, pred[4096]{0:T(1024)(128)(4,1)S(1)} %compare_and_fusion), kind=kLoop, calls=%fused_computation.20 | loop fusion | flops 262144 | bytes 1052672 | tf_op jit(solution)/shard_map/jit(_take)/select_n | solution.py:49
  31.8 16.7 %copy.75 = bf16[1,4096,64]{2,0,1:T(2,128)(2,1)S(1)} copy(bf16[1,4096,64]{2,1,0:T(8,128)(2,1)S(1)} %bitcast_select_fusion.1) | data formatting | bytes 1048576 | tf_op jit(solution)/shard_map/jit(_take)/select_n | solution.py:49
  48.4 0.5 broadcast.315
  49.0 22.4 %reduce.1 = bf16[4096,64]{1,0:T(8,128)(2,1)S(1)} reduce(bf16[4096,1,64]{2,1,0:T(2,128)(2,1)S(1)} %bitcast.65, bf16[]{:T(256)} %broadcast.315), dimensions={1}, to_apply=%bitcast.58.reduce_sub_computation | reduce | bytes 1048578
  71.4 1.5 reshape.380
  72.9 10.7 %all-to-all-start.2 = ((bf16[32,2,4096]{2,1,0:T(2,128)(2,1)}), bf16[32,2,4096]{2,1,0:T(2,128)(2,1)}, u32[]{:S(2)}, u32[]{:S(2)}) async-start(bf16[32,2,4096]{2,1,0:T(2,128)(2,1)} %reshape.380), calls=%async_computation.2 | async-start | bytes 1048576 | tf_op jit(solution)/shard_map/all_to_all | solution.py:50
  83.8 3.4 %fusion = bf16[8,2,2048]{2,1,0:T(2,128)(2,1)S(1)} fusion(bf16[128,2,8]{0,1,2:T(2,128)(2,1)S(1)} %reshape.348, bf16[8,2048,128]{2,1,0:T(8,128)(2,1)} %param.12, f32[8,2048]{1,0:T(8,128)S(1)} %fusion.12), kind=kOutput, calls=%fused_computation.4 | convolution fusion | flops 8454144 | bytes 4329472 | tf_op jit(solution)/shard_map/mlr,srcm->smcl/dot_general | solution.py:52
  87.2 14.1 %all-gather = bf16[64,2,2048]{2,1,0:T(2,128)(2,1)S(1)} all-gather(bf16[8,2,2048]{2,1,0:T(2,128)(2,1)S(1)} %fusion), channel_id=2, replica_groups=mesh['shell'=8,'radial'=32] {'shell'}, dimensions={0}, use_global_device_ids=true | all-gather | bytes 589824 | tf_op jit(solution)/shard_map/all_gather | solution.py:58
  101.3 0.9 copy.48
  102.2 13.8 %gather_fusion = bf16[4096,64,2]{1,2,0:T(2,128)(2,1)S(1)} fusion(bf16[64,2,2048]{0,1,2:T(2,128)(2,1)S(1)} %copy.48, s32[4096]{0:T(1024)S(1)} %broadcast_clamp_fusion), kind=kCustom, calls=%fused_computation | custom fusion | bytes 2113536 | tf_op jit(solution)/shard_map/jit(_take)/gather | solution.py:59
  115.9 2.5 %copy.49 = bf16[4096,64,2]{0,1,2:T(8,128)(2,1)S(1)} copy(bf16[4096,64,2]{1,2,0:T(2,128)(2,1)S(1)} %gather_fusion) | data formatting | bytes 2097152 | tf_op jit(solution)/shard_map/jit(_take)/gather | solution.py:59
  118.5 1.1 fusion.6
  119.6 5.0 %copy.50 = bf16[1,64,2,4096]{1,2,0,3:T(2,128)(2,1)S(1)} copy(bf16[1,64,2,4096]{3,1,2,0:T(8,128)(2,1)} %fusion.6) | data formatting | bytes 2097152 | tf_op jit(solution)/shard_map/mul | solution.py:59
  124.6 2.2 %reshape.378 = bf16[32,2,8192]{2,1,0:T(2,128)(2,1)} reshape(bf16[4096,1,2,64]{3,2,1,0:T(2,128)(2,1)S(1)} %bitcast.64) | data formatting | bytes 2097152
  126.9 9.6 %all-to-all-start.1 = ((bf16[32,2,8192]{2,1,0:T(2,128)(2,1)}), bf16[32,2,8192]{2,1,0:T(2,128)(2,1)}, u32[]{:S(2)}, u32[]{:S(2)}) async-start(bf16[32,2,8192]{2,1,0:T(2,128)(2,1)} %reshape.378), calls=%async_computation.1 | async-start | bytes 2097152 | tf_op jit(solution)/shard_map/all_to_all | solution.py:60
  136.4 4.1 %reshape.381 = bf16[4096,1,64]{2,1,0:T(2,128)(2,1)S(1)} reshape(bf16[32,2,4096]{2,1,0:T(2,128)(2,1)} %all-to-all-done.2) | data formatting | bytes 1048576
  140.6 0.1 copy.65
  140.7 22.8 %all-to-all-done.1 = bf16[32,2,8192]{2,1,0:T(2,128)(2,1)} async-done(((bf16[32,2,8192]{2,1,0:T(2,128)(2,1)}), bf16[32,2,8192]{2,1,0:T(2,128)(2,1)}, u32[]{:S(2)}, u32[]{:S(2)}) %all-to-all-start.1) | async-done | bytes 1048608 | tf_op jit(solution)/shard_map/all_to_all | solution.py:60
  163.5 5.0 %reshape.379 = bf16[4096,1,2,64]{3,2,1,0:T(2,128)(2,1)S(1)} reshape(bf16[32,2,8192]{2,1,0:T(2,128)(2,1)} %all-to-all-done.1) | data formatting | bytes 2097152
  168.5 4.7 %convolution_convert_fusion = bf16[128,64,2,64]{3,1,2,0:T(8,128)(2,1)} fusion(bf16[1,64,2,32,128]{1,2,4,3,0:T(2,128)(2,1)S(1)} %bitcast.61, bf16[32,128,64,1]{2,1,0,3:T(8,128)(2,1)S(1)} %bitcast.66), kind=kOutput, calls=%fused_computation.2 | convolution fusion | flops 68157440 | bytes 3670016 | tf_op jit(solution)/shard_map/skn,smck->kncm/dot_general | solution.py:61
  173.2 4.8 %copy.57 = bf16[128,64,128]{2,1,0:T(8,128)(2,1)} copy(bf16[128,64,128]{1,2,0:T(8,128)(2,1)} %bitcast.60) | data formatting | bytes 4194304 | tf_op jit(solution)/shard_map/convert_element_type | solution.py:62
  (28 shorter events, 1.0 us)
Async XLA Ops:
  5.5 1.0 copy-start
  5.5 1.0 copy-start.1
  5.7 3.4 %copy-start.3 = (s32[64]{0:T(128)S(1)}, s32[64]{0:T(128)}, u32[]{:S(2)}) copy-start(s32[64]{0:T(128)} %param.10) | copy-start | bytes 772
  5.7 10.8 %copy-start.4 = (s32[32]{0:T(128)S(1)}, s32[32]{0:T(128)}, u32[]{:S(2)}) copy-start(s32[32]{0:T(128)} %param.11) | copy-start | bytes 388
  5.7 11.4 %copy-start.2 = (bf16[1,2048,64]{1,2,0:T(8,128)(2,1)S(1)}, bf16[1,2048,64]{1,2,0:T(8,128)(2,1)}, u32[]{:S(2)}) copy-start(bf16[1,2048,64]{1,2,0:T(8,128)(2,1)} %param.13) | copy-start | bytes 786436
  10.0 62.9 %all-to-all-start = ((bf16[8,2,128]{2,1,0:T(2,128)(2,1)}), bf16[8,2,128]{2,1,0:T(2,128)(2,1)S(1)}, u32[]{:S(2)}, u32[]{:S(2)}) async-start(bf16[8,2,128]{2,1,0:T(2,128)(2,1)} %reshape.376), calls=%async_computation | async-start | bytes 8192 | tf_op jit(solution)/shard_map/all_to_all | solution.py:51
  72.9 54.0 %all-to-all-start.2 = ((bf16[32,2,4096]{2,1,0:T(2,128)(2,1)}), bf16[32,2,4096]{2,1,0:T(2,128)(2,1)}, u32[]{:S(2)}, u32[]{:S(2)}) async-start(bf16[32,2,4096]{2,1,0:T(2,128)(2,1)} %reshape.380), calls=%async_computation.2 | async-start | bytes 1048576 | tf_op jit(solution)/shard_map/all_to_all | solution.py:50
  126.9 36.6 %all-to-all-start.1 = ((bf16[32,2,8192]{2,1,0:T(2,128)(2,1)}), bf16[32,2,8192]{2,1,0:T(2,128)(2,1)}, u32[]{:S(2)}, u32[]{:S(2)}) async-start(bf16[32,2,8192]{2,1,0:T(2,128)(2,1)} %reshape.378), calls=%async_computation.1 | async-start | bytes 2097152 | tf_op jit(solution)/shard_map/all_to_all | solution.py:60
where the time goes:
time: 179 us; the launch traced here: 178 us
  local copies, waits for them, and re-layouts  71.7 us (40%)
  other arithmetic  31.9 us (18%)
  starting transfers between devices  26.7 us (15%)
  waiting for transfers between devices  22.8 us (13%)
  blocking collectives  14.1 us (8%)
  matrix products  10.6 us (6%)
    all_to_all x1, waiting for transfers between devices, on_device(): lax.all_to_all(send_wide, 'radial', split_axis=3, concat_axis=0, tiled=True)  22.8 us
    unnamed x1, other arithmetic  22.4 us
    select_n x1, local copies, waits for them, and re-layouts, on_device(): radial_send = jnp.take(bessel, rows, axis=1)  16.7 us
    gather x2, local copies, waits for them, and re-layouts, on_device(): send_wide = jnp.take(every_order, rows, axis=3) * slot_keep  16.3 us
    unnamed x19, local copies, waits for them, and re-layouts  15.5 us
    all_gather x1, blocking collectives, on_device(): every_order = lax.all_gather(harmonic, 'shell', axis=1, tiled=True)  14.1 us
    gather x1, local copies, waits for them, and re-layouts, on_device(): radial_send = jnp.take(bessel, rows, axis=1)  12.1 us
    all_to_all x1, starting transfers between devices, on_device(): lax.all_to_all(radial_send, 'radial', split_axis=1, concat_axis=0, tiled=...  10.7 us
  transfers between devices with their start and end apart: 3, of which 1 were waited for; matrix products, arithmetic and copies ran while one was open for 50% of the time, Pallas kernels for 0%

commit v1 on v0

v1 whole, which is shorter than its diff:
```python
import math

import jax
import jax.numpy as jnp
from jax import lax
from jax.experimental import pallas as pl
from jax.experimental.pallas import tpu as pltpu
from jax.sharding import PartitionSpec as P

NSIDE = 1024
F32 = jnp.float32
BF16 = jnp.bfloat16
VMEM_LIMIT = 40 * 1024 * 1024

SMEM_SPEC = pl.BlockSpec(memory_space=pltpu.SMEM)
VMEM_SPEC = pl.BlockSpec(memory_space=pltpu.VMEM)
ANY_SPEC = pl.BlockSpec(memory_space=pl.ANY)


def params():
    return pltpu.CompilerParams(vmem_limit_bytes=VMEM_LIMIT)


def cos_sin(turns):
    quarter = (turns + 1024) >> 11
    x = (turns - (quarter << 11)).astype(F32) * (math.pi / 4096)
    z = x * x
    s = x + x * z * (-1.6666654611e-1 + z * (8.3321608736e-3 + z * -1.9515295891e-4))
    c = 1.0 - 0.5 * z + z * z * (4.166664568298827e-2 + z * (-1.388731625493765e-3 + z * 2.443315711809948e-5))
    odd = (quarter & 1) == 1
    even_sign = jnp.where((quarter & 2) == 2, -1.0, 1.0)
    cos = jnp.where(odd, -s, c) * even_sign
    sin = jnp.where(odd, c, s) * even_sign
    return cos, sin


def dft_kernel(where_ref, cycle_ref, order_ref, density_ref, footprint_ref, out_ref):
    rows, nphi = density_ref.shape
    order = order_ref[...]
    lane = lax.broadcasted_iota(jnp.int32, (1, 128), 1)
    part = (lane >> 3) & 1
    sixty_four = lax.broadcasted_iota(jnp.int32, (64, 128), 0)
    pa, qa = cos_sin((sixty_four * 128 * order + 2048 * part) & 8191)
    qa = -qa
    cb, sb = cos_sin((sixty_four * 2 * order) & 8191)
    total = jnp.zeros((2 * rows, 256), F32)
    for chunk in range(nphi // 256):
        tables = []
        for a in range(4 * chunk, 4 * chunk + 4):
            tables.append(pa[a : a + 1] * cb + qa[a : a + 1] * sb)
        table = jnp.concatenate(tables, axis=0)
        high = table.astype(BF16)
        low = (table - high.astype(F32)).astype(BF16)
        cut = slice(256 * chunk, 256 * chunk + 256)
        pixels = density_ref[:, cut] * footprint_ref[:, cut].astype(F32)
        p_high = pixels.astype(BF16)
        p_low = (pixels - p_high.astype(F32)).astype(BF16)
        total = total + jnp.dot(
            jnp.concatenate([p_high, p_low], axis=0),
            jnp.concatenate([high, low], axis=1),
            preferred_element_type=F32,
        )
    x = total[:rows, :128] + (total[:rows, 128:] + total[rows:, :128])
    row = lax.broadcasted_iota(jnp.int32, (rows, 128), 0)
    cycle = jnp.zeros((rows, 128), jnp.int32)
    for r in range(rows):
        cycle = jnp.where(row == r, cycle_ref[r], cycle)
    parity = (cycle - (NSIDE - 1)) & 1
    cos_t, sin_t = cos_sin((order * (2 - parity)) & 8191)
    other = jnp.where(part == 0, pltpu.roll(x, 120, 1), -pltpu.roll(x, 8, 1))
    four = (x * cos_t + other * sin_t).astype(BF16)
    lanes = lax.broadcasted_iota(jnp.int32, (rows, 128), 1)
    place = (lanes == row + rows * where_ref[1]).astype(BF16)
    out_ref[...] = lax.dot_general(four, place, (((0,), (0,)), ((), ())), preferred_element_type=F32).astype(BF16)


def send_kernel(lengths_ref, bessel_ref, out_ref, wide_ref):
    deg, modes = bessel_ref.shape
    blocks = out_ref.shape[0]
    wide_ref[pl.ds(0, deg), pl.ds(0, modes)] = bessel_ref[...].astype(F32)
    wide_ref[pl.ds(deg, 128), :] = jnp.zeros((128, 128), F32)

    def step(k, start):
        low = wide_ref[pl.ds(start, 64), :]
        high = wide_ref[pl.ds(start + 64, 64), :]
        lane = lax.broadcasted_iota(jnp.int32, (64, 128), 1)
        out_ref[k] = jnp.where(lane < 64, low, pltpu.roll(high, 64, 1)).astype(BF16)
        return start + lengths_ref[k]

    lax.fori_loop(0, blocks, step, jnp.int32(0))


def block_start(lengths_ref, block):
    return lax.fori_loop(0, block, lambda k, total: total + lengths_ref[k], jnp.int32(0))


def rows_kernel(where_ref, lengths_ref, legendre_ref, out_ref, window_ref, wide_ref, sem):
    deg = legendre_ref.shape[1]
    window = window_ref.shape[1]
    start = block_start(lengths_ref, where_ref[0])
    base = jnp.minimum((start // 16) * 16, deg - window)
    base = pl.multiple_of(base, 16)
    copy = pltpu.make_async_copy(legendre_ref.at[:, pl.ds(base, window), :], window_ref, sem)
    copy.start()
    copy.wait()
    shift = start - base
    wide_ref[pl.ds(window, 128), :] = jnp.zeros((128, 128), F32)
    for q in range(out_ref.shape[0]):
        wide_ref[pl.ds(0, window), :] = window_ref[q].astype(F32)
        out_ref[q] = wide_ref[pl.ds(shift, 128), :].astype(BF16)


def harmonic_kernel(where_ref, lengths_ref, order_ref, four_ref, rows_ref, out_ref, four32_ref, out32_ref):
    four32_ref[...] = four_ref[...].astype(F32)
    start = block_start(lengths_ref, where_ref[0])
    lane = lax.broadcasted_iota(jnp.int32, (32, 128), 1)
    degree = start + lax.broadcasted_iota(jnp.int32, (32, 128), 0) + 32 * (lane >> 5)
    group = lane >> 5
    for q in range(8):
        order = order_ref[8 * where_ref[1] + q]
        for c in range(2):
            one = four32_ref[pl.ds(c * 8 + q, 32, stride=16), :]
            four = jnp.concatenate([one] * 4, axis=0).astype(BF16)
            full = lax.dot_general(rows_ref[q], four, (((1,), (1,)), ((), ())), preferred_element_type=F32)
            packed = full[96:128]
            for j in range(3):
                packed = jnp.where(group == j, full[32 * j : 32 * j + 32], packed)
            packed = jnp.where(degree >= order, packed, 0.0)
            out32_ref[pl.ds(c * 8 + q, 32, stride=16), :] = packed
    out_ref[...] = out32_ref[...].astype(BF16)


def radial_kernel(where_ref, lengths_ref, recv_ref, out_ref, wide_ref):
    length = lengths_ref[where_ref[0]]
    wide_ref[...] = recv_ref[...].astype(F32)
    half = lax.broadcasted_iota(jnp.int32, (32, 128), 1) >> 6
    zero = jnp.zeros((32, 128), F32)

    def step(g, carry):
        turned = []
        for odd in range(2):
            x = wide_ref[pl.ds(g + 32 * odd, 32, stride=64), :]
            p = 64 * half + 32 * odd + g
            x = jnp.where(p < length, x, 0.0)
            low = jnp.where(half == 0, x, 0.0)
            high = jnp.where(half == 1, x, 0.0)
            pieces = [zero, low, zero, high] if odd else [low, zero, high, zero]
            turned.append(jnp.transpose(jnp.concatenate(pieces, axis=0)))
        even, other = turned
        out_ref[g] = jnp.concatenate([even[:64], other[:64], even[64:], other[64:]], axis=0).astype(BF16)
        return carry

    lax.fori_loop(0, 32, step, 0)


def final_kernel(radial_ref, harmonic_ref, out_ref):
    for g in range(radial_ref.shape[0]):
        h = harmonic_ref[:, g].astype(F32)
        right = jnp.concatenate([h[:, :8].reshape(64, 128), h[:, 8:].reshape(64, 128)], axis=0).astype(BF16)
        result = lax.dot_general(radial_ref[g], right, (((1,), (1,)), ((), ())), preferred_element_type=F32)
        out_ref[:, g] = result.reshape(4, 64, 128).astype(BF16)


def on_device(density, footprint, cycle_index, order_values, block_lengths, legendre, bessel):
    shape = jax.ShapeDtypeStruct
    rows, nphi = density.shape[1:]
    deg, modes = bessel.shape[1:]
    where = jnp.stack([lax.axis_index("radial"), lax.axis_index("shell")]).astype(jnp.int32)
    order_lanes = jnp.broadcast_to(order_values.reshape(8, 1, 8), (8, 2, 8)).reshape(1, 128)

    four = pl.pallas_call(
        dft_kernel,
        out_shape=shape((128, 128), BF16),
        in_specs=[SMEM_SPEC, SMEM_SPEC, VMEM_SPEC, VMEM_SPEC, VMEM_SPEC],
        out_specs=VMEM_SPEC,
        compiler_params=params(),
        name="dft",
    )(where, cycle_index, order_lanes, density.reshape(rows, nphi), footprint.reshape(rows, nphi))

    send = pl.pallas_call(
        send_kernel,
        out_shape=shape((32, 64, 128), BF16),
        in_specs=[SMEM_SPEC, VMEM_SPEC],
        out_specs=VMEM_SPEC,
        scratch_shapes=[pltpu.VMEM((deg + 128, 128), F32)],
        compiler_params=params(),
        name="bessel_send",
    )(block_lengths, bessel.reshape(deg, modes))
    recv = lax.all_to_all(send, "radial", split_axis=0, concat_axis=0, tiled=True)

    leg_rows = pl.pallas_call(
        rows_kernel,
        out_shape=shape((8, 128, 128), BF16),
        in_specs=[SMEM_SPEC, SMEM_SPEC, ANY_SPEC],
        out_specs=VMEM_SPEC,
        scratch_shapes=[pltpu.VMEM((8, 144, 128), BF16), pltpu.VMEM((144 + 128, 128), F32), pltpu.SemaphoreType.DMA],
        compiler_params=params(),
        name="legendre_rows",
    )(where, block_lengths, legendre)

    by_order = lax.all_to_all(four.reshape(8, 16, 128), "shell", split_axis=0, concat_axis=0, tiled=True)
    mine = jnp.sum(by_order, axis=0, dtype=F32).astype(BF16)
    every_shell = lax.all_to_all(jnp.broadcast_to(mine[None], (32, 16, 128)), "radial", split_axis=0, concat_axis=0, tiled=True)

    harmonic = pl.pallas_call(
        harmonic_kernel,
        out_shape=shape((512, 128), BF16),
        in_specs=[SMEM_SPEC, SMEM_SPEC, SMEM_SPEC, VMEM_SPEC, VMEM_SPEC],
        out_specs=VMEM_SPEC,
        scratch_shapes=[pltpu.VMEM((512, 128), F32), pltpu.VMEM((512, 128), F32)],
        compiler_params=params(),
        name="harmonic",
    )(where, block_lengths, order_values, every_shell.reshape(512, 128), leg_rows)
    every_order = lax.all_to_all(jnp.broadcast_to(harmonic[None], (8, 512, 128)), "shell", split_axis=0, concat_axis=0, tiled=True)

    radial = pl.pallas_call(
        radial_kernel,
        out_shape=shape((32, 256, 128), BF16),
        in_specs=[SMEM_SPEC, SMEM_SPEC, VMEM_SPEC],
        out_specs=VMEM_SPEC,
        scratch_shapes=[pltpu.VMEM((2048, 128), F32)],
        compiler_params=params(),
        name="radial_rows",
    )(where, block_lengths, recv.reshape(2048, 128))

    step = 4
    out = pl.pallas_call(
        final_kernel,
        out_shape=shape((4, 32, 64, 128), BF16),
        grid=(32 // step,),
        in_specs=[
            pl.BlockSpec((step, 256, 128), lambda g: (g, 0, 0)),
            pl.BlockSpec((8, step, 16, 128), lambda g: (0, g, 0, 0)),
        ],
        out_specs=pl.BlockSpec((4, step, 64, 128), lambda g: (0, g, 0, 0)),
        compiler_params=params(),
        name="combine",
    )(radial, every_order.reshape(8, 32, 16, 128))
    return out.reshape(128, modes, 128)


def solution(mesh):
    return jax.shard_map(
        on_device,
        mesh=mesh,
        in_specs=(
            P("radial", "shell", None),
            P("radial", "shell", None),
            P("shell"),
            P(),
            P(),
            P("shell", None, None),
            P("radial", None, "shell"),
        ),
        out_specs=P("radial", "shell", None),
        check_vma=False,
    )
```

time: 179 us -> 85.3 us (0.48)
  local copies, waits for them, and re-layouts: 71.7 us -> 10.3 us
  other arithmetic: 31.9 us -> 0.09 us
  Pallas kernels: 0 us -> 15.9 us
  matrix products: 10.6 us -> 0 us
  blocking collectives: 14.1 us -> 10.3 us
  starting transfers between devices: 26.7 us -> 23.7 us
    gather x3 -> x0, local copies, waits for them, and re-layouts: 28.4 us -> none  [the longest x2 16.3 us: on_device(): send_wide = jnp.take(every_order, rows, axis=3) * slot_keep]
    unnamed x1 -> x0, other arithmetic: 22.4 us -> none
    select_n x1 -> x0, local copies, waits for them, and re-layouts: 16.7 us -> none  [on_device(): radial_send = jnp.take(bessel, rows, axis=1)]
    pallas_call x0 -> x6, Pallas kernels: none -> 15.9 us  [the longest x1 4.65 us: on_device(): pl.pallas_call(radial_kernel, out_shape=shape((32, 256, 128), BF16), in_s...]
    all_gather x1 -> x0, blocking collectives: 14.1 us -> none  [on_device(): every_order = lax.all_gather(harmonic, 'shell', axis=1, tiled=True)]
    dot_general x3 -> x0, matrix products: 10.6 us -> none  [the longest x1 4.74 us: on_device(): jnp.einsum('skn,smck->kncm', radial_rows, coeffs, preferred_element_type=...]
    all_to_all x0 -> x1, blocking collectives: none -> 10.3 us  [on_device(): lax.all_to_all(four.reshape(8, 16, 128), 'shell', split_axis=0, concat_ax...]
    unnamed x19, local copies, waits for them, and re-layouts: 15.5 us -> 7.67 us
  transfers between devices with their start and end apart: 3 -> 3, of which waited for: 1 -> 3; matrix products, arithmetic and copies ran while one was open for 50% -> 1% of each run, Pallas kernels for 0% -> 12%
where the time goes in v1:
time: 85.3 us; the launch traced here: 84.8 us
  waiting for transfers between devices  24.4 us (29%)
  starting transfers between devices  23.7 us (28%)
  Pallas kernels  15.9 us (19%)
  local copies, waits for them, and re-layouts  10.3 us (12%)
  blocking collectives  10.3 us (12%)
    all_to_all x1, waiting for transfers between devices, on_device(): lax.all_to_all(send, 'radial', split_axis=0, concat_axis=0, tiled=True)  11.4 us
    all_to_all x1, starting transfers between devices, on_device(): lax.all_to_all(jnp.broadcast_to(mine[None], (32, 16, 128)), 'radial', spl...  11.2 us
    all_to_all x1, blocking collectives, on_device(): lax.all_to_all(four.reshape(8, 16, 128), 'shell', split_axis=0, concat_ax...  10.3 us
    all_to_all x1, waiting for transfers between devices, on_device(): lax.all_to_all(jnp.broadcast_to(harmonic[None], (8, 512, 128)), 'shell',...  9.42 us
    unnamed x19, local copies, waits for them, and re-layouts  7.67 us
    all_to_all x1, starting transfers between devices, on_device(): lax.all_to_all(jnp.broadcast_to(harmonic[None], (8, 512, 128)), 'shell',...  6.84 us
    all_to_all x1, starting transfers between devices, on_device(): lax.all_to_all(send, 'radial', split_axis=0, concat_axis=0, tiled=True)  5.64 us
    pallas_call x1, Pallas kernels, on_device(): pl.pallas_call(radial_kernel, out_shape=shape((32, 256, 128), BF16), in_s...  4.65 us
  transfers between devices with their start and end apart: 3, of which 3 were waited for; matrix products, arithmetic and copies ran while one was open for 1% of the time, Pallas kernels for 12%

profile of v1, /device:TPU:1, one launch (start us, length us, event | category | flops | bytes accessed | tf_op | source)
XLA Modules:
  0.0 84.8 jit_solution(12925883665409039329)
XLA Ops:
  0.0 0.7 broadcast_in_dim.8
  0.7 0.1 reshape.33.order_ref
  0.8 0.1 pad_add_fusion.where_ref
  0.9 0.0 copy-start.3
  0.9 0.9 %copy-done.3 = f32[1,16,4096]{2,1,0:T(8,128)S(1)} copy-done((f32[1,16,4096]{2,1,0:T(8,128)S(1)}, f32[1,16,4096]{2,1,0:T(8,128)}, u32[]{:S(2)}) %copy-start.3) | copy-done | bytes 262168
  1.9 0.0 copy-start.4
  1.9 0.9 %copy-done.4 = s32[1,16,4096]{2,1,0:T(8,128)S(1)} copy-done((s32[1,16,4096]{2,1,0:T(8,128)S(1)}, s32[1,16,4096]{2,1,0:T(8,128)}, u32[]{:S(2)}) %copy-start.4) | copy-done | bytes 262168
  2.8 0.7 copy-done.8
  3.5 1.5 %dft.1 = bf16[128,128]{1,0:T(8,128)(2,1)S(1)} custom-call(s32[2]{0:T(128)S(1)} %pad_add_fusion.where_ref, s32[16]{0:T(128)S(1)} %copy-done.8, s32[1,128]{1,0:T(1,128)S(1)} %reshape.33.order_ref, f32[16,4096]{1,0:T(8,128)S(1)} %bitcast.14, s32[16,4096]{1,0:T(8,128)S(1)} %bitcast.15), custom_call_target="tpu_custom_call" | custom-call | tf_op jit(solution)/shard_map/dft/pallas_call | solution.py:171
  5.0 10.3 %all_to_all.20 = bf16[8,16,128]{2,1,0:T(8,128)(2,1)S(1)} all-to-all(bf16[8,16,128]{2,1,0:T(8,128)(2,1)S(1)} %bitcast.16), channel_id=1, replica_groups=mesh['shell'=8,'radial'=32] {'shell'}, dimensions={0} | all-to-all | bytes 65536 | tf_op jit(solution)/shard_map/all_to_all | solution.py:201
  15.3 0.7 broadcast_in_dim.10
  16.0 11.2 %all-to-all-start.2 = ((bf16[32,16,128]{2,1,0:T(8,128)(2,1)}), bf16[32,16,128]{2,1,0:T(8,128)(2,1)S(1)}, u32[]{:S(2)}, u32[]{:S(2)}) async-start(bf16[32,16,128]{2,1,0:T(8,128)(2,1)} %broadcast_in_dim.10), calls=%async_computation.2 | async-start | bytes 262144 | tf_op jit(solution)/shard_map/all_to_all | solution.py:203
  27.2 1.2 %copy.8 = bf16[1,2048,64]{2,1,0:T(8,128)(2,1)S(1)} copy(bf16[1,2048,64]{1,2,0:T(8,128)(2,1)} %param.13) | data formatting | bytes 524288 | tf_op args[6]
  28.4 0.0 copy-start.5
  28.4 0.6 copy-done.5
  29.1 3.9 %bessel_send.1 = bf16[32,64,128]{2,1,0:T(8,128)(2,1)} custom-call(s32[32]{0:T(128)S(1)} %copy-done.5, bf16[2048,64]{1,0:T(8,128)(2,1)S(1)} %bitcast.12), custom_call_target="tpu_custom_call" | custom-call | tf_op jit(solution)/shard_map/bessel_send/pallas_call | solution.py:180
  33.0 3.6 %all-to-all-done.2 = bf16[32,16,128]{2,1,0:T(8,128)(2,1)S(1)} async-done(((bf16[32,16,128]{2,1,0:T(8,128)(2,1)}), bf16[32,16,128]{2,1,0:T(8,128)(2,1)S(1)}, u32[]{:S(2)}, u32[]{:S(2)}) %all-to-all-start.2) | async-done | bytes 131104 | tf_op jit(solution)/shard_map/all_to_all | solution.py:203
  36.5 5.6 %all-to-all-start = ((bf16[32,64,128]{2,1,0:T(8,128)(2,1)}), bf16[32,64,128]{2,1,0:T(8,128)(2,1)S(1)}, u32[]{:S(2)}, u32[]{:S(2)}) async-start(bf16[32,64,128]{2,1,0:T(8,128)(2,1)} %bessel_send.1), calls=%async_computation | async-start | bytes 1048576 | tf_op jit(solution)/shard_map/all_to_all | solution.py:189
  42.2 0.0 copy-start
  42.2 2.2 %copy-done = bf16[8,2048,128]{2,1,0:T(8,128)(2,1)S(1)} copy-done((bf16[8,2048,128]{2,1,0:T(8,128)(2,1)S(1)}, bf16[8,2048,128]{2,1,0:T(8,128)(2,1)}, u32[]{:S(2)}) %copy-start) | copy-done | bytes 4194328
  44.4 0.7 legendre_rows.1.rows_ref
  45.1 0.0 copy-done.6
  45.1 0.0 copy-done.7
  45.1 1.1 %harmonic.1 = bf16[512,128]{1,0:T(8,128)(2,1)S(1)} custom-call(s32[2]{0:T(128)S(1)} %pad_add_fusion.where_ref, s32[32]{0:T(128)S(1)} %copy-done.6, s32[64]{0:T(128)S(1)} %copy-done.7, bf16[512,128]{1,0:T(8,128)(2,1)S(1)} %bitcast.13, bf16[8,128,128]{2,1,0:T(8,128)(2,1)S(1)} %legendre_rows.1.rows_ref), custom_call_target="tpu_custom_call" | custom-call | tf_op jit(solution)/shard_map/harmonic/pallas_call | solution.py:205
  46.2 11.4 %all-to-all-done = bf16[32,64,128]{2,1,0:T(8,128)(2,1)S(1)} async-done(((bf16[32,64,128]{2,1,0:T(8,128)(2,1)}), bf16[32,64,128]{2,1,0:T(8,128)(2,1)S(1)}, u32[]{:S(2)}, u32[]{:S(2)}) %all-to-all-start) | async-done | bytes 524320 | tf_op jit(solution)/shard_map/all_to_all | solution.py:189
  57.6 1.1 %broadcast_in_dim.22 = bf16[8,512,128]{2,1,0:T(8,128)(2,1)} broadcast(bf16[512,128]{1,0:T(8,128)(2,1)S(1)} %harmonic.1), dimensions={1,2} | broadcast | bytes 1179648 | tf_op jit(solution)/shard_map/broadcast_in_dim | solution.py:214
  58.8 6.8 %all-to-all-start.3 = ((bf16[8,512,128]{2,1,0:T(8,128)(2,1)}), bf16[8,512,128]{2,1,0:T(8,128)(2,1)S(1)}, u32[]{:S(2)}, u32[]{:S(2)}) async-start(bf16[8,512,128]{2,1,0:T(8,128)(2,1)} %broadcast_in_dim.22), calls=%async_computation.3 | async-start | bytes 2097152 | tf_op jit(solution)/shard_map/all_to_all | solution.py:214
  65.6 0.0 copy-done.1
  65.6 1.0 %copy-done.2 = bf16[32,64,128]{2,1,0:T(8,128)(2,1)S(1)} copy-done((bf16[32,64,128]{2,1,0:T(8,128)(2,1)S(1)}, bf16[32,64,128]{2,1,0:T(8,128)(2,1)}, u32[]{:S(2)}) %copy-start.2) | copy-done | bytes 524312
  66.7 4.6 %radial_rows.1.radial_ref = bf16[32,256,128]{2,1,0:T(8,128)(2,1)S(1)} custom-call(s32[2]{0:T(128)S(1)} %pad_add_fusion.where_ref, s32[32]{0:T(128)S(1)} %copy-done.6, bf16[2048,128]{1,0:T(8,128)(2,1)S(1)} %bitcast.11), custom_call_target="tpu_custom_call" | custom-call | tf_op jit(solution)/shard_map/radial_rows/pallas_call | solution.py:216
  71.3 9.4 %all-to-all-done.3 = bf16[8,512,128]{2,1,0:T(8,128)(2,1)S(1)} async-done(((bf16[8,512,128]{2,1,0:T(8,128)(2,1)}), bf16[8,512,128]{2,1,0:T(8,128)(2,1)S(1)}, u32[]{:S(2)}, u32[]{:S(2)}) %all-to-all-start.3) | async-done | bytes 1048608 | tf_op jit(solution)/shard_map/all_to_all | solution.py:214
  80.7 4.1 %combine.1 = bf16[4,32,64,128]{3,2,1,0:T(8,128)(2,1)} custom-call(bf16[32,256,128]{2,1,0:T(8,128)(2,1)S(1)} %radial_rows.1.radial_ref, bf16[8,32,16,128]{3,2,1,0:T(8,128)(2,1)S(1)} %bitcast.10), custom_call_target="tpu_custom_call" | custom-call | tf_op jit(solution)/shard_map/combine/pallas_call | solution.py:227
  (7 shorter events, 0.0 us)
Async XLA Ops:
  0.9 1.0 %copy-start.3 = (f32[1,16,4096]{2,1,0:T(8,128)S(1)}, f32[1,16,4096]{2,1,0:T(8,128)}, u32[]{:S(2)}) copy-start(f32[1,16,4096]{2,1,0:T(8,128)} %param.7) | copy-start | bytes 786436
  1.9 0.9 %copy-start.4 = (s32[1,16,4096]{2,1,0:T(8,128)S(1)}, s32[1,16,4096]{2,1,0:T(8,128)}, u32[]{:S(2)}) copy-start(s32[1,16,4096]{2,1,0:T(8,128)} %param.8) | copy-start | bytes 786436
  2.8 0.7 copy-start.8
  16.0 20.6 %all-to-all-start.2 = ((bf16[32,16,128]{2,1,0:T(8,128)(2,1)}), bf16[32,16,128]{2,1,0:T(8,128)(2,1)S(1)}, u32[]{:S(2)}, u32[]{:S(2)}) async-start(bf16[32,16,128]{2,1,0:T(8,128)(2,1)} %broadcast_in_dim.10), calls=%async_computation.2 | async-start | bytes 262144 | tf_op jit(solution)/shard_map/all_to_all | solution.py:203
  28.4 0.7 copy-start.5
  36.5 21.1 %all-to-all-start = ((bf16[32,64,128]{2,1,0:T(8,128)(2,1)}), bf16[32,64,128]{2,1,0:T(8,128)(2,1)S(1)}, u32[]{:S(2)}, u32[]{:S(2)}) async-start(bf16[32,64,128]{2,1,0:T(8,128)(2,1)} %bessel_send.1), calls=%async_computation | async-start | bytes 1048576 | tf_op jit(solution)/shard_map/all_to_all | solution.py:189
  42.2 2.2 %copy-start = (bf16[8,2048,128]{2,1,0:T(8,128)(2,1)S(1)}, bf16[8,2048,128]{2,1,0:T(8,128)(2,1)}, u32[]{:S(2)}) copy-start(bf16[8,2048,128]{2,1,0:T(8,128)(2,1)} %legendre_ref.1) | copy-start | bytes 12582916
  44.4 0.7 copy-start.6
  44.4 0.7 copy-start.7
  57.6 8.0 %copy-start.1 = (bf16[32,64,128]{2,1,0:T(8,128)(2,1)}, bf16[32,64,128]{2,1,0:T(8,128)(2,1)S(1)}, u32[]{:S(2)}) copy-start(bf16[32,64,128]{2,1,0:T(8,128)(2,1)S(1)} %all-to-all-done) | copy-start | bytes 1572868
  58.8 22.0 %all-to-all-start.3 = ((bf16[8,512,128]{2,1,0:T(8,128)(2,1)}), bf16[8,512,128]{2,1,0:T(8,128)(2,1)S(1)}, u32[]{:S(2)}, u32[]{:S(2)}) async-start(bf16[8,512,128]{2,1,0:T(8,128)(2,1)} %broadcast_in_dim.22), calls=%async_computation.3 | async-start | bytes 2097152 | tf_op jit(solution)/shard_map/all_to_all | solution.py:214
  65.6 1.0 %copy-start.2 = (bf16[32,64,128]{2,1,0:T(8,128)(2,1)S(1)}, bf16[32,64,128]{2,1,0:T(8,128)(2,1)}, u32[]{:S(2)}) copy-start(bf16[32,64,128]{2,1,0:T(8,128)(2,1)} %copy-done.1) | copy-start | bytes 1572868

commit v2 on v1

v2 whole, which is shorter than its diff:
```python
import math

import jax
import jax.numpy as jnp
from jax import lax
from jax.experimental import pallas as pl
from jax.experimental.pallas import tpu as pltpu
from jax.sharding import PartitionSpec as P

NSIDE = 1024
F32 = jnp.float32
BF16 = jnp.bfloat16
VMEM_LIMIT = 24 * 1024 * 1024

SMEM_SPEC = pl.BlockSpec(memory_space=pltpu.SMEM)
VMEM_SPEC = pl.BlockSpec(memory_space=pltpu.VMEM)
ANY_SPEC = pl.BlockSpec(memory_space=pl.ANY)
HBM_SPEC = pl.BlockSpec(memory_space=pltpu.HBM)


def params():
    return pltpu.CompilerParams(vmem_limit_bytes=VMEM_LIMIT)


def cost(microseconds, transferred):
    return pl.CostEstimate(flops=microseconds * 500_000_000, bytes_accessed=transferred, transcendentals=0)


def cos_sin(turns):
    quarter = (turns + 1024) >> 11
    x = (turns - (quarter << 11)).astype(F32) * (math.pi / 4096)
    z = x * x
    s = x + x * z * (-1.6666654611e-1 + z * (8.3321608736e-3 + z * -1.9515295891e-4))
    c = 1.0 - 0.5 * z + z * z * (4.166664568298827e-2 + z * (-1.388731625493765e-3 + z * 2.443315711809948e-5))
    odd = (quarter & 1) == 1
    even_sign = jnp.where((quarter & 2) == 2, -1.0, 1.0)
    cos = jnp.where(odd, -s, c) * even_sign
    sin = jnp.where(odd, c, s) * even_sign
    return cos, sin


def dft_kernel(cycle_hbm, order_hbm, density_hbm, footprint_hbm, out_ref, cycle_ref, order_ref, density_ref, footprint_ref, sems):
    _, rows, nphi = density_ref.shape
    copies = [
        pltpu.make_async_copy(order_hbm, order_ref, sems.at[0]),
        pltpu.make_async_copy(cycle_hbm, cycle_ref, sems.at[1]),
        pltpu.make_async_copy(density_hbm, density_ref, sems.at[2]),
        pltpu.make_async_copy(footprint_hbm, footprint_ref, sems.at[3]),
    ]
    for copy in copies:
        copy.start()
    copies[0].wait()
    lane = lax.broadcasted_iota(jnp.int32, (1, 128), 1)
    part = (lane >> 3) & 1
    slot = ((lane >> 4) << 3) + (lane & 7)
    order = jnp.zeros((1, 128), jnp.int32)
    for q in range(64):
        order = jnp.where(slot == q, order_ref[q], order)
    sixty_four = lax.broadcasted_iota(jnp.int32, (64, 128), 0)
    pa, qa = cos_sin((sixty_four * 128 * order + 2048 * part) & 8191)
    qa = -qa
    cb, sb = cos_sin((sixty_four * 2 * order) & 8191)
    for copy in copies[1:]:
        copy.wait()
    total = jnp.zeros((2 * rows, 256), F32)
    for chunk in range(nphi // 256):
        tables = []
        for a in range(4 * chunk, 4 * chunk + 4):
            tables.append(pa[a : a + 1] * cb + qa[a : a + 1] * sb)
        table = jnp.concatenate(tables, axis=0)
        high = table.astype(BF16)
        low = (table - high.astype(F32)).astype(BF16)
        cut = slice(256 * chunk, 256 * chunk + 256)
        pixels = density_ref[0, :, cut] * footprint_ref[0, :, cut].astype(F32)
        p_high = pixels.astype(BF16)
        p_low = (pixels - p_high.astype(F32)).astype(BF16)
        total = total + jnp.dot(
            jnp.concatenate([p_high, p_low], axis=0),
            jnp.concatenate([high, low], axis=1),
            preferred_element_type=F32,
        )
    x = total[:rows, :128] + (total[:rows, 128:] + total[rows:, :128])
    row = lax.broadcasted_iota(jnp.int32, (rows, 128), 0)
    cycle = jnp.zeros((rows, 128), jnp.int32)
    for r in range(rows):
        cycle = jnp.where(row == r, cycle_ref[r], cycle)
    parity = (cycle - (NSIDE - 1)) & 1
    cos_t, sin_t = cos_sin((order * (2 - parity)) & 8191)
    other = jnp.where(part == 0, pltpu.roll(x, 120, 1), -pltpu.roll(x, 8, 1))
    four = (x * cos_t + other * sin_t).astype(BF16)
    lanes = lax.broadcasted_iota(jnp.int32, (rows, 128), 1)
    place = (lanes == row + rows * lax.axis_index("shell")).astype(BF16)
    out_ref[...] = lax.dot_general(four, place, (((0,), (0,)), ((), ())), preferred_element_type=F32).astype(BF16)


def send_kernel(lengths_ref, bessel_ref, out_ref, wide_ref):
    modes, deg = bessel_ref.shape
    blocks = out_ref.shape[0]
    wide_ref[:, pl.ds(0, deg)] = bessel_ref[...].astype(F32)
    wide_ref[:, pl.ds(deg, 256)] = jnp.zeros((modes, 256), F32)
    lane = lax.broadcasted_iota(jnp.int32, (modes, 128), 1)

    def step(k, start):
        base = pl.multiple_of((start >> 7) << 7, 128)
        shift = start - base
        back = (128 - shift) & 127
        low = pltpu.roll(wide_ref[:, pl.ds(base, 128)], back, 1)
        high = pltpu.roll(wide_ref[:, pl.ds(base + 128, 128)], back, 1)
        out_ref[k, 16:, :] = jnp.where(lane < 128 - shift, low, high).astype(BF16)
        return start + lengths_ref[k]

    lax.fori_loop(0, blocks, step, jnp.int32(0), unroll=4)


def fill_kernel(parts_ref, send_ref, out_ref, tile_ref, sem):
    total = parts_ref[0].astype(F32)
    for h in range(1, parts_ref.shape[0]):
        total = total + parts_ref[h].astype(F32)
    tile_ref[...] = jnp.broadcast_to(total.astype(BF16)[None], tile_ref.shape)
    copy = pltpu.make_async_copy(tile_ref, out_ref.at[:, pl.ds(0, 16), :], sem)
    copy.start()
    copy.wait()


def block_start(lengths_ref, block):
    return lax.fori_loop(0, block, lambda k, total: total + lengths_ref[k], jnp.int32(0))


def rows_kernel(lengths_ref, legendre_ref, out_ref, window_ref, wide_ref, sem):
    deg = legendre_ref.shape[1]
    window = window_ref.shape[1]
    start = block_start(lengths_ref, lax.axis_index("radial"))
    base = jnp.minimum((start >> 4) << 4, deg - window)
    base = pl.multiple_of(base, 16)
    copy = pltpu.make_async_copy(legendre_ref.at[:, pl.ds(base, window), :], window_ref, sem)
    copy.start()
    copy.wait()
    shift = start - base
    wide_ref[pl.ds(window, 128), :] = jnp.zeros((128, 128), F32)
    for q in range(out_ref.shape[0]):
        wide_ref[pl.ds(0, window), :] = window_ref[q].astype(F32)
        out_ref[q] = wide_ref[pl.ds(shift, 128), :].astype(BF16)


def harmonic_kernel(lengths_ref, order_ref, recv_ref, rows_ref, out_ref, four32_ref, out32_ref):
    four32_ref[...] = recv_ref[:, :16].astype(F32).reshape(512, 128)
    start = block_start(lengths_ref, lax.axis_index("radial"))
    lane = lax.broadcasted_iota(jnp.int32, (32, 128), 1)
    degree = start + lax.broadcasted_iota(jnp.int32, (32, 128), 0) + 32 * (lane >> 5)
    group = lane >> 5
    for q in range(8):
        order = order_ref[8 * lax.axis_index("shell") + q]
        for c in range(2):
            one = four32_ref[pl.ds(c * 8 + q, 32, stride=16), :]
            four = jnp.concatenate([one] * 4, axis=0).astype(BF16)
            full = lax.dot_general(rows_ref[q], four, (((1,), (1,)), ((), ())), preferred_element_type=F32)
            packed = full[96:128]
            for j in range(3):
                packed = jnp.where(group == j, full[32 * j : 32 * j + 32], packed)
            packed = jnp.where(degree >= order, packed, 0.0)
            out32_ref[pl.ds(c * 8 + q, 32, stride=16), :] = packed
    out_ref[...] = out32_ref[...].astype(BF16)


def radial_kernel(lengths_ref, recv_ref, out_ref, wide_ref, turned_ref):
    length = lengths_ref[lax.axis_index("radial")]
    modes = 64
    wide_ref[...] = recv_ref[:, 16:].astype(F32).reshape(32 * modes, 128)
    slot = lax.broadcasted_iota(jnp.int32, (128, 128), 1)
    group = lax.broadcasted_iota(jnp.int32, (128, 128), 0)
    keep = ((slot >> 5) == (group >> 5)) & (slot < length)

    def step(n, carry):
        x = wide_ref[pl.ds(n, 32, stride=modes), :]
        x = jnp.where(keep, jnp.concatenate([x] * 4, axis=0), 0.0)
        turned = jnp.transpose(x)
        for j in range(4):
            turned_ref[pl.ds(j * modes + n, 32, stride=4 * modes), :] = turned[32 * j : 32 * j + 32]
        return carry

    lax.fori_loop(0, modes, step, 0, unroll=2)
    for g in range(32):
        out_ref[g] = turned_ref[pl.ds(g * 256, 256), :].astype(BF16)


def final_kernel(radial_ref, *refs):
    pieces, out_ref, right_ref = refs[:8], refs[8], refs[9]
    mine = lax.axis_index("shell")
    steps = out_ref.shape[1]
    for i in range(steps):
        g = pl.program_id(0) * steps + i
        for d in range(8):
            h = mine ^ d
            piece = pieces[d][pl.ds(pl.multiple_of(g * 16, 16), 16), :].astype(F32)
            right_ref[i, 0, h] = piece[:8]
            right_ref[i, 1, h] = piece[8:]
        right = right_ref[i].reshape(128, 128).astype(BF16)
        result = lax.dot_general(radial_ref[g], right, (((1,), (1,)), ((), ())), preferred_element_type=F32)
        out_ref[:, i] = result.reshape(4, 64, 128).astype(BF16)


def on_device(density, footprint, cycle_index, order_values, block_lengths, legendre, bessel):
    shape = jax.ShapeDtypeStruct
    rows, nphi = density.shape[1:]
    deg, modes = bessel.shape[1:]
    dma = pltpu.SemaphoreType.DMA

    four = pl.pallas_call(
        dft_kernel,
        out_shape=shape((128, 128), BF16),
        in_specs=[HBM_SPEC] * 4,
        out_specs=VMEM_SPEC,
        scratch_shapes=[
            pltpu.SMEM((rows,), jnp.int32),
            pltpu.SMEM((64,), jnp.int32),
            pltpu.VMEM((1, rows, nphi), F32),
            pltpu.VMEM((1, rows, nphi), jnp.int32),
            dma((4,)),
        ],
        compiler_params=params(),
        cost_estimate=cost(2, 1 << 19),
        name="dft",
    )(cycle_index, order_values, density, footprint)
    by_order = lax.all_to_all(four.reshape(8, 16, 128), "shell", split_axis=0, concat_axis=0, tiled=True)

    send = pl.pallas_call(
        send_kernel,
        out_shape=shape((32, 16 + modes, 128), BF16),
        in_specs=[SMEM_SPEC, VMEM_SPEC],
        out_specs=VMEM_SPEC,
        scratch_shapes=[pltpu.VMEM((modes, deg + 256), F32)],
        compiler_params=params(),
        cost_estimate=cost(2, 1 << 20),
        name="bessel_send",
    )(block_lengths, jnp.swapaxes(bessel, 1, 2).reshape(modes, deg))
    send = pl.pallas_call(
        fill_kernel,
        out_shape=shape(send.shape, BF16),
        in_specs=[VMEM_SPEC, ANY_SPEC],
        out_specs=ANY_SPEC,
        scratch_shapes=[pltpu.VMEM((32, 16, 128), BF16), dma],
        input_output_aliases={1: 0},
        compiler_params=params(),
        cost_estimate=cost(1, 1 << 17),
        name="fill",
    )(by_order, send)
    recv = lax.all_to_all(send, "radial", split_axis=0, concat_axis=0, tiled=True)

    leg_rows = pl.pallas_call(
        rows_kernel,
        out_shape=shape((8, 128, 128), BF16),
        in_specs=[SMEM_SPEC, HBM_SPEC],
        out_specs=VMEM_SPEC,
        scratch_shapes=[pltpu.VMEM((8, 144, 128), BF16), pltpu.VMEM((144 + 128, 128), F32), dma],
        compiler_params=params(),
        cost_estimate=cost(1, 1 << 19),
        name="legendre_rows",
    )(block_lengths, legendre)

    harmonic = pl.pallas_call(
        harmonic_kernel,
        out_shape=shape((512, 128), BF16),
        in_specs=[SMEM_SPEC, SMEM_SPEC, VMEM_SPEC, VMEM_SPEC],
        out_specs=VMEM_SPEC,
        scratch_shapes=[pltpu.VMEM((512, 128), F32), pltpu.VMEM((512, 128), F32)],
        compiler_params=params(),
        cost_estimate=cost(1, 1 << 19),
        name="harmonic",
    )(block_lengths, order_values, recv, leg_rows)

    def swap(x, d):
        return lax.ppermute(x, "shell", [(i, i ^ d) for i in range(8)])

    pieces = {0: harmonic}
    for d in (2, 6, 4):
        pieces[d] = swap(harmonic, d)
    for d in (0, 2, 6, 4):
        pieces[d + 1] = swap(pieces[d], 1)

    radial = pl.pallas_call(
        radial_kernel,
        out_shape=shape((32, 4 * modes, 128), BF16),
        in_specs=[SMEM_SPEC, VMEM_SPEC],
        out_specs=VMEM_SPEC,
        scratch_shapes=[pltpu.VMEM((32 * modes, 128), F32), pltpu.VMEM((128 * modes, 128), F32)],
        compiler_params=params(),
        cost_estimate=cost(5, 1 << 21),
        name="radial_rows",
    )(block_lengths, recv)

    step = 4
    out = pl.pallas_call(
        final_kernel,
        out_shape=shape((4, 32, modes, 128), BF16),
        grid=(32 // step,),
        in_specs=[VMEM_SPEC] * 9,
        out_specs=pl.BlockSpec((4, step, modes, 128), lambda g: (0, g, 0, 0)),
        scratch_shapes=[pltpu.VMEM((step, 2, 8, 8, 128), F32)],
        compiler_params=params(),
        cost_estimate=cost(4, 1 << 22),
        name="combine",
    )(radial, *[pieces[d] for d in range(8)])
    return out.reshape(128, modes, 128)


def solution(mesh):
    return jax.shard_map(
        on_device,
        mesh=mesh,
        in_specs=(
            P("radial", "shell", None),
            P("radial", "shell", None),
            P("shell"),
            P(),
            P(),
            P("shell", None, None),
            P("radial", None, "shell"),
        ),
        out_specs=P("radial", "shell", None),
        check_vma=False,
    )
```

time: 85.3 us -> 69.5 us (0.81)
  blocking collectives: 10.3 us -> 0 us
  waiting for transfers between devices: 24.4 us -> 18.4 us
  local copies, waits for them, and re-layouts: 10.3 us -> 5.42 us
  starting transfers between devices: 23.7 us -> 27.9 us
  Pallas kernels: 15.9 us -> 17.3 us
    all_to_all x2 -> x1, starting transfers between devices: 18 us -> 6.48 us  [on_device(): lax.all_to_all(four.reshape(8, 16, 128), 'shell', split_axis=0, concat_ax...]
    ppermute x0 -> x7, starting transfers between devices: none -> 10.9 us  [swap(): return lax.ppermute(x, 'shell', [(i, i ^ d) for i in range(8)])]
    all_to_all x2 -> x1, waiting for transfers between devices: 13 us -> 2.48 us  [on_device(): lax.all_to_all(four.reshape(8, 16, 128), 'shell', split_axis=0, concat_ax...]
    all_to_all x1 -> x0, blocking collectives: 10.3 us -> none  [on_device(): lax.all_to_all(four.reshape(8, 16, 128), 'shell', split_axis=0, concat_ax...]
    all_to_all x1, starting transfers between devices: 5.64 us -> 10.5 us  [on_device(): lax.all_to_all(send, 'radial', split_axis=0, concat_axis=0, tiled=True)]
    all_to_all x1, waiting for transfers between devices: 11.4 us -> 15.9 us  [on_device(): lax.all_to_all(send, 'radial', split_axis=0, concat_axis=0, tiled=True)]
    broadcast_in_dim x4 -> x0, local copies, waits for them, and re-layouts: 2.54 us -> none  [the longest x1 1.14 us: on_device(): jnp.broadcast_to(harmonic[None], (8, 512, 128))]
    unnamed x19 -> x16, local copies, waits for them, and re-layouts: 7.67 us -> 5.42 us
  transfers between devices with their start and end apart: 3 -> 9, of which waited for: 3 -> 2; matrix products, arithmetic and copies ran while one was open for 1% -> 0% of each run, Pallas kernels for 12% -> 13%
where the time goes in v2:
time: 69.5 us; the launch traced here: 69.2 us
  starting transfers between devices  27.9 us (40%)
  waiting for transfers between devices  18.4 us (26%)
  Pallas kernels  17.3 us (25%)
  local copies, waits for them, and re-layouts  5.42 us (8%)
    all_to_all x1, waiting for transfers between devices, on_device(): lax.all_to_all(send, 'radial', split_axis=0, concat_axis=0, tiled=True)  15.9 us
    ppermute x7, starting transfers between devices, swap(): return lax.ppermute(x, 'shell', [(i, i ^ d) for i in range(8)])  10.9 us
    all_to_all x1, starting transfers between devices, on_device(): lax.all_to_all(send, 'radial', split_axis=0, concat_axis=0, tiled=True)  10.5 us
    all_to_all x1, starting transfers between devices, on_device(): lax.all_to_all(four.reshape(8, 16, 128), 'shell', split_axis=0, concat_ax...  6.48 us
    pallas_call x1, Pallas kernels, on_device(): pl.pallas_call(radial_kernel, out_shape=shape((32, 4 * modes, 128), BF16)...  6.31 us
    unnamed x16, local copies, waits for them, and re-layouts  5.42 us
    pallas_call x1, Pallas kernels, on_device(): pl.pallas_call(final_kernel, out_shape=shape((4, 32, modes, 128), BF16),...  4.13 us
    all_to_all x1, waiting for transfers between devices, on_device(): lax.all_to_all(four.reshape(8, 16, 128), 'shell', split_axis=0, concat_ax...  2.48 us
  transfers between devices with their start and end apart: 9, of which 2 were waited for; matrix products, arithmetic and copies ran while one was open for 0% of the time, Pallas kernels for 13%

profile of v2, /device:TPU:1, one launch (start us, length us, event | category | flops | bytes accessed | tf_op | source)
XLA Modules:
  0.0 69.2 jit_solution(300678591630005961)
XLA Ops:
  0.0 1.0 %copy-done.2 = f32[1,16,4096]{2,1,0:T(8,128)S(1)} copy-done((f32[1,16,4096]{2,1,0:T(8,128)S(1)}, f32[1,16,4096]{2,1,0:T(8,128)}, u32[]{:S(2)}) %copy-start.2) | copy-done | bytes 262168
  1.0 0.9 %copy-done.3 = s32[1,16,4096]{2,1,0:T(8,128)S(1)} copy-done((s32[1,16,4096]{2,1,0:T(8,128)S(1)}, s32[1,16,4096]{2,1,0:T(8,128)}, u32[]{:S(2)}) %copy-start.3) | copy-done | bytes 262168
  1.9 0.7 copy-done.5
  2.6 0.7 copy-done.6
  3.2 2.2 %dft.1 = bf16[128,128]{1,0:T(8,128)(2,1)} custom-call(s32[16]{0:T(128)S(1)} %copy-done.5, s32[64]{0:T(128)S(1)} %copy-done.6, f32[1,16,4096]{2,1,0:T(8,128)S(1)} %copy-done.2, s32[1,16,4096]{2,1,0:T(8,128)S(1)} %copy-done.3), custom_call_target="tpu_custom_call" | custom-call | flops 1000000000 | bytes 524288 | tf_op jit(solution)/shard_map/dft/pallas_call | solution.py:208
  5.4 6.5 %all-to-all-start = ((bf16[8,16,128]{2,1,0:T(8,128)(2,1)}), bf16[8,16,128]{2,1,0:T(8,128)(2,1)S(1)}, u32[]{:S(2)}, u32[]{:S(2)}) async-start(bf16[8,16,128]{2,1,0:T(8,128)(2,1)} %bitcast), calls=%async_computation | async-start | bytes 65536 | tf_op jit(solution)/shard_map/all_to_all | solution.py:224
  11.9 0.0 copy-done.1
  11.9 2.3 %bessel_send.1.send_ref = bf16[32,80,128]{2,1,0:T(8,128)(2,1)} custom-call(s32[32]{0:T(128)S(1)} %copy-done.1, bf16[64,2048]{1,0:T(8,128)(2,1)S(1)} %bitcast.5), custom_call_target="tpu_custom_call" | custom-call | flops 1000000000 | bytes 1048576 | tf_op jit(solution)/shard_map/bessel_send/pallas_call | solution.py:226
  14.2 2.5 %all-to-all-done.parts_ref = bf16[8,16,128]{2,1,0:T(8,128)(2,1)S(1)} async-done(((bf16[8,16,128]{2,1,0:T(8,128)(2,1)}), bf16[8,16,128]{2,1,0:T(8,128)(2,1)S(1)}, u32[]{:S(2)}, u32[]{:S(2)}) %all-to-all-start) | async-done | bytes 32800 | tf_op jit(solution)/shard_map/all_to_all | solution.py:224
  16.7 0.7 fill.1
  17.4 10.5 %all-to-all-start.1 = ((bf16[32,80,128]{2,1,0:T(8,128)(2,1)}), bf16[32,80,128]{2,1,0:T(8,128)(2,1)S(1)}, u32[]{:S(2)}, u32[]{:S(2)}) async-start(bf16[32,80,128]{2,1,0:T(8,128)(2,1)} %fill.1), calls=%async_computation.1 | async-start | bytes 1310720 | tf_op jit(solution)/shard_map/all_to_all | solution.py:247
  27.9 0.0 copy-start
  27.9 2.2 %copy-done = bf16[8,2048,128]{2,1,0:T(8,128)(2,1)S(1)} copy-done((bf16[8,2048,128]{2,1,0:T(8,128)(2,1)S(1)}, bf16[8,2048,128]{2,1,0:T(8,128)(2,1)}, u32[]{:S(2)}) %copy-start) | copy-done | bytes 4194328
  30.1 0.7 legendre_rows.1.rows_ref
  30.8 15.9 %all-to-all-done.1.recv_ref = bf16[32,80,128]{2,1,0:T(8,128)(2,1)S(1)} async-done(((bf16[32,80,128]{2,1,0:T(8,128)(2,1)}), bf16[32,80,128]{2,1,0:T(8,128)(2,1)S(1)}, u32[]{:S(2)}, u32[]{:S(2)}) %all-to-all-start.1) | async-done | bytes 655392 | tf_op jit(solution)/shard_map/all_to_all | solution.py:247
  46.6 1.1 %harmonic.1.refs_0_ = bf16[512,128]{1,0:T(8,128)(2,1)S(1)} custom-call(s32[32]{0:T(128)S(1)} %copy-done.1, s32[64]{0:T(128)S(1)} %copy-done.7, bf16[32,80,128]{2,1,0:T(8,128)(2,1)S(1)} %all-to-all-done.1.recv_ref, bf16[8,128,128]{2,1,0:T(8,128)(2,1)S(1)} %legendre_rows.1.rows_ref), custom_call_target="tpu_custom_call" | custom-call | flops 500000000 | bytes 524288 | tf_op jit(solution)/shard_map/harmonic/pallas_call | solution.py:260
  47.7 1.0 %collective-permute-start.5 = (bf16[512,128]{1,0:T(8,128)(2,1)S(1)}, bf16[512,128]{1,0:T(8,128)(2,1)S(1)}, u32[]{:S(2)}, u32[]{:S(2)}) collective-permute-start(bf16[512,128]{1,0:T(8,128)(2,1)S(1)} %harmonic.1.refs_0_), channel_id=1, source_target_pairs={{0,192},{32,224},{64,128},{96,160},{128,64},{160,96},{192,0},{224,... | collective-permute-start | bytes 393224 | tf_op jit(solution)/shard_map/ppermute | solution.py:272
  48.7 1.2 %collective-permute-start.3 = (bf16[512,128]{1,0:T(8,128)(2,1)S(1)}, bf16[512,128]{1,0:T(8,128)(2,1)S(1)}, u32[]{:S(2)}, u32[]{:S(2)}) collective-permute-start(bf16[512,128]{1,0:T(8,128)(2,1)S(1)} %harmonic.1.refs_0_), channel_id=1, source_target_pairs={{0,128},{32,160},{64,192},{96,224},{128,0},{160,32},{192,64},{224,... | collective-permute-start | bytes 393224 | tf_op jit(solution)/shard_map/ppermute | solution.py:272
  49.9 1.2 %collective-permute-start.1 = (bf16[512,128]{1,0:T(8,128)(2,1)S(1)}, bf16[512,128]{1,0:T(8,128)(2,1)S(1)}, u32[]{:S(2)}, u32[]{:S(2)}) collective-permute-start(bf16[512,128]{1,0:T(8,128)(2,1)S(1)} %harmonic.1.refs_0_), channel_id=1, source_target_pairs={{0,64},{32,96},{64,0},{96,32},{128,192},{160,224},{192,128},{224,1... | collective-permute-start | bytes 393224 | tf_op jit(solution)/shard_map/ppermute | solution.py:272
  51.1 3.3 %collective-permute-start = (bf16[512,128]{1,0:T(8,128)(2,1)S(1)}, bf16[512,128]{1,0:T(8,128)(2,1)S(1)}, u32[]{:S(2)}, u32[]{:S(2)}) collective-permute-start(bf16[512,128]{1,0:T(8,128)(2,1)S(1)} %harmonic.1.refs_0_), channel_id=1, source_target_pairs={{0,32},{32,0},{64,96},{96,64},{128,160},{160,128},{192,224},{224,1... | collective-permute-start | bytes 393224 | tf_op jit(solution)/shard_map/ppermute | solution.py:272
  54.3 0.0 collective-permute-done.5.refs_6_
  54.4 2.1 %collective-permute-start.6 = (bf16[512,128]{1,0:T(8,128)(2,1)S(1)}, bf16[512,128]{1,0:T(8,128)(2,1)S(1)}, u32[]{:S(2)}, u32[]{:S(2)}) collective-permute-start(bf16[512,128]{1,0:T(8,128)(2,1)S(1)} %collective-permute-done.5.refs_6_), channel_id=1, source_target_pairs={{0,32},{32,0},{64,96},{96,64},{128,160},{160,128},{192,224},{224,1... | collective-permute-start | bytes 393224 | tf_op jit(solution)/shard_map/ppermute | solution.py:272
  56.4 0.0 collective-permute-done.3.refs_4_
  56.4 1.5 %collective-permute-start.4 = (bf16[512,128]{1,0:T(8,128)(2,1)S(1)}, bf16[512,128]{1,0:T(8,128)(2,1)S(1)}, u32[]{:S(2)}, u32[]{:S(2)}) collective-permute-start(bf16[512,128]{1,0:T(8,128)(2,1)S(1)} %collective-permute-done.3.refs_4_), channel_id=1, source_target_pairs={{0,32},{32,0},{64,96},{96,64},{128,160},{160,128},{192,224},{224,1... | collective-permute-start | bytes 393224 | tf_op jit(solution)/shard_map/ppermute | solution.py:272
  57.9 0.0 collective-permute-done.1.refs_2_
  57.9 0.8 %collective-permute-start.2 = (bf16[512,128]{1,0:T(8,128)(2,1)S(1)}, bf16[512,128]{1,0:T(8,128)(2,1)S(1)}, u32[]{:S(2)}, u32[]{:S(2)}) collective-permute-start(bf16[512,128]{1,0:T(8,128)(2,1)S(1)} %collective-permute-done.1.refs_2_), channel_id=1, source_target_pairs={{0,32},{32,0},{64,96},{96,64},{128,160},{160,128},{192,224},{224,1... | collective-permute-start | bytes 393224 | tf_op jit(solution)/shard_map/ppermute | solution.py:272
  58.7 6.3 %radial_rows.1.radial_ref = bf16[32,256,128]{2,1,0:T(8,128)(2,1)S(1)} custom-call(s32[32]{0:T(128)S(1)} %copy-done.1, bf16[32,80,128]{2,1,0:T(8,128)(2,1)S(1)} %all-to-all-done.1.recv_ref), custom_call_target="tpu_custom_call" | custom-call | flops 2500000000 | bytes 2097152 | tf_op jit(solution)/shard_map/radial_rows/pallas_call | solution.py:280
  65.0 0.0 collective-permute-done.refs_1_
  65.0 0.0 collective-permute-done.6.refs_7_
  65.0 0.0 collective-permute-done.4.refs_5_
  65.0 0.0 collective-permute-done.2.refs_3_
  65.1 4.1 %combine.1 = bf16[4,32,64,128]{3,2,1,0:T(8,128)(2,1)} custom-call(bf16[32,256,128]{2,1,0:T(8,128)(2,1)S(1)} %radial_rows.1.radial_ref, bf16[512,128]{1,0:T(8,128)(2,1)S(1)} %harmonic.1.refs_0_, bf16[512,128]{1,0:T(8,128)(2,1)S(1)} %collective-permute-done.refs_1_, bf16[512,128]{1,0:T(8,128)(2,1)S(1)} %collective-permute-done.1.refs_2_, ...), custom_call_target="tpu_custom_call" | custom-call | flops 2000000000 | bytes 4194304 | tf_op jit(solution)/shard_map/combine/pallas_call | solution.py:292
  (9 shorter events, 0.0 us)
Async XLA Ops:
  0.0 11.9 %copy-start.1 = (s32[32]{0:T(128)S(1)}, s32[32]{0:T(128)}, u32[]{:S(2)}) copy-start(s32[32]{0:T(128)} %lengths_ref.7) | copy-start | bytes 388
  0.0 1.0 %copy-start.2 = (f32[1,16,4096]{2,1,0:T(8,128)S(1)}, f32[1,16,4096]{2,1,0:T(8,128)}, u32[]{:S(2)}) copy-start(f32[1,16,4096]{2,1,0:T(8,128)} %density_hbm.1) | copy-start | bytes 786436
  1.0 0.9 %copy-start.3 = (s32[1,16,4096]{2,1,0:T(8,128)S(1)}, s32[1,16,4096]{2,1,0:T(8,128)}, u32[]{:S(2)}) copy-start(s32[1,16,4096]{2,1,0:T(8,128)} %footprint_hbm.1) | copy-start | bytes 786436
  1.9 0.7 copy-start.5
  2.6 0.7 copy-start.6
  3.2 8.7 %copy-start.4 = (bf16[1,2048,64]{1,2,0:T(8,128)(2,1)S(1)}, bf16[1,2048,64]{1,2,0:T(8,128)(2,1)}, u32[]{:S(2)}) copy-start(bf16[1,2048,64]{1,2,0:T(8,128)(2,1)} %param.13) | copy-start | bytes 786436
  5.4 11.2 %all-to-all-start = ((bf16[8,16,128]{2,1,0:T(8,128)(2,1)}), bf16[8,16,128]{2,1,0:T(8,128)(2,1)S(1)}, u32[]{:S(2)}, u32[]{:S(2)}) async-start(bf16[8,16,128]{2,1,0:T(8,128)(2,1)} %bitcast), calls=%async_computation | async-start | bytes 65536 | tf_op jit(solution)/shard_map/all_to_all | solution.py:224
  17.4 29.3 %all-to-all-start.1 = ((bf16[32,80,128]{2,1,0:T(8,128)(2,1)}), bf16[32,80,128]{2,1,0:T(8,128)(2,1)S(1)}, u32[]{:S(2)}, u32[]{:S(2)}) async-start(bf16[32,80,128]{2,1,0:T(8,128)(2,1)} %fill.1), calls=%async_computation.1 | async-start | bytes 1310720 | tf_op jit(solution)/shard_map/all_to_all | solution.py:247
  27.9 2.2 %copy-start = (bf16[8,2048,128]{2,1,0:T(8,128)(2,1)S(1)}, bf16[8,2048,128]{2,1,0:T(8,128)(2,1)}, u32[]{:S(2)}) copy-start(bf16[8,2048,128]{2,1,0:T(8,128)(2,1)} %legendre_ref.1) | copy-start | bytes 12582916
  30.1 16.6 %copy-start.7 = (s32[64]{0:T(128)S(1)}, s32[64]{0:T(128)}, u32[]{:S(2)}) copy-start(s32[64]{0:T(128)} %order_ref.1) | copy-start | bytes 772
  47.7 6.6 %collective-permute-start.5 = (bf16[512,128]{1,0:T(8,128)(2,1)S(1)}, bf16[512,128]{1,0:T(8,128)(2,1)S(1)}, u32[]{:S(2)}, u32[]{:S(2)}) collective-permute-start(bf16[512,128]{1,0:T(8,128)(2,1)S(1)} %harmonic.1.refs_0_), channel_id=1, source_target_pairs={{0,192},{32,224},{64,128},{96,160},{128,64},{160,96},{192,0},{224,... | collective-permute-start | bytes 393224 | tf_op jit(solution)/shard_map/ppermute | solution.py:272
  48.7 7.7 %collective-permute-start.3 = (bf16[512,128]{1,0:T(8,128)(2,1)S(1)}, bf16[512,128]{1,0:T(8,128)(2,1)S(1)}, u32[]{:S(2)}, u32[]{:S(2)}) collective-permute-start(bf16[512,128]{1,0:T(8,128)(2,1)S(1)} %harmonic.1.refs_0_), channel_id=1, source_target_pairs={{0,128},{32,160},{64,192},{96,224},{128,0},{160,32},{192,64},{224,... | collective-permute-start | bytes 393224 | tf_op jit(solution)/shard_map/ppermute | solution.py:272
  49.9 8.0 %collective-permute-start.1 = (bf16[512,128]{1,0:T(8,128)(2,1)S(1)}, bf16[512,128]{1,0:T(8,128)(2,1)S(1)}, u32[]{:S(2)}, u32[]{:S(2)}) collective-permute-start(bf16[512,128]{1,0:T(8,128)(2,1)S(1)} %harmonic.1.refs_0_), channel_id=1, source_target_pairs={{0,64},{32,96},{64,0},{96,32},{128,192},{160,224},{192,128},{224,1... | collective-permute-start | bytes 393224 | tf_op jit(solution)/shard_map/ppermute | solution.py:272
  51.1 13.9 %collective-permute-start = (bf16[512,128]{1,0:T(8,128)(2,1)S(1)}, bf16[512,128]{1,0:T(8,128)(2,1)S(1)}, u32[]{:S(2)}, u32[]{:S(2)}) collective-permute-start(bf16[512,128]{1,0:T(8,128)(2,1)S(1)} %harmonic.1.refs_0_), channel_id=1, source_target_pairs={{0,32},{32,0},{64,96},{96,64},{128,160},{160,128},{192,224},{224,1... | collective-permute-start | bytes 393224 | tf_op jit(solution)/shard_map/ppermute | solution.py:272
  54.4 10.7 %collective-permute-start.6 = (bf16[512,128]{1,0:T(8,128)(2,1)S(1)}, bf16[512,128]{1,0:T(8,128)(2,1)S(1)}, u32[]{:S(2)}, u32[]{:S(2)}) collective-permute-start(bf16[512,128]{1,0:T(8,128)(2,1)S(1)} %collective-permute-done.5.refs_6_), channel_id=1, source_target_pairs={{0,32},{32,0},{64,96},{96,64},{128,160},{160,128},{192,224},{224,1... | collective-permute-start | bytes 393224 | tf_op jit(solution)/shard_map/ppermute | solution.py:272
  56.4 8.6 %collective-permute-start.4 = (bf16[512,128]{1,0:T(8,128)(2,1)S(1)}, bf16[512,128]{1,0:T(8,128)(2,1)S(1)}, u32[]{:S(2)}, u32[]{:S(2)}) collective-permute-start(bf16[512,128]{1,0:T(8,128)(2,1)S(1)} %collective-permute-done.3.refs_4_), channel_id=1, source_target_pairs={{0,32},{32,0},{64,96},{96,64},{128,160},{160,128},{192,224},{224,1... | collective-permute-start | bytes 393224 | tf_op jit(solution)/shard_map/ppermute | solution.py:272
  57.9 7.1 %collective-permute-start.2 = (bf16[512,128]{1,0:T(8,128)(2,1)S(1)}, bf16[512,128]{1,0:T(8,128)(2,1)S(1)}, u32[]{:S(2)}, u32[]{:S(2)}) collective-permute-start(bf16[512,128]{1,0:T(8,128)(2,1)S(1)} %collective-permute-done.1.refs_2_), channel_id=1, source_target_pairs={{0,32},{32,0},{64,96},{96,64},{128,160},{160,128},{192,224},{224,1... | collective-permute-start | bytes 393224 | tf_op jit(solution)/shard_map/ppermute | solution.py:272

commit v3 on v2

--- a/solution.py
+++ b/solution.py
@@ -10,7 +10,9 @@
 NSIDE = 1024
 F32 = jnp.float32
 BF16 = jnp.bfloat16
-VMEM_LIMIT = 24 * 1024 * 1024
+VMEM_LIMIT = 16 * 1024 * 1024
+VMEM_WHOLE = 64 * 1024 * 1024
+CHUNKS = 4
 
 SMEM_SPEC = pl.BlockSpec(memory_space=pltpu.SMEM)
 VMEM_SPEC = pl.BlockSpec(memory_space=pltpu.VMEM)
@@ -18,8 +20,8 @@
 HBM_SPEC = pl.BlockSpec(memory_space=pltpu.HBM)
 
 
-def params():
-    return pltpu.CompilerParams(vmem_limit_bytes=VMEM_LIMIT)
+def params(limit=VMEM_LIMIT):
+    return pltpu.CompilerParams(vmem_limit_bytes=limit)
 
 
 def cost(microseconds, transferred):
@@ -99,6 +101,7 @@
     wide_ref[:, pl.ds(0, deg)] = bessel_ref[...].astype(F32)
     wide_ref[:, pl.ds(deg, 256)] = jnp.zeros((modes, 256), F32)
     lane = lax.broadcasted_iota(jnp.int32, (modes, 128), 1)
+    tile = lax.broadcasted_iota(jnp.int32, (16, 128), 1) >> 5
 
     def step(k, start):
         base = pl.multiple_of((start >> 7) << 7, 128)
@@ -106,7 +109,13 @@
         back = (128 - shift) & 127
         low = pltpu.roll(wide_ref[:, pl.ds(base, 128)], back, 1)
         high = pltpu.roll(wide_ref[:, pl.ds(base + 128, 128)], back, 1)
-        out_ref[k, 16:, :] = jnp.where(lane < 128 - shift, low, high).astype(BF16)
+        block = jnp.where(lane < 128 - shift, low, high)
+        for j in range(4):
+            row = block[16 * j : 16 * j + 16]
+            for m in range(4):
+                if m != j:
+                    row = jnp.where(tile == m, pltpu.roll(block[16 * m : 16 * m + 16], (32 * (m - j)) % 128, 1), row)
+            out_ref[k, 16 + 16 * j : 32 + 16 * j, :] = row.astype(BF16)
         return start + lengths_ref[k]
 
     lax.fori_loop(0, blocks, step, jnp.int32(0), unroll=4)
@@ -164,39 +173,46 @@
 
 def radial_kernel(lengths_ref, recv_ref, out_ref, wide_ref, turned_ref):
     length = lengths_ref[lax.axis_index("radial")]
-    modes = 64
-    wide_ref[...] = recv_ref[:, 16:].astype(F32).reshape(32 * modes, 128)
-    slot = lax.broadcasted_iota(jnp.int32, (128, 128), 1)
-    group = lax.broadcasted_iota(jnp.int32, (128, 128), 0)
-    keep = ((slot >> 5) == (group >> 5)) & (slot < length)
-
-    def step(n, carry):
-        x = wide_ref[pl.ds(n, 32, stride=modes), :]
-        x = jnp.where(keep, jnp.concatenate([x] * 4, axis=0), 0.0)
-        turned = jnp.transpose(x)
-        for j in range(4):
-            turned_ref[pl.ds(j * modes + n, 32, stride=4 * modes), :] = turned[32 * j : 32 * j + 32]
+    wide_ref[...] = recv_ref[:, 16:].astype(F32).reshape(wide_ref.shape)
+    lane = lax.broadcasted_iota(jnp.int32, (128, 128), 1)
+    row = lax.broadcasted_iota(jnp.int32, (128, 128), 0)
+    keep = 32 * (row >> 5) + (lane & 31) < length
+
+    def step(a, carry):
+        x = jnp.concatenate([wide_ref[pl.ds(16 * j + a, 32, stride=64), :] for j in range(4)], axis=0)
+        turned = jnp.transpose(jnp.where(keep, x, 0.0))
+        for m in range(4):
+            turned_ref[pl.ds(16 * m + a, 32, stride=64), :] = turned[32 * m : 32 * m + 32]
         return carry
 
-    lax.fori_loop(0, modes, step, 0, unroll=2)
+    lax.fori_loop(0, 16, step, 0, unroll=4)
+    out_ref[...] = turned_ref[...].astype(BF16).reshape(out_ref.shape)
+
+
+def final_kernel(radial_ref, *refs):
+    pieces, out_ref, right_ref, block_ref, sems = refs[:8], refs[8], refs[9], refs[10], refs[11]
+    mine = lax.axis_index("shell")
+    group = lax.broadcasted_iota(jnp.int32, (64, 128), 1) >> 5
+    zero = jnp.zeros((64, 128), BF16)
+    per = 32 // CHUNKS
+    copies = []
     for g in range(32):
-        out_ref[g] = turned_ref[pl.ds(g * 256, 256), :].astype(BF16)
-
-
-def final_kernel(radial_ref, *refs):
-    pieces, out_ref, right_ref = refs[:8], refs[8], refs[9]
-    mine = lax.axis_index("shell")
-    steps = out_ref.shape[1]
-    for i in range(steps):
-        g = pl.program_id(0) * steps + i
         for d in range(8):
             h = mine ^ d
-            piece = pieces[d][pl.ds(pl.multiple_of(g * 16, 16), 16), :].astype(F32)
-            right_ref[i, 0, h] = piece[:8]
-            right_ref[i, 1, h] = piece[8:]
-        right = right_ref[i].reshape(128, 128).astype(BF16)
-        result = lax.dot_general(radial_ref[g], right, (((1,), (1,)), ((), ())), preferred_element_type=F32)
-        out_ref[:, i] = result.reshape(4, 64, 128).astype(BF16)
+            piece = pieces[d][g * 16 : g * 16 + 16, :].astype(F32)
+            right_ref[g, 0, h] = piece[:8]
+            right_ref[g, 1, h] = piece[8:]
+        right = right_ref[g].reshape(128, 128).astype(BF16)
+        left = jnp.concatenate([jnp.where(group == j, radial_ref[g], zero) for j in range(4)], axis=0)
+        result = lax.dot_general(left, right, (((1,), (1,)), ((), ())), preferred_element_type=F32)
+        block_ref[:, g] = result.reshape(4, 64, 128).astype(BF16)
+        if g % per == per - 1:
+            part = pl.ds(g + 1 - per, per)
+            copy = pltpu.make_async_copy(block_ref.at[:, part], out_ref.at[:, part], sems.at[g // per])
+            copy.start()
+            copies.append(copy)
+    for copy in copies:
+        copy.wait()
 
 
 def on_device(density, footprint, cycle_index, order_values, block_lengths, legendre, bessel):
@@ -217,7 +233,7 @@
             pltpu.VMEM((1, rows, nphi), jnp.int32),
             dma((4,)),
         ],
-        compiler_params=params(),
+        compiler_params=params(VMEM_WHOLE),
         cost_estimate=cost(2, 1 << 19),
         name="dft",
     )(cycle_index, order_values, density, footprint)
@@ -279,25 +295,23 @@
 
     radial = pl.pallas_call(
         radial_kernel,
-        out_shape=shape((32, 4 * modes, 128), BF16),
+        out_shape=shape((32, modes, 128), BF16),
         in_specs=[SMEM_SPEC, VMEM_SPEC],
         out_specs=VMEM_SPEC,
-        scratch_shapes=[pltpu.VMEM((32 * modes, 128), F32), pltpu.VMEM((128 * modes, 128), F32)],
-        compiler_params=params(),
-        cost_estimate=cost(5, 1 << 21),
+        scratch_shapes=[pltpu.VMEM((32 * modes, 128), F32), pltpu.VMEM((32 * modes, 128), F32)],
+        compiler_params=params(),
+        cost_estimate=cost(3, 1 << 20),
         name="radial_rows",
     )(block_lengths, recv)
 
-    step = 4
     out = pl.pallas_call(
         final_kernel,
         out_shape=shape((4, 32, modes, 128), BF16),
-        grid=(32 // step,),
         in_specs=[VMEM_SPEC] * 9,
-        out_specs=pl.BlockSpec((4, step, modes, 128), lambda g: (0, g, 0, 0)),
-        scratch_shapes=[pltpu.VMEM((step, 2, 8, 8, 128), F32)],
-        compiler_params=params(),
-        cost_estimate=cost(4, 1 << 22),
+        out_specs=HBM_SPEC,
+        scratch_shapes=[pltpu.VMEM((32, 2, 8, 8, 128), F32), pltpu.VMEM((4, 32, modes, 128), BF16), dma((CHUNKS,))],
+        compiler_params=params(),
+        cost_estimate=cost(2, 1 << 22),
         name="combine",
     )(radial, *[pieces[d] for d in range(8)])
     return out.reshape(128, modes, 128)

time: 69.5 us -> 60.7 us (0.87)
  Pallas kernels: 17.3 us -> 11.7 us
  waiting for transfers between devices: 18.4 us -> 16 us
  local copies, waits for them, and re-layouts: 5.42 us -> 3.8 us
  starting transfers between devices: 27.9 us -> 28.7 us
    pallas_call x1, Pallas kernels: 6.31 us -> 2.05 us  [on_device(): pl.pallas_call(radial_kernel, out_shape=shape((32, modes, 128), BF16), in...]
    pallas_call x1, Pallas kernels: 4.13 us -> 1.68 us  [on_device(): pl.pallas_call(final_kernel, out_shape=shape((4, 32, modes, 128), BF16),...]
    all_to_all x1, waiting for transfers between devices: 2.48 us -> 0.13 us  [on_device(): lax.all_to_all(four.reshape(8, 16, 128), 'shell', split_axis=0, concat_ax...]
    unnamed x16 -> x10, local copies, waits for them, and re-layouts: 5.42 us -> 3.8 us
    ppermute x7, starting transfers between devices: 10.9 us -> 11.7 us  [swap(): return lax.ppermute(x, 'shell', [(i, i ^ d) for i in range(8)])]
    pallas_call x1, Pallas kernels: 2.25 us -> 3 us  [on_device(): pl.pallas_call(send_kernel, out_shape=shape((32, 16 + modes, 128), BF16),...]
  transfers between devices with their start and end apart: 9 -> 9, of which waited for: 2 -> 2; matrix products, arithmetic and copies ran while one was open for 0% -> 0% of each run, Pallas kernels for 13% -> 9%
where the time goes in v3:
time: 60.7 us; the launch traced here: 60.4 us
  starting transfers between devices  28.7 us (47%)
  waiting for transfers between devices  16 us (26%)
  Pallas kernels  11.7 us (19%)
  local copies, waits for them, and re-layouts  3.8 us (6%)
    all_to_all x1, waiting for transfers between devices, on_device(): lax.all_to_all(send, 'radial', split_axis=0, concat_axis=0, tiled=True)  15.9 us
    ppermute x7, starting transfers between devices, swap(): return lax.ppermute(x, 'shell', [(i, i ^ d) for i in range(8)])  11.7 us
    all_to_all x1, starting transfers between devices, on_device(): lax.all_to_all(send, 'radial', split_axis=0, concat_axis=0, tiled=True)  10.5 us
    all_to_all x1, starting transfers between devices, on_device(): lax.all_to_all(four.reshape(8, 16, 128), 'shell', split_axis=0, concat_ax...  6.48 us
    unnamed x10, local copies, waits for them, and re-layouts  3.8 us
    pallas_call x1, Pallas kernels, on_device(): pl.pallas_call(send_kernel, out_shape=shape((32, 16 + modes, 128), BF16),...  3 us
    pallas_call x1, Pallas kernels, on_device(): pl.pallas_call(dft_kernel, out_shape=shape((128, 128), BF16), in_specs=[H...  2.54 us
    pallas_call x1, Pallas kernels, on_device(): pl.pallas_call(radial_kernel, out_shape=shape((32, modes, 128), BF16), in...  2.05 us
  transfers between devices with their start and end apart: 9, of which 2 were waited for; matrix products, arithmetic and copies ran while one was open for 0% of the time, Pallas kernels for 9%

profile of v3, /device:TPU:1, one launch (start us, length us, event | category | flops | bytes accessed | tf_op | source)
XLA Modules:
  0.0 60.4 jit_solution(12903369648548302494)
XLA Ops:
  0.0 2.5 %dft.1 = bf16[128,128]{1,0:T(8,128)(2,1)} custom-call(s32[16]{0:T(128)} %cycle_hbm.1, s32[64]{0:T(128)} %order_ref.1, f32[1,16,4096]{2,1,0:T(8,128)} %density_hbm.1, s32[1,16,4096]{2,1,0:T(8,128)} %footprint_hbm.1), custom_call_target="tpu_custom_call" | custom-call | flops 1000000000 | bytes 524288 | tf_op jit(solution)/shard_map/dft/pallas_call | solution.py:224
  2.5 0.0 copy-start.2
  2.6 6.5 %all-to-all-start = ((bf16[8,16,128]{2,1,0:T(8,128)(2,1)}), bf16[8,16,128]{2,1,0:T(8,128)(2,1)S(1)}, u32[]{:S(2)}, u32[]{:S(2)}) async-start(bf16[8,16,128]{2,1,0:T(8,128)(2,1)} %bitcast.6), calls=%async_computation | async-start | bytes 65536 | tf_op jit(solution)/shard_map/all_to_all | solution.py:240
  9.0 0.7 %copy-done.1 = s32[32]{0:T(128)S(1)} copy-done((s32[32]{0:T(128)S(1)}, s32[32]{0:T(128)}, u32[]{:S(2)}) %copy-start.1) | copy-done | bytes 152
  9.7 0.9 %copy-done.3 = bf16[1,2048,64]{1,2,0:T(8,128)(2,1)S(1)} copy-done((bf16[1,2048,64]{1,2,0:T(8,128)(2,1)S(1)}, bf16[1,2048,64]{1,2,0:T(8,128)(2,1)}, u32[]{:S(2)}) %copy-start.3) | copy-done | bytes 262168
  10.6 3.0 %bessel_send.1.send_ref = bf16[32,80,128]{2,1,0:T(8,128)(2,1)} custom-call(s32[32]{0:T(128)S(1)} %copy-done.1, bf16[64,2048]{1,0:T(8,128)(2,1)S(1)} %bitcast.5), custom_call_target="tpu_custom_call" | custom-call | flops 1000000000 | bytes 1048576 | tf_op jit(solution)/shard_map/bessel_send/pallas_call | solution.py:242
  13.6 0.1 all-to-all-done.parts_ref
  13.8 0.7 %fill.1 = bf16[32,80,128]{2,1,0:T(8,128)(2,1)} custom-call(bf16[8,16,128]{2,1,0:T(8,128)(2,1)S(1)} %all-to-all-done.parts_ref, bf16[32,80,128]{2,1,0:T(8,128)(2,1)} %bessel_send.1.send_ref), custom_call_target="tpu_custom_call", output_to_operand_aliasing={{}: (1, {})} | custom-call | flops 500000000 | bytes 131072 | tf_op jit(solution)/shard_map/fill/pallas_call | solution.py:252
  14.5 10.5 %all-to-all-start.1 = ((bf16[32,80,128]{2,1,0:T(8,128)(2,1)}), bf16[32,80,128]{2,1,0:T(8,128)(2,1)S(1)}, u32[]{:S(2)}, u32[]{:S(2)}) async-start(bf16[32,80,128]{2,1,0:T(8,128)(2,1)} %fill.1), calls=%async_computation.1 | async-start | bytes 1310720 | tf_op jit(solution)/shard_map/all_to_all | solution.py:263
  25.0 0.0 copy-done.2
  25.0 0.0 copy-start
  25.0 2.2 %copy-done = bf16[8,2048,128]{2,1,0:T(8,128)(2,1)S(1)} copy-done((bf16[8,2048,128]{2,1,0:T(8,128)(2,1)S(1)}, bf16[8,2048,128]{2,1,0:T(8,128)(2,1)}, u32[]{:S(2)}) %copy-start) | copy-done | bytes 4194328
  27.2 0.7 %legendre_rows.1.rows_ref = bf16[8,128,128]{2,1,0:T(8,128)(2,1)S(1)} custom-call(s32[32]{0:T(128)S(1)} %copy-done.2, bf16[8,2048,128]{2,1,0:T(8,128)(2,1)S(1)} %copy-done), custom_call_target="tpu_custom_call" | custom-call | flops 500000000 | bytes 524288 | tf_op jit(solution)/shard_map/legendre_rows/pallas_call | solution.py:265
  27.9 15.9 %all-to-all-done.1.recv_ref = bf16[32,80,128]{2,1,0:T(8,128)(2,1)S(1)} async-done(((bf16[32,80,128]{2,1,0:T(8,128)(2,1)}), bf16[32,80,128]{2,1,0:T(8,128)(2,1)S(1)}, u32[]{:S(2)}, u32[]{:S(2)}) %all-to-all-start.1) | async-done | bytes 655392 | tf_op jit(solution)/shard_map/all_to_all | solution.py:263
  43.8 0.0 copy-done.4
  43.8 1.1 %harmonic.1.refs_0_ = bf16[512,128]{1,0:T(8,128)(2,1)S(1)} custom-call(s32[32]{0:T(128)S(1)} %copy-done.2, s32[64]{0:T(128)S(1)} %copy-done.4, bf16[32,80,128]{2,1,0:T(8,128)(2,1)S(1)} %all-to-all-done.1.recv_ref, bf16[8,128,128]{2,1,0:T(8,128)(2,1)S(1)} %legendre_rows.1.rows_ref), custom_call_target="tpu_custom_call" | custom-call | flops 500000000 | bytes 524288 | tf_op jit(solution)/shard_map/harmonic/pallas_call | solution.py:276
  44.9 2.6 %collective-permute-start.5 = (bf16[512,128]{1,0:T(8,128)(2,1)S(1)}, bf16[512,128]{1,0:T(8,128)(2,1)S(1)}, u32[]{:S(2)}, u32[]{:S(2)}) collective-permute-start(bf16[512,128]{1,0:T(8,128)(2,1)S(1)} %harmonic.1.refs_0_), channel_id=1, source_target_pairs={{0,192},{32,224},{64,128},{96,160},{128,64},{160,96},{192,0},{224,... | collective-permute-start | bytes 393224 | tf_op jit(solution)/shard_map/ppermute | solution.py:288
  47.5 0.6 collective-permute-start.3
  48.0 0.2 collective-permute-start.1
  48.2 3.2 %collective-permute-start = (bf16[512,128]{1,0:T(8,128)(2,1)S(1)}, bf16[512,128]{1,0:T(8,128)(2,1)S(1)}, u32[]{:S(2)}, u32[]{:S(2)}) collective-permute-start(bf16[512,128]{1,0:T(8,128)(2,1)S(1)} %harmonic.1.refs_0_), channel_id=1, source_target_pairs={{0,32},{32,0},{64,96},{96,64},{128,160},{160,128},{192,224},{224,1... | collective-permute-start | bytes 393224 | tf_op jit(solution)/shard_map/ppermute | solution.py:288
  51.5 0.0 collective-permute-done.5.refs_6_
  51.5 3.4 %collective-permute-start.6 = (bf16[512,128]{1,0:T(8,128)(2,1)S(1)}, bf16[512,128]{1,0:T(8,128)(2,1)S(1)}, u32[]{:S(2)}, u32[]{:S(2)}) collective-permute-start(bf16[512,128]{1,0:T(8,128)(2,1)S(1)} %collective-permute-done.5.refs_6_), channel_id=1, source_target_pairs={{0,32},{32,0},{64,96},{96,64},{128,160},{160,128},{192,224},{224,1... | collective-permute-start | bytes 393224 | tf_op jit(solution)/shard_map/ppermute | solution.py:288
  54.9 0.0 collective-permute-done.3.refs_4_
  54.9 1.7 %collective-permute-start.4 = (bf16[512,128]{1,0:T(8,128)(2,1)S(1)}, bf16[512,128]{1,0:T(8,128)(2,1)S(1)}, u32[]{:S(2)}, u32[]{:S(2)}) collective-permute-start(bf16[512,128]{1,0:T(8,128)(2,1)S(1)} %collective-permute-done.3.refs_4_), channel_id=1, source_target_pairs={{0,32},{32,0},{64,96},{96,64},{128,160},{160,128},{192,224},{224,1... | collective-permute-start | bytes 393224 | tf_op jit(solution)/shard_map/ppermute | solution.py:288
  56.6 0.0 collective-permute-done.1.refs_2_
  56.6 0.0 collective-permute-start.2
  56.6 2.0 %radial_rows.1.radial_ref = bf16[32,64,128]{2,1,0:T(8,128)(2,1)S(1)} custom-call(s32[32]{0:T(128)S(1)} %copy-done.2, bf16[32,80,128]{2,1,0:T(8,128)(2,1)S(1)} %all-to-all-done.1.recv_ref), custom_call_target="tpu_custom_call" | custom-call | flops 1500000000 | bytes 1048576 | tf_op jit(solution)/shard_map/radial_rows/pallas_call | solution.py:296
  58.7 0.0 collective-permute-done.refs_1_
  58.7 0.0 collective-permute-done.6.refs_7_
  58.7 0.0 collective-permute-done.4.refs_5_
  58.7 0.0 collective-permute-done.2.refs_3_
  58.7 1.7 %combine.1 = bf16[4,32,64,128]{3,2,1,0:T(8,128)(2,1)} custom-call(bf16[32,64,128]{2,1,0:T(8,128)(2,1)S(1)} %radial_rows.1.radial_ref, bf16[512,128]{1,0:T(8,128)(2,1)S(1)} %harmonic.1.refs_0_, bf16[512,128]{1,0:T(8,128)(2,1)S(1)} %collective-permute-done.refs_1_, bf16[512,128]{1,0:T(8,128)(2,1)S(1)} %collective-permute-done.1.refs_2_, ...), custom_call_target="tpu_custom_call" | custom-call | flops 1000000000 | bytes 4194304 | tf_op jit(solution)/shard_map/combine/pallas_call | solution.py:307
  (3 shorter events, 0.0 us)
Async XLA Ops:
  2.5 22.5 %copy-start.2 = (s32[32]{0:T(128)S(1)}, s32[32]{0:T(128)}, u32[]{:S(2)}) copy-start(s32[32]{0:T(128)} %lengths_ref.7) | copy-start | bytes 388
  2.6 11.2 %all-to-all-start = ((bf16[8,16,128]{2,1,0:T(8,128)(2,1)}), bf16[8,16,128]{2,1,0:T(8,128)(2,1)S(1)}, u32[]{:S(2)}, u32[]{:S(2)}) async-start(bf16[8,16,128]{2,1,0:T(8,128)(2,1)} %bitcast.6), calls=%async_computation | async-start | bytes 65536 | tf_op jit(solution)/shard_map/all_to_all | solution.py:240
  9.0 0.7 %copy-start.1 = (s32[32]{0:T(128)S(1)}, s32[32]{0:T(128)}, u32[]{:S(2)}) copy-start(s32[32]{0:T(128)} %lengths_ref.7) | copy-start | bytes 388
  9.7 0.9 %copy-start.3 = (bf16[1,2048,64]{1,2,0:T(8,128)(2,1)S(1)}, bf16[1,2048,64]{1,2,0:T(8,128)(2,1)}, u32[]{:S(2)}) copy-start(bf16[1,2048,64]{1,2,0:T(8,128)(2,1)} %param.13) | copy-start | bytes 786436
  13.6 30.1 %copy-start.4 = (s32[64]{0:T(128)S(1)}, s32[64]{0:T(128)}, u32[]{:S(2)}) copy-start(s32[64]{0:T(128)} %order_ref.1) | copy-start | bytes 772
  14.5 29.3 %all-to-all-start.1 = ((bf16[32,80,128]{2,1,0:T(8,128)(2,1)}), bf16[32,80,128]{2,1,0:T(8,128)(2,1)S(1)}, u32[]{:S(2)}, u32[]{:S(2)}) async-start(bf16[32,80,128]{2,1,0:T(8,128)(2,1)} %fill.1), calls=%async_computation.1 | async-start | bytes 1310720 | tf_op jit(solution)/shard_map/all_to_all | solution.py:263
  25.0 2.2 %copy-start = (bf16[8,2048,128]{2,1,0:T(8,128)(2,1)S(1)}, bf16[8,2048,128]{2,1,0:T(8,128)(2,1)}, u32[]{:S(2)}) copy-start(bf16[8,2048,128]{2,1,0:T(8,128)(2,1)} %legendre_ref.1) | copy-start | bytes 12582916
  44.9 6.6 %collective-permute-start.5 = (bf16[512,128]{1,0:T(8,128)(2,1)S(1)}, bf16[512,128]{1,0:T(8,128)(2,1)S(1)}, u32[]{:S(2)}, u32[]{:S(2)}) collective-permute-start(bf16[512,128]{1,0:T(8,128)(2,1)S(1)} %harmonic.1.refs_0_), channel_id=1, source_target_pairs={{0,192},{32,224},{64,128},{96,160},{128,64},{160,96},{192,0},{224,... | collective-permute-start | bytes 393224 | tf_op jit(solution)/shard_map/ppermute | solution.py:288
  47.5 7.4 %collective-permute-start.3 = (bf16[512,128]{1,0:T(8,128)(2,1)S(1)}, bf16[512,128]{1,0:T(8,128)(2,1)S(1)}, u32[]{:S(2)}, u32[]{:S(2)}) collective-permute-start(bf16[512,128]{1,0:T(8,128)(2,1)S(1)} %harmonic.1.refs_0_), channel_id=1, source_target_pairs={{0,128},{32,160},{64,192},{96,224},{128,0},{160,32},{192,64},{224,... | collective-permute-start | bytes 393224 | tf_op jit(solution)/shard_map/ppermute | solution.py:288
  48.0 8.6 %collective-permute-start.1 = (bf16[512,128]{1,0:T(8,128)(2,1)S(1)}, bf16[512,128]{1,0:T(8,128)(2,1)S(1)}, u32[]{:S(2)}, u32[]{:S(2)}) collective-permute-start(bf16[512,128]{1,0:T(8,128)(2,1)S(1)} %harmonic.1.refs_0_), channel_id=1, source_target_pairs={{0,64},{32,96},{64,0},{96,32},{128,192},{160,224},{192,128},{224,1... | collective-permute-start | bytes 393224 | tf_op jit(solution)/shard_map/ppermute | solution.py:288
  48.2 10.5 %collective-permute-start = (bf16[512,128]{1,0:T(8,128)(2,1)S(1)}, bf16[512,128]{1,0:T(8,128)(2,1)S(1)}, u32[]{:S(2)}, u32[]{:S(2)}) collective-permute-start(bf16[512,128]{1,0:T(8,128)(2,1)S(1)} %harmonic.1.refs_0_), channel_id=1, source_target_pairs={{0,32},{32,0},{64,96},{96,64},{128,160},{160,128},{192,224},{224,1... | collective-permute-start | bytes 393224 | tf_op jit(solution)/shard_map/ppermute | solution.py:288
  51.5 7.2 %collective-permute-start.6 = (bf16[512,128]{1,0:T(8,128)(2,1)S(1)}, bf16[512,128]{1,0:T(8,128)(2,1)S(1)}, u32[]{:S(2)}, u32[]{:S(2)}) collective-permute-start(bf16[512,128]{1,0:T(8,128)(2,1)S(1)} %collective-permute-done.5.refs_6_), channel_id=1, source_target_pairs={{0,32},{32,0},{64,96},{96,64},{128,160},{160,128},{192,224},{224,1... | collective-permute-start | bytes 393224 | tf_op jit(solution)/shard_map/ppermute | solution.py:288
  54.9 3.8 %collective-permute-start.4 = (bf16[512,128]{1,0:T(8,128)(2,1)S(1)}, bf16[512,128]{1,0:T(8,128)(2,1)S(1)}, u32[]{:S(2)}, u32[]{:S(2)}) collective-permute-start(bf16[512,128]{1,0:T(8,128)(2,1)S(1)} %collective-permute-done.3.refs_4_), channel_id=1, source_target_pairs={{0,32},{32,0},{64,96},{96,64},{128,160},{160,128},{192,224},{224,1... | collective-permute-start | bytes 393224 | tf_op jit(solution)/shard_map/ppermute | solution.py:288
  56.6 2.1 %collective-permute-start.2 = (bf16[512,128]{1,0:T(8,128)(2,1)S(1)}, bf16[512,128]{1,0:T(8,128)(2,1)S(1)}, u32[]{:S(2)}, u32[]{:S(2)}) collective-permute-start(bf16[512,128]{1,0:T(8,128)(2,1)S(1)} %collective-permute-done.1.refs_2_), channel_id=1, source_target_pairs={{0,32},{32,0},{64,96},{96,64},{128,160},{160,128},{192,224},{224,1... | collective-permute-start | bytes 393224 | tf_op jit(solution)/shard_map/ppermute | solution.py:288

commit v4 on v0

v4 whole, which is shorter than its diff:
```python
import math

import jax
import jax.numpy as jnp
from jax import lax
from jax.experimental import pallas as pl
from jax.experimental.pallas import tpu as pltpu
from jax.sharding import PartitionSpec as P

NSIDE = 1024
F32 = jnp.float32
BF16 = jnp.bfloat16
VMEM_LIMIT = 16 * 1024 * 1024
VMEM_WHOLE = 64 * 1024 * 1024

SMEM_SPEC = pl.BlockSpec(memory_space=pltpu.SMEM)
VMEM_SPEC = pl.BlockSpec(memory_space=pltpu.VMEM)
HBM_SPEC = pl.BlockSpec(memory_space=pltpu.HBM)


def params(limit=VMEM_LIMIT):
    return pltpu.CompilerParams(vmem_limit_bytes=limit)


def cost(microseconds, transferred):
    return pl.CostEstimate(flops=microseconds * 500_000_000, bytes_accessed=transferred, transcendentals=0)


def split_start(start):
    base = pl.multiple_of((start >> 7) << 7, 128)
    return base, start - base


def cos_sin(turns):
    quarter = (turns + 1024) >> 11
    x = (turns - (quarter << 11)).astype(F32) * (math.pi / 4096)
    z = x * x
    s = x + x * z * (-1.6666654611e-1 + z * (8.3321608736e-3 + z * -1.9515295891e-4))
    c = 1.0 - 0.5 * z + z * z * (4.166664568298827e-2 + z * (-1.388731625493765e-3 + z * 2.443315711809948e-5))
    odd = (quarter & 1) == 1
    even_sign = jnp.where((quarter & 2) == 2, -1.0, 1.0)
    cos = jnp.where(odd, -s, c) * even_sign
    sin = jnp.where(odd, c, s) * even_sign
    return cos, sin


def front_kernel(
    lengths_hbm, cycle_hbm, order_hbm, density_hbm, footprint_hbm, bessel_hbm, legendre_hbm, send_hbm, rows_hbm,
    lengths_ref, cycle_ref, order_ref, density_ref, footprint_ref, bessel_ref, low_ref, high_ref,
    block_ref, tile_ref, rows_ref, sems,
):
    _, rows, nphi = density_ref.shape
    modes, deg = bessel_ref.shape
    inputs = [
        (lengths_hbm, lengths_ref),
        (bessel_hbm, bessel_ref),
        (order_hbm, order_ref),
        (density_hbm, density_ref),
        (footprint_hbm, footprint_ref),
        (cycle_hbm, cycle_ref),
    ]
    copies = [pltpu.make_async_copy(source, target, sems.at[i]) for i, (source, target) in enumerate(inputs)]
    for copy in copies:
        copy.start()
    copies[0].wait()
    base, shift = split_start(block_start(lengths_ref))
    after = pl.multiple_of(jnp.minimum(base + 128, deg - 128), 128)
    windows = [
        pltpu.make_async_copy(legendre_hbm.at[:, pl.ds(base, 128), :], low_ref, sems.at[6]),
        pltpu.make_async_copy(legendre_hbm.at[:, pl.ds(after, 128), :], high_ref, sems.at[7]),
    ]
    for copy in windows:
        copy.start()
    copies[1].wait()
    lane = lax.broadcasted_iota(jnp.int32, (modes, 128), 1)
    tile = lax.broadcasted_iota(jnp.int32, (16, 128), 1) >> 5

    def step(k, start):
        base, shift = split_start(start)
        after = pl.multiple_of(jnp.minimum(base + 128, deg - 128), 128)
        block = jnp.where(lane >= shift, bessel_ref[:, pl.ds(base, 128)], bessel_ref[:, pl.ds(after, 128)])
        for j in range(4):
            row = block[16 * j : 16 * j + 16]
            for i in range(4):
                if i != j:
                    row = jnp.where(tile == i, pltpu.roll(block[16 * i : 16 * i + 16], (32 * (i - j)) % 128, 1), row)
            block_ref[k, 16 * j : 16 * j + 16, :] = row
        return start + lengths_ref[k]

    lax.fori_loop(0, block_ref.shape[0], step, jnp.int32(0), unroll=4)
    outputs = [pltpu.make_async_copy(block_ref, send_hbm.at[:, pl.ds(16, modes), :], sems.at[8])]
    outputs[0].start()

    for copy in windows:
        copy.wait()
    slot = lax.broadcasted_iota(jnp.int32, (128, 128), 0)
    for q in range(rows_ref.shape[0]):
        rows_ref[q] = jnp.where(slot >= shift, low_ref[q], high_ref[q])
    outputs.append(pltpu.make_async_copy(rows_ref, rows_hbm, sems.at[9]))
    outputs[1].start()

    for copy in copies[2:]:
        copy.wait()
    lane = lax.broadcasted_iota(jnp.int32, (1, 128), 1)
    part = (lane >> 5) & 1
    order_slot = 2 * (lane & 31) + (lane >> 6)
    order = jnp.zeros((1, 128), jnp.int32)
    for q in range(64):
        order = jnp.where(order_slot == q, order_ref[q], order)
    sixty_four = lax.broadcasted_iota(jnp.int32, (64, 128), 0)
    pa, qa = cos_sin((sixty_four * 128 * order + 2048 * part) & 8191)
    qa = -qa
    cb, sb = cos_sin((sixty_four * 2 * order) & 8191)
    total = jnp.zeros((2 * rows, 256), F32)
    for chunk in range(nphi // 256):
        tables = []
        for a in range(4 * chunk, 4 * chunk + 4):
            tables.append(pa[a : a + 1] * cb + qa[a : a + 1] * sb)
        table = jnp.concatenate(tables, axis=0)
        high = table.astype(BF16)
        low = (table - high.astype(F32)).astype(BF16)
        cut = slice(256 * chunk, 256 * chunk + 256)
        pixels = density_ref[0, :, cut] * footprint_ref[0, :, cut].astype(F32)
        p_high = pixels.astype(BF16)
        p_low = (pixels - p_high.astype(F32)).astype(BF16)
        total = total + jnp.dot(
            jnp.concatenate([p_high, p_low], axis=0),
            jnp.concatenate([high, low], axis=1),
            preferred_element_type=F32,
        )
    x = total[:rows, :128] + (total[:rows, 128:] + total[rows:, :128])
    row = lax.broadcasted_iota(jnp.int32, (rows, 128), 0)
    cycle = jnp.zeros((rows, 128), jnp.int32)
    for r in range(rows):
        cycle = jnp.where(row == r, cycle_ref[r], cycle)
    parity = (cycle - (NSIDE - 1)) & 1
    cos_t, sin_t = cos_sin((order * (2 - parity)) & 8191)
    other = jnp.where(part == 0, pltpu.roll(x, 96, 1), -pltpu.roll(x, 32, 1))
    four = (x * cos_t + other * sin_t).astype(BF16)
    tile_ref[...] = jnp.broadcast_to(four[None], tile_ref.shape)
    outputs.append(pltpu.make_async_copy(tile_ref, send_hbm.at[:, pl.ds(0, 16), :], sems.at[10]))
    outputs[2].start()
    for copy in outputs:
        copy.wait()


def turn_kernel(recv_ref, out_ref, wide_ref, turned_ref):
    wide_ref[...] = recv_ref[:, :16].astype(F32).reshape(512, 128)
    tile = lax.broadcasted_iota(jnp.int32, (32, 128), 1) >> 5
    for a in range(4):
        x = [wide_ref[pl.ds(4 * a + b, 32, stride=16), :] for b in range(4)]
        pieces = []
        for u in range(4):
            piece = x[u]
            for b in range(4):
                if b != u:
                    piece = jnp.where(tile == b, pltpu.roll(x[b], (32 * (b - u)) % 128, 1), piece)
            pieces.append(piece)
        turned = jnp.transpose(jnp.concatenate(pieces, axis=0))
        for b in range(4):
            turned_ref[pl.ds(4 * a + b, 32, stride=16), :] = turned[32 * b : 32 * b + 32]
    out_ref[...] = turned_ref[...].astype(BF16)


def block_start(lengths_ref):
    return lax.fori_loop(0, lax.axis_index("radial"), lambda k, total: total + lengths_ref[k], jnp.int32(0))


def radial_kernel(lengths_ref, recv_ref, out_ref, wide_ref, turned_ref):
    length = lengths_ref[lax.axis_index("radial")]
    start = block_start(lengths_ref)
    wide_ref[...] = recv_ref[:, 16:].astype(F32).reshape(wide_ref.shape)
    lane = lax.broadcasted_iota(jnp.int32, (128, 128), 1)
    row = lax.broadcasted_iota(jnp.int32, (128, 128), 0)
    slot = 32 * (row >> 5) + (lane & 31)
    keep = ((slot - start) & 127) < length

    def step(a, carry):
        x = jnp.concatenate([wide_ref[pl.ds(16 * j + a, 32, stride=64), :] for j in range(4)], axis=0)
        turned = jnp.transpose(jnp.where(keep, x, 0.0))
        for m in range(4):
            turned_ref[pl.ds(16 * m + a, 32, stride=64), :] = turned[32 * m : 32 * m + 32]
        return carry

    lax.fori_loop(0, 16, step, 0, unroll=4)
    out_ref[...] = turned_ref[...].astype(BF16).reshape(out_ref.shape)


def final_kernel(lengths_ref, order_ref, radial_ref, *refs):
    fours, rows, out_ref = refs[:8], refs[8:16], refs[16]
    four_ref, harmonic_ref, block_ref, sems = refs[17:]
    mine = lax.axis_index("shell")
    start = block_start(lengths_ref)
    base, shift = split_start(start)
    for d in range(8):
        four_ref[:, mine ^ d] = fours[d][...].reshape(32, 16, 128)
    lane = lax.broadcasted_iota(jnp.int32, (128, 128), 1)
    slot = lax.broadcasted_iota(jnp.int32, (128, 128), 0)
    degree = base + slot + jnp.where(slot < shift, 128, 0)
    first_half = lane < 64
    tile = lax.broadcasted_iota(jnp.int32, (32, 128), 1) >> 5
    for d in range(8):
        for i in range(4):
            pair = 4 * (mine ^ d) + i
            left = rows[d][2 * i : 2 * i + 2].reshape(256, 128)
            both = jnp.dot(left, four_ref[pair].reshape(128, 128), preferred_element_type=F32)
            value = jnp.where(first_half, both[:128], both[128:])
            order = jnp.where(first_half, order_ref[2 * pair], order_ref[2 * pair + 1])
            value = jnp.where(degree >= order, value, 0.0)
            for u in range(4):
                packed = value[32 * u : 32 * u + 32]
                for j in range(4):
                    if j != u:
                        packed = jnp.where(tile == j, pltpu.roll(value[32 * j : 32 * j + 32], (32 * (j - u)) % 128, 1), packed)
                harmonic_ref[pl.ds(2 * pair + (u & 1) * 64 + (u >> 1), 32, stride=128), :] = packed
    group = lax.broadcasted_iota(jnp.int32, (64, 128), 1) >> 5
    zero = jnp.zeros((64, 128), BF16)
    for g in range(32):
        right = harmonic_ref[128 * g : 128 * g + 128, :].astype(BF16)
        left = jnp.concatenate([jnp.where(group == j, radial_ref[g], zero) for j in range(4)], axis=0)
        result = lax.dot_general(left, right, (((1,), (1,)), ((), ())), preferred_element_type=F32)
        block_ref[:, g] = result.reshape(4, 64, 128).astype(BF16)
        if g % 8 == 7:
            for j in range(4):
                first = g - 7
                sem = sems.at[4 * (g // 8) + j]
                row = (32 * j + first - start) & 127

                @pl.when(row <= 120)
                def _(j=j, first=first, sem=sem, row=row):
                    pltpu.make_async_copy(block_ref.at[j, pl.ds(first, 8)], out_ref.at[pl.ds(row, 8)], sem).start()

                @pl.when(row > 120)
                def _(j=j, first=first, sem=sem, row=row):
                    for i in range(8):
                        pltpu.make_async_copy(block_ref.at[j, first + i], out_ref.at[(row + i) & 127], sem).start()

    for i in range(16):
        pltpu.make_async_copy(block_ref.at[0, pl.ds(0, 8)], out_ref.at[pl.ds(0, 8)], sems.at[i]).wait()


def on_device(density, footprint, cycle_index, order_values, block_lengths, legendre, bessel):
    shape = jax.ShapeDtypeStruct
    rows, nphi = density.shape[1:]
    deg, modes = bessel.shape[1:]
    dma = pltpu.SemaphoreType.DMA

    def swap(x, d):
        return lax.ppermute(x, "shell", [(i, i ^ d) for i in range(8)])

    send, leg_rows = pl.pallas_call(
        front_kernel,
        out_shape=[shape((32, 16 + modes, 128), BF16), shape((8, 128, 128), BF16)],
        in_specs=[HBM_SPEC] * 7,
        out_specs=[HBM_SPEC] * 2,
        scratch_shapes=[
            pltpu.SMEM((32,), jnp.int32),
            pltpu.SMEM((rows,), jnp.int32),
            pltpu.SMEM((64,), jnp.int32),
            pltpu.VMEM((1, rows, nphi), F32),
            pltpu.VMEM((1, rows, nphi), jnp.int32),
            pltpu.VMEM((modes, deg), BF16),
            pltpu.VMEM((8, 128, 128), BF16),
            pltpu.VMEM((8, 128, 128), BF16),
            pltpu.VMEM((32, modes, 128), BF16),
            pltpu.VMEM((32, 16, 128), BF16),
            pltpu.VMEM((8, 128, 128), BF16),
            dma((11,)),
        ],
        compiler_params=params(VMEM_WHOLE),
        cost_estimate=cost(4, 1 << 21),
        name="front",
    )(block_lengths, cycle_index, order_values, density, footprint, jnp.swapaxes(bessel, 1, 2).reshape(modes, deg), legendre)
    recv = lax.all_to_all(send, "radial", split_axis=0, concat_axis=0, tiled=True)

    row_pieces = {0: leg_rows}
    for d in (4, 2, 6):
        row_pieces[d] = swap(leg_rows, d)
    for d in (0, 4, 2, 6):
        row_pieces[d + 1] = swap(row_pieces[d], 1)

    four = pl.pallas_call(
        turn_kernel,
        out_shape=shape((512, 128), BF16),
        in_specs=[VMEM_SPEC],
        out_specs=VMEM_SPEC,
        scratch_shapes=[pltpu.VMEM((512, 128), F32), pltpu.VMEM((512, 128), F32)],
        compiler_params=params(),
        cost_estimate=cost(1, 1 << 19),
        name="turn",
    )(recv)

    radial = pl.pallas_call(
        radial_kernel,
        out_shape=shape((32, modes, 128), BF16),
        in_specs=[SMEM_SPEC, VMEM_SPEC],
        out_specs=VMEM_SPEC,
        scratch_shapes=[pltpu.VMEM((32 * modes, 128), F32), pltpu.VMEM((32 * modes, 128), F32)],
        compiler_params=params(),
        cost_estimate=cost(3, 1 << 20),
        name="radial_rows",
    )(block_lengths, recv)

    pieces = {0: four}
    for d in (2, 6, 4):
        pieces[d] = swap(four, d)
    own, radial = lax.optimization_barrier((four, radial))
    pieces[1] = swap(own, 1)
    for d in (2, 6, 4):
        pieces[d + 1] = swap(pieces[d], 1)

    return pl.pallas_call(
        final_kernel,
        out_shape=shape((128, modes, 128), BF16),
        in_specs=[SMEM_SPEC] * 2 + [VMEM_SPEC] * 17,
        out_specs=HBM_SPEC,
        scratch_shapes=[
            pltpu.VMEM((32, 8, 16, 128), BF16),
            pltpu.VMEM((32 * 128, 128), F32),
            pltpu.VMEM((4, 32, modes, 128), BF16),
            dma((16,)),
        ],
        compiler_params=params(),
        cost_estimate=cost(5, 1 << 22),
        name="finish",
    )(block_lengths, order_values, radial, *[pieces[d] for d in range(8)], *[row_pieces[d] for d in range(8)])


def solution(mesh):
    return jax.shard_map(
        on_device,
        mesh=mesh,
        in_specs=(
            P("radial", "shell", None),
            P("radial", "shell", None),
            P("shell"),
            P(),
            P(),
            P("shell", None, None),
            P("radial", None, "shell"),
        ),
        out_specs=P("radial", "shell", None),
        check_vma=False,
    )
```

time: 179 us -> 54.5 us (0.30)
  local copies, waits for them, and re-layouts: 71.7 us -> 0.67 us
  other arithmetic: 31.9 us -> 0 us
  blocking collectives: 14.1 us -> 0 us
  Pallas kernels: 0 us -> 12.1 us
  matrix products: 10.6 us -> 0 us
  waiting for transfers between devices: 22.8 us -> 12.4 us
  starting transfers between devices: 26.7 us -> 28.8 us
    gather x3 -> x0, local copies, waits for them, and re-layouts: 28.4 us -> none  [the longest x2 16.3 us: on_device(): send_wide = jnp.take(every_order, rows, axis=3) * slot_keep]
    unnamed x1 -> x0, other arithmetic: 22.4 us -> none
    all_to_all x3 -> x1, waiting for transfers between devices: 22.8 us -> 2.23 us  [on_device(): lax.all_to_all(send, 'radial', split_axis=0, concat_axis=0, tiled=True)]
    select_n x1 -> x0, local copies, waits for them, and re-layouts: 16.7 us -> none  [on_device(): radial_send = jnp.take(bessel, rows, axis=1)]
    ppermute x0 -> x14, starting transfers between devices: none -> 16.7 us  [swap(): return lax.ppermute(x, 'shell', [(i, i ^ d) for i in range(8)])]
    unnamed x19 -> x6, local copies, waits for them, and re-layouts: 15.5 us -> 0.67 us
    all_to_all x3 -> x1, starting transfers between devices: 26.7 us -> 12.2 us  [on_device(): lax.all_to_all(send, 'radial', split_axis=0, concat_axis=0, tiled=True)]
    all_gather x1 -> x0, blocking collectives: 14.1 us -> none  [on_device(): every_order = lax.all_gather(harmonic, 'shell', axis=1, tiled=True)]
  transfers between devices with their start and end apart: 3 -> 15, of which waited for: 1 -> 4; matrix products, arithmetic and copies ran while one was open for 50% -> 0% of each run, Pallas kernels for 0% -> 5%
where the time goes in v4:
time: 54.5 us; the launch traced here: 54.3 us
  starting transfers between devices  28.8 us (53%)
  waiting for transfers between devices  12.4 us (23%)
  Pallas kernels  12.1 us (22%)
  local copies, waits for them, and re-layouts  0.67 us (1%)
    ppermute x14, starting transfers between devices, swap(): return lax.ppermute(x, 'shell', [(i, i ^ d) for i in range(8)])  16.7 us
    all_to_all x1, starting transfers between devices, on_device(): lax.all_to_all(send, 'radial', split_axis=0, concat_axis=0, tiled=True)  12.2 us
    ppermute x14, waiting for transfers between devices, swap(): return lax.ppermute(x, 'shell', [(i, i ^ d) for i in range(8)])  10.2 us
    pallas_call x1, Pallas kernels, on_device(): pl.pallas_call(final_kernel, out_shape=shape((128, modes, 128), BF16), in...  5.94 us
    pallas_call x1, Pallas kernels, on_device(): pl.pallas_call(front_kernel, out_shape=[shape((32, 16 + modes, 128), BF16...  3.64 us
    all_to_all x1, waiting for transfers between devices, on_device(): lax.all_to_all(send, 'radial', split_axis=0, concat_axis=0, tiled=True)  2.23 us
    pallas_call x1, Pallas kernels, on_device(): pl.pallas_call(radial_kernel, out_shape=shape((32, modes, 128), BF16), in...  2.06 us
  transfers between devices with their start and end apart: 15, of which 4 were waited for; matrix products, arithmetic and copies ran while one was open for 0% of the time, Pallas kernels for 5%

profile of v4, /device:TPU:1, one launch (start us, length us, event | category | flops | bytes accessed | tf_op | source)
XLA Modules:
  0.0 54.3 jit_solution(11747319273571034249)
XLA Ops:
  0.0 3.6 %front.1 = (bf16[32,80,128]{2,1,0:T(8,128)(2,1)}, bf16[8,128,128]{2,1,0:T(8,128)(2,1)}) custom-call(s32[32]{0:T(128)} %lengths_ref.3, s32[16]{0:T(128)} %cycle_hbm.1, s32[64]{0:T(128)} %order_ref.1, f32[1,16,4096]{2,1,0:T(8,128)} %density_hbm.1, s32[1,16,4096]{2,1,0:T(8,128)} %footprint_hbm.1, bf16[64,2048]{1,0:T(8,128)(2,1)} %bitcast.3, ...), custom_call_target="tpu_custom_call" | custom-call | flops 2000000000 | bytes 2097152 | tf_op jit(solution)/shard_map/front/pallas_call | solution.py:251
  3.7 0.0 copy-start.2
  3.7 12.2 %all-to-all-start = ((bf16[32,80,128]{2,1,0:T(8,128)(2,1)}), bf16[32,80,128]{2,1,0:T(8,128)(2,1)S(1)}, u32[]{:S(2)}, u32[]{:S(2)}) async-start(bf16[32,80,128]{2,1,0:T(8,128)(2,1)} %get-tuple-element.9), calls=%async_computation | async-start | bytes 1310720 | tf_op jit(solution)/shard_map/all_to_all | solution.py:274
  15.9 2.6 %collective-permute-start.12 = (bf16[8,128,128]{2,1,0:T(8,128)(2,1)}, bf16[8,128,128]{2,1,0:T(8,128)(2,1)S(1)}, u32[]{:S(2)}, u32[]{:S(2)}) collective-permute-start(bf16[8,128,128]{2,1,0:T(8,128)(2,1)} %get-tuple-element.12.refs_8_), channel_id=1, source_target_pairs={{0,192},{32,224},{64,128},{96,160},{128,64},{160,96},{192,0},{224,... | collective-permute-start | bytes 786440 | tf_op jit(solution)/shard_map/ppermute | solution.py:249
  18.4 0.5 collective-permute-start.10
  18.9 0.3 collective-permute-start.8
  19.2 1.8 %collective-permute-start.7 = (bf16[8,128,128]{2,1,0:T(8,128)(2,1)}, bf16[8,128,128]{2,1,0:T(8,128)(2,1)S(1)}, u32[]{:S(2)}, u32[]{:S(2)}) collective-permute-start(bf16[8,128,128]{2,1,0:T(8,128)(2,1)} %get-tuple-element.12.refs_8_), channel_id=1, source_target_pairs={{0,32},{32,0},{64,96},{96,64},{128,160},{160,128},{192,224},{224,1... | collective-permute-start | bytes 786440 | tf_op jit(solution)/shard_map/ppermute | solution.py:249
  21.0 8.8 %collective-permute-done.12.refs_14_ = bf16[8,128,128]{2,1,0:T(8,128)(2,1)S(1)} collective-permute-done((bf16[8,128,128]{2,1,0:T(8,128)(2,1)}, bf16[8,128,128]{2,1,0:T(8,128)(2,1)S(1)}, u32[]{:S(2)}, u32[]{:S(2)}) %collective-permute-start.12) | collective-permute-done | bytes 262176 | tf_op jit(solution)/shard_map/ppermute | solution.py:249
  29.8 1.9 %collective-permute-start.13 = (bf16[8,128,128]{2,1,0:T(8,128)(2,1)S(1)}, bf16[8,128,128]{2,1,0:T(8,128)(2,1)S(1)}, u32[]{:S(2)}, u32[]{:S(2)}) collective-permute-start(bf16[8,128,128]{2,1,0:T(8,128)(2,1)S(1)} %collective-permute-done.12.refs_14_), channel_id=1, source_target_pairs={{0,32},{32,0},{64,96},{96,64},{128,160},{160,128},{192,224},{224,1... | collective-permute-start | bytes 786440 | tf_op jit(solution)/shard_map/ppermute | solution.py:249
  31.7 0.0 collective-permute-done.10.refs_12_
  31.7 0.0 collective-permute-start.11
  31.7 0.6 %collective-permute-start.9 = (bf16[8,128,128]{2,1,0:T(8,128)(2,1)S(1)}, bf16[8,128,128]{2,1,0:T(8,128)(2,1)S(1)}, u32[]{:S(2)}, u32[]{:S(2)}) collective-permute-start(bf16[8,128,128]{2,1,0:T(8,128)(2,1)S(1)} %collective-permute-done.8.refs_10_), channel_id=1, source_target_pairs={{0,32},{32,0},{64,96},{96,64},{128,160},{160,128},{192,224},{224,1... | collective-permute-start | bytes 786440 | tf_op jit(solution)/shard_map/ppermute | solution.py:249
  32.3 2.2 %all-to-all-done.recv_ref = bf16[32,80,128]{2,1,0:T(8,128)(2,1)S(1)} async-done(((bf16[32,80,128]{2,1,0:T(8,128)(2,1)}), bf16[32,80,128]{2,1,0:T(8,128)(2,1)S(1)}, u32[]{:S(2)}, u32[]{:S(2)}) %all-to-all-start) | async-done | bytes 655392 | tf_op jit(solution)/shard_map/all_to_all | solution.py:274
  34.6 0.5 turn.1.refs_0_
  35.0 2.6 %collective-permute-start.5 = (bf16[512,128]{1,0:T(8,128)(2,1)S(1)}, bf16[512,128]{1,0:T(8,128)(2,1)S(1)}, u32[]{:S(2)}, u32[]{:S(2)}) collective-permute-start(bf16[512,128]{1,0:T(8,128)(2,1)S(1)} %turn.1.refs_0_), channel_id=1, source_target_pairs={{0,192},{32,224},{64,128},{96,160},{128,64},{160,96},{192,0},{224,... | collective-permute-start | bytes 393224 | tf_op jit(solution)/shard_map/ppermute | solution.py:249
  37.6 0.0 collective-permute-done.7.refs_9_
  37.6 0.5 collective-permute-start.3
  38.1 0.0 collective-permute-done.13.refs_15_
  38.1 0.3 collective-permute-start.1
  38.4 0.7 %copy-done.1 = s32[32]{0:T(128)S(1)} copy-done((s32[32]{0:T(128)S(1)}, s32[32]{0:T(128)}, u32[]{:S(2)}) %copy-start.1) | copy-done | bytes 152
  39.0 2.1 %radial_rows.1.radial_ref = bf16[32,64,128]{2,1,0:T(8,128)(2,1)S(1)} custom-call(s32[32]{0:T(128)S(1)} %copy-done.1, bf16[32,80,128]{2,1,0:T(8,128)(2,1)S(1)} %all-to-all-done.recv_ref), custom_call_target="tpu_custom_call" | custom-call | flops 1500000000 | bytes 1048576 | tf_op jit(solution)/shard_map/radial_rows/pallas_call | solution.py:293
  41.1 0.0 collective-permute-done.11.refs_13_
  41.1 3.4 %collective-permute-start = (bf16[512,128]{1,0:T(8,128)(2,1)S(1)}, bf16[512,128]{1,0:T(8,128)(2,1)S(1)}, u32[]{:S(2)}, u32[]{:S(2)}) collective-permute-start(bf16[512,128]{1,0:T(8,128)(2,1)S(1)} %turn.1.refs_0_), channel_id=1, source_target_pairs={{0,32},{32,0},{64,96},{96,64},{128,160},{160,128},{192,224},{224,1... | collective-permute-start | bytes 393224 | tf_op jit(solution)/shard_map/ppermute | solution.py:249
  44.5 0.0 collective-permute-done.5.refs_6_
  44.5 0.5 collective-permute-start.6
  45.0 1.8 %collective-permute-start.4 = (bf16[512,128]{1,0:T(8,128)(2,1)S(1)}, bf16[512,128]{1,0:T(8,128)(2,1)S(1)}, u32[]{:S(2)}, u32[]{:S(2)}) collective-permute-start(bf16[512,128]{1,0:T(8,128)(2,1)S(1)} %collective-permute-done.3.refs_4_), channel_id=1, source_target_pairs={{0,32},{32,0},{64,96},{96,64},{128,160},{160,128},{192,224},{224,1... | collective-permute-start | bytes 393224 | tf_op jit(solution)/shard_map/ppermute | solution.py:249
  46.8 0.0 collective-permute-done.1.refs_2_
  46.8 0.0 collective-permute-start.2
  46.8 0.0 collective-permute-done.9.refs_11_
  46.9 1.0 %collective-permute-done.4.refs_5_ = bf16[512,128]{1,0:T(8,128)(2,1)S(1)} collective-permute-done((bf16[512,128]{1,0:T(8,128)(2,1)S(1)}, bf16[512,128]{1,0:T(8,128)(2,1)S(1)}, u32[]{:S(2)}, u32[]{:S(2)}) %collective-permute-start.4) | collective-permute-done | bytes 131104 | tf_op jit(solution)/shard_map/ppermute | solution.py:249
  47.8 0.4 collective-permute-done.2.refs_3_
  48.2 5.9 %finish.1 = bf16[128,64,128]{2,1,0:T(8,128)(2,1)} custom-call(s32[32]{0:T(128)S(1)} %copy-done.1, s32[64]{0:T(128)S(1)} %copy-done.2, bf16[32,64,128]{2,1,0:T(8,128)(2,1)S(1)} %radial_rows.1.radial_ref, bf16[512,128]{1,0:T(8,128)(2,1)S(1)} %turn.1.refs_0_, bf16[512,128]{1,0:T(8,128)(2,1)S(1)} %collective-permute-done.refs_1_, ...), custom_call_target="tpu_custom_call" | custom-call | flops 2500000000 | bytes 4194304 | tf_op jit(solution)/shard_map/finish/pallas_call | solution.py:312
  (8 shorter events, 0.0 us)
Async XLA Ops:
  3.6 44.5 %copy-start = (bf16[8,128,128]{2,1,0:T(8,128)(2,1)S(1)}, bf16[8,128,128]{2,1,0:T(8,128)(2,1)}, u32[]{:S(2)}) copy-start(bf16[8,128,128]{2,1,0:T(8,128)(2,1)} %get-tuple-element.12.refs_8_) | copy-start | bytes 786436
  3.7 44.5 %copy-start.2 = (s32[64]{0:T(128)S(1)}, s32[64]{0:T(128)}, u32[]{:S(2)}) copy-start(s32[64]{0:T(128)} %order_ref.1) | copy-start | bytes 772
  3.7 30.9 %all-to-all-start = ((bf16[32,80,128]{2,1,0:T(8,128)(2,1)}), bf16[32,80,128]{2,1,0:T(8,128)(2,1)S(1)}, u32[]{:S(2)}, u32[]{:S(2)}) async-start(bf16[32,80,128]{2,1,0:T(8,128)(2,1)} %get-tuple-element.9), calls=%async_computation | async-start | bytes 1310720 | tf_op jit(solution)/shard_map/all_to_all | solution.py:274
  15.9 14.0 %collective-permute-start.12 = (bf16[8,128,128]{2,1,0:T(8,128)(2,1)}, bf16[8,128,128]{2,1,0:T(8,128)(2,1)S(1)}, u32[]{:S(2)}, u32[]{:S(2)}) collective-permute-start(bf16[8,128,128]{2,1,0:T(8,128)(2,1)} %get-tuple-element.12.refs_8_), channel_id=1, source_target_pairs={{0,192},{32,224},{64,128},{96,160},{128,64},{160,96},{192,0},{224,... | collective-permute-start | bytes 786440 | tf_op jit(solution)/shard_map/ppermute | solution.py:249
  18.4 13.3 %collective-permute-start.10 = (bf16[8,128,128]{2,1,0:T(8,128)(2,1)}, bf16[8,128,128]{2,1,0:T(8,128)(2,1)S(1)}, u32[]{:S(2)}, u32[]{:S(2)}) collective-permute-start(bf16[8,128,128]{2,1,0:T(8,128)(2,1)} %get-tuple-element.12.refs_8_), channel_id=1, source_target_pairs={{0,128},{32,160},{64,192},{96,224},{128,0},{160,32},{192,64},{224,... | collective-permute-start | bytes 786440 | tf_op jit(solution)/shard_map/ppermute | solution.py:249
  18.9 12.8 %collective-permute-start.8 = (bf16[8,128,128]{2,1,0:T(8,128)(2,1)}, bf16[8,128,128]{2,1,0:T(8,128)(2,1)S(1)}, u32[]{:S(2)}, u32[]{:S(2)}) collective-permute-start(bf16[8,128,128]{2,1,0:T(8,128)(2,1)} %get-tuple-element.12.refs_8_), channel_id=1, source_target_pairs={{0,64},{32,96},{64,0},{96,32},{128,192},{160,224},{192,128},{224,1... | collective-permute-start | bytes 786440 | tf_op jit(solution)/shard_map/ppermute | solution.py:249
  19.2 18.4 %collective-permute-start.7 = (bf16[8,128,128]{2,1,0:T(8,128)(2,1)}, bf16[8,128,128]{2,1,0:T(8,128)(2,1)S(1)}, u32[]{:S(2)}, u32[]{:S(2)}) collective-permute-start(bf16[8,128,128]{2,1,0:T(8,128)(2,1)} %get-tuple-element.12.refs_8_), channel_id=1, source_target_pairs={{0,32},{32,0},{64,96},{96,64},{128,160},{160,128},{192,224},{224,1... | collective-permute-start | bytes 786440 | tf_op jit(solution)/shard_map/ppermute | solution.py:249
  29.8 8.3 %collective-permute-start.13 = (bf16[8,128,128]{2,1,0:T(8,128)(2,1)S(1)}, bf16[8,128,128]{2,1,0:T(8,128)(2,1)S(1)}, u32[]{:S(2)}, u32[]{:S(2)}) collective-permute-start(bf16[8,128,128]{2,1,0:T(8,128)(2,1)S(1)} %collective-permute-done.12.refs_14_), channel_id=1, source_target_pairs={{0,32},{32,0},{64,96},{96,64},{128,160},{160,128},{192,224},{224,1... | collective-permute-start | bytes 786440 | tf_op jit(solution)/shard_map/ppermute | solution.py:249
  31.7 9.4 %collective-permute-start.11 = (bf16[8,128,128]{2,1,0:T(8,128)(2,1)S(1)}, bf16[8,128,128]{2,1,0:T(8,128)(2,1)S(1)}, u32[]{:S(2)}, u32[]{:S(2)}) collective-permute-start(bf16[8,128,128]{2,1,0:T(8,128)(2,1)S(1)} %collective-permute-done.10.refs_12_), channel_id=1, source_target_pairs={{0,32},{32,0},{64,96},{96,64},{128,160},{160,128},{192,224},{224,1... | collective-permute-start | bytes 786440 | tf_op jit(solution)/shard_map/ppermute | solution.py:249
  31.7 15.1 %collective-permute-start.9 = (bf16[8,128,128]{2,1,0:T(8,128)(2,1)S(1)}, bf16[8,128,128]{2,1,0:T(8,128)(2,1)S(1)}, u32[]{:S(2)}, u32[]{:S(2)}) collective-permute-start(bf16[8,128,128]{2,1,0:T(8,128)(2,1)S(1)} %collective-permute-done.8.refs_10_), channel_id=1, source_target_pairs={{0,32},{32,0},{64,96},{96,64},{128,160},{160,128},{192,224},{224,1... | collective-permute-start | bytes 786440 | tf_op jit(solution)/shard_map/ppermute | solution.py:249
  35.0 9.5 %collective-permute-start.5 = (bf16[512,128]{1,0:T(8,128)(2,1)S(1)}, bf16[512,128]{1,0:T(8,128)(2,1)S(1)}, u32[]{:S(2)}, u32[]{:S(2)}) collective-permute-start(bf16[512,128]{1,0:T(8,128)(2,1)S(1)} %turn.1.refs_0_), channel_id=1, source_target_pairs={{0,192},{32,224},{64,128},{96,160},{128,64},{160,96},{192,0},{224,... | collective-permute-start | bytes 393224 | tf_op jit(solution)/shard_map/ppermute | solution.py:249
  37.6 7.4 %collective-permute-start.3 = (bf16[512,128]{1,0:T(8,128)(2,1)S(1)}, bf16[512,128]{1,0:T(8,128)(2,1)S(1)}, u32[]{:S(2)}, u32[]{:S(2)}) collective-permute-start(bf16[512,128]{1,0:T(8,128)(2,1)S(1)} %turn.1.refs_0_), channel_id=1, source_target_pairs={{0,128},{32,160},{64,192},{96,224},{128,0},{160,32},{192,64},{224,... | collective-permute-start | bytes 393224 | tf_op jit(solution)/shard_map/ppermute | solution.py:249
  38.1 8.7 %collective-permute-start.1 = (bf16[512,128]{1,0:T(8,128)(2,1)S(1)}, bf16[512,128]{1,0:T(8,128)(2,1)S(1)}, u32[]{:S(2)}, u32[]{:S(2)}) collective-permute-start(bf16[512,128]{1,0:T(8,128)(2,1)S(1)} %turn.1.refs_0_), channel_id=1, source_target_pairs={{0,64},{32,96},{64,0},{96,32},{128,192},{160,224},{192,128},{224,1... | collective-permute-start | bytes 393224 | tf_op jit(solution)/shard_map/ppermute | solution.py:249
  38.4 0.7 %copy-start.1 = (s32[32]{0:T(128)S(1)}, s32[32]{0:T(128)}, u32[]{:S(2)}) copy-start(s32[32]{0:T(128)} %lengths_ref.3) | copy-start | bytes 388
  41.1 5.7 %collective-permute-start = (bf16[512,128]{1,0:T(8,128)(2,1)S(1)}, bf16[512,128]{1,0:T(8,128)(2,1)S(1)}, u32[]{:S(2)}, u32[]{:S(2)}) collective-permute-start(bf16[512,128]{1,0:T(8,128)(2,1)S(1)} %turn.1.refs_0_), channel_id=1, source_target_pairs={{0,32},{32,0},{64,96},{96,64},{128,160},{160,128},{192,224},{224,1... | collective-permute-start | bytes 393224 | tf_op jit(solution)/shard_map/ppermute | solution.py:249
  44.5 2.3 %collective-permute-start.6 = (bf16[512,128]{1,0:T(8,128)(2,1)S(1)}, bf16[512,128]{1,0:T(8,128)(2,1)S(1)}, u32[]{:S(2)}, u32[]{:S(2)}) collective-permute-start(bf16[512,128]{1,0:T(8,128)(2,1)S(1)} %collective-permute-done.5.refs_6_), channel_id=1, source_target_pairs={{0,32},{32,0},{64,96},{96,64},{128,160},{160,128},{192,224},{224,1... | collective-permute-start | bytes 393224 | tf_op jit(solution)/shard_map/ppermute | solution.py:249
  45.0 2.8 %collective-permute-start.4 = (bf16[512,128]{1,0:T(8,128)(2,1)S(1)}, bf16[512,128]{1,0:T(8,128)(2,1)S(1)}, u32[]{:S(2)}, u32[]{:S(2)}) collective-permute-start(bf16[512,128]{1,0:T(8,128)(2,1)S(1)} %collective-permute-done.3.refs_4_), channel_id=1, source_target_pairs={{0,32},{32,0},{64,96},{96,64},{128,160},{160,128},{192,224},{224,1... | collective-permute-start | bytes 393224 | tf_op jit(solution)/shard_map/ppermute | solution.py:249
  46.8 1.3 %collective-permute-start.2 = (bf16[512,128]{1,0:T(8,128)(2,1)S(1)}, bf16[512,128]{1,0:T(8,128)(2,1)S(1)}, u32[]{:S(2)}, u32[]{:S(2)}) collective-permute-start(bf16[512,128]{1,0:T(8,128)(2,1)S(1)} %collective-permute-done.1.refs_2_), channel_id=1, source_target_pairs={{0,32},{32,0},{64,96},{96,64},{128,160},{160,128},{192,224},{224,1... | collective-permute-start | bytes 393224 | tf_op jit(solution)/shard_map/ppermute | solution.py:249

commit v5 on v4

--- a/solution.py
+++ b/solution.py
@@ -13,7 +13,6 @@
 VMEM_LIMIT = 16 * 1024 * 1024
 VMEM_WHOLE = 64 * 1024 * 1024
 
-SMEM_SPEC = pl.BlockSpec(memory_space=pltpu.SMEM)
 VMEM_SPEC = pl.BlockSpec(memory_space=pltpu.VMEM)
 HBM_SPEC = pl.BlockSpec(memory_space=pltpu.HBM)
 
@@ -45,9 +44,9 @@
 
 
 def front_kernel(
-    lengths_hbm, cycle_hbm, order_hbm, density_hbm, footprint_hbm, bessel_hbm, legendre_hbm, send_hbm, rows_hbm,
+    lengths_hbm, cycle_hbm, order_hbm, density_hbm, footprint_hbm, bessel_hbm, legendre_hbm, send_hbm, rows_hbm, info_hbm,
     lengths_ref, cycle_ref, order_ref, density_ref, footprint_ref, bessel_ref, low_ref, high_ref,
-    block_ref, tile_ref, rows_ref, sems,
+    block_ref, tile_ref, rows_ref, info_ref, sems,
 ):
     _, rows, nphi = density_ref.shape
     modes, deg = bessel_ref.shape
@@ -63,7 +62,8 @@
     for copy in copies:
         copy.start()
     copies[0].wait()
-    base, shift = split_start(block_start(lengths_ref))
+    first = block_start(lengths_ref)
+    base, shift = split_start(first)
     after = pl.multiple_of(jnp.minimum(base + 128, deg - 128), 128)
     windows = [
         pltpu.make_async_copy(legendre_hbm.at[:, pl.ds(base, 128), :], low_ref, sems.at[6]),
@@ -111,6 +111,12 @@
     pa, qa = cos_sin((sixty_four * 128 * order + 2048 * part) & 8191)
     qa = -qa
     cb, sb = cos_sin((sixty_four * 2 * order) & 8191)
+    info_ref[32:33] = jnp.full((1, 128), first, jnp.int32)
+    info_ref[33:34] = jnp.full((1, 128), lengths_ref[lax.axis_index("radial")], jnp.int32)
+    for i in range(32):
+        info_ref[i : i + 1] = jnp.where(lane < 64, order_ref[2 * i], order_ref[2 * i + 1])
+    outputs.append(pltpu.make_async_copy(info_ref, info_hbm, sems.at[11]))
+    outputs[2].start()
     total = jnp.zeros((2 * rows, 256), F32)
     for chunk in range(nphi // 256):
         tables = []
@@ -139,16 +145,17 @@
     four = (x * cos_t + other * sin_t).astype(BF16)
     tile_ref[...] = jnp.broadcast_to(four[None], tile_ref.shape)
     outputs.append(pltpu.make_async_copy(tile_ref, send_hbm.at[:, pl.ds(0, 16), :], sems.at[10]))
-    outputs[2].start()
+    outputs[3].start()
     for copy in outputs:
         copy.wait()
 
 
 def turn_kernel(recv_ref, out_ref, wide_ref, turned_ref):
-    wide_ref[...] = recv_ref[:, :16].astype(F32).reshape(512, 128)
+    for s in range(32):
+        wide_ref[24 * s : 24 * s + 16, :] = recv_ref[s, :16].astype(F32)
     tile = lax.broadcasted_iota(jnp.int32, (32, 128), 1) >> 5
     for a in range(4):
-        x = [wide_ref[pl.ds(4 * a + b, 32, stride=16), :] for b in range(4)]
+        x = [wide_ref[pl.ds(4 * a + b, 32, stride=24), :] for b in range(4)]
         pieces = []
         for u in range(4):
             piece = x[u]
@@ -158,40 +165,42 @@
             pieces.append(piece)
         turned = jnp.transpose(jnp.concatenate(pieces, axis=0))
         for b in range(4):
-            turned_ref[pl.ds(4 * a + b, 32, stride=16), :] = turned[32 * b : 32 * b + 32]
-    out_ref[...] = turned_ref[...].astype(BF16)
+            turned_ref[pl.ds(4 * a + b, 32, stride=24), :] = turned[32 * b : 32 * b + 32]
+    for i in range(32):
+        out_ref[16 * i : 16 * i + 16] = turned_ref[24 * i : 24 * i + 16, :].astype(BF16)
 
 
 def block_start(lengths_ref):
     return lax.fori_loop(0, lax.axis_index("radial"), lambda k, total: total + lengths_ref[k], jnp.int32(0))
 
 
-def radial_kernel(lengths_ref, recv_ref, out_ref, wide_ref, turned_ref):
-    length = lengths_ref[lax.axis_index("radial")]
-    start = block_start(lengths_ref)
-    wide_ref[...] = recv_ref[:, 16:].astype(F32).reshape(wide_ref.shape)
+def radial_kernel(info_ref, recv_ref, out_ref, wide_ref, turned_ref):
+    for s in range(32):
+        wide_ref[72 * s : 72 * s + 64, :] = recv_ref[s, 16:].astype(F32)
     lane = lax.broadcasted_iota(jnp.int32, (128, 128), 1)
     row = lax.broadcasted_iota(jnp.int32, (128, 128), 0)
     slot = 32 * (row >> 5) + (lane & 31)
-    keep = ((slot - start) & 127) < length
+    keep = ((slot - info_ref[32:33]) & 127) < info_ref[33:34]
 
     def step(a, carry):
-        x = jnp.concatenate([wide_ref[pl.ds(16 * j + a, 32, stride=64), :] for j in range(4)], axis=0)
+        x = jnp.concatenate([wide_ref[pl.ds(16 * j + a, 32, stride=72), :] for j in range(4)], axis=0)
         turned = jnp.transpose(jnp.where(keep, x, 0.0))
         for m in range(4):
-            turned_ref[pl.ds(16 * m + a, 32, stride=64), :] = turned[32 * m : 32 * m + 32]
+            turned_ref[pl.ds(16 * m + a, 32, stride=72), :] = turned[32 * m : 32 * m + 32]
         return carry
 
     lax.fori_loop(0, 16, step, 0, unroll=4)
-    out_ref[...] = turned_ref[...].astype(BF16).reshape(out_ref.shape)
-
-
-def final_kernel(lengths_ref, order_ref, radial_ref, *refs):
+    for g in range(32):
+        out_ref[g] = turned_ref[72 * g : 72 * g + 64, :].astype(BF16)
+
+
+def final_kernel(info_ref, radial_ref, *refs):
     fours, rows, out_ref = refs[:8], refs[8:16], refs[16]
     four_ref, harmonic_ref, block_ref, sems = refs[17:]
     mine = lax.axis_index("shell")
-    start = block_start(lengths_ref)
-    base, shift = split_start(start)
+    start = jnp.max(info_ref[32:33].astype(F32)).astype(jnp.int32)
+    shift = info_ref[32:33] & 127
+    base = info_ref[32:33] - shift
     for d in range(8):
         four_ref[:, mine ^ d] = fours[d][...].reshape(32, 16, 128)
     lane = lax.broadcasted_iota(jnp.int32, (128, 128), 1)
@@ -205,18 +214,17 @@
             left = rows[d][2 * i : 2 * i + 2].reshape(256, 128)
             both = jnp.dot(left, four_ref[pair].reshape(128, 128), preferred_element_type=F32)
             value = jnp.where(first_half, both[:128], both[128:])
-            order = jnp.where(first_half, order_ref[2 * pair], order_ref[2 * pair + 1])
-            value = jnp.where(degree >= order, value, 0.0)
+            value = jnp.where(degree >= info_ref[pl.ds(pair, 1), :], value, 0.0)
             for u in range(4):
                 packed = value[32 * u : 32 * u + 32]
                 for j in range(4):
                     if j != u:
                         packed = jnp.where(tile == j, pltpu.roll(value[32 * j : 32 * j + 32], (32 * (j - u)) % 128, 1), packed)
-                harmonic_ref[pl.ds(2 * pair + (u & 1) * 64 + (u >> 1), 32, stride=128), :] = packed
+                harmonic_ref[pl.ds(2 * pair + (u & 1) * 64 + (u >> 1), 32, stride=136), :] = packed
     group = lax.broadcasted_iota(jnp.int32, (64, 128), 1) >> 5
     zero = jnp.zeros((64, 128), BF16)
     for g in range(32):
-        right = harmonic_ref[128 * g : 128 * g + 128, :].astype(BF16)
+        right = harmonic_ref[136 * g : 136 * g + 128, :].astype(BF16)
         left = jnp.concatenate([jnp.where(group == j, radial_ref[g], zero) for j in range(4)], axis=0)
         result = lax.dot_general(left, right, (((1,), (1,)), ((), ())), preferred_element_type=F32)
         block_ref[:, g] = result.reshape(4, 64, 128).astype(BF16)
@@ -248,11 +256,11 @@
     def swap(x, d):
         return lax.ppermute(x, "shell", [(i, i ^ d) for i in range(8)])
 
-    send, leg_rows = pl.pallas_call(
+    send, leg_rows, info = pl.pallas_call(
         front_kernel,
-        out_shape=[shape((32, 16 + modes, 128), BF16), shape((8, 128, 128), BF16)],
+        out_shape=[shape((32, 16 + modes, 128), BF16), shape((8, 128, 128), BF16), shape((40, 128), jnp.int32)],
         in_specs=[HBM_SPEC] * 7,
-        out_specs=[HBM_SPEC] * 2,
+        out_specs=[HBM_SPEC] * 3,
         scratch_shapes=[
             pltpu.SMEM((32,), jnp.int32),
             pltpu.SMEM((rows,), jnp.int32),
@@ -265,7 +273,8 @@
             pltpu.VMEM((32, modes, 128), BF16),
             pltpu.VMEM((32, 16, 128), BF16),
             pltpu.VMEM((8, 128, 128), BF16),
-            dma((11,)),
+            pltpu.VMEM((40, 128), jnp.int32),
+            dma((12,)),
         ],
         compiler_params=params(VMEM_WHOLE),
         cost_estimate=cost(4, 1 << 21),
@@ -273,18 +282,16 @@
     )(block_lengths, cycle_index, order_values, density, footprint, jnp.swapaxes(bessel, 1, 2).reshape(modes, deg), legendre)
     recv = lax.all_to_all(send, "radial", split_axis=0, concat_axis=0, tiled=True)
 
-    row_pieces = {0: leg_rows}
+    row_pieces = {0: leg_rows, 1: swap(leg_rows, 1)}
     for d in (4, 2, 6):
         row_pieces[d] = swap(leg_rows, d)
-    for d in (0, 4, 2, 6):
-        row_pieces[d + 1] = swap(row_pieces[d], 1)
 
     four = pl.pallas_call(
         turn_kernel,
         out_shape=shape((512, 128), BF16),
         in_specs=[VMEM_SPEC],
         out_specs=VMEM_SPEC,
-        scratch_shapes=[pltpu.VMEM((512, 128), F32), pltpu.VMEM((512, 128), F32)],
+        scratch_shapes=[pltpu.VMEM((32 * 24, 128), F32)] * 2,
         compiler_params=params(),
         cost_estimate=cost(1, 1 << 19),
         name="turn",
@@ -293,37 +300,40 @@
     radial = pl.pallas_call(
         radial_kernel,
         out_shape=shape((32, modes, 128), BF16),
-        in_specs=[SMEM_SPEC, VMEM_SPEC],
+        in_specs=[VMEM_SPEC] * 2,
         out_specs=VMEM_SPEC,
-        scratch_shapes=[pltpu.VMEM((32 * modes, 128), F32), pltpu.VMEM((32 * modes, 128), F32)],
+        scratch_shapes=[pltpu.VMEM((32 * 72, 128), F32)] * 2,
         compiler_params=params(),
         cost_estimate=cost(3, 1 << 20),
         name="radial_rows",
-    )(block_lengths, recv)
+    )(info, recv)
 
     pieces = {0: four}
     for d in (2, 6, 4):
         pieces[d] = swap(four, d)
-    own, radial = lax.optimization_barrier((four, radial))
+    own, radial, *moved = lax.optimization_barrier((four, radial, *[row_pieces[d] for d in (4, 2, 6)]))
     pieces[1] = swap(own, 1)
+    for d, piece in zip((4, 2, 6), moved):
+        row_pieces[d] = piece
+        row_pieces[d + 1] = swap(piece, 1)
     for d in (2, 6, 4):
         pieces[d + 1] = swap(pieces[d], 1)
 
     return pl.pallas_call(
         final_kernel,
         out_shape=shape((128, modes, 128), BF16),
-        in_specs=[SMEM_SPEC] * 2 + [VMEM_SPEC] * 17,
+        in_specs=[VMEM_SPEC] * 18,
         out_specs=HBM_SPEC,
         scratch_shapes=[
             pltpu.VMEM((32, 8, 16, 128), BF16),
-            pltpu.VMEM((32 * 128, 128), F32),
+            pltpu.VMEM((32 * 136, 128), F32),
             pltpu.VMEM((4, 32, modes, 128), BF16),
             dma((16,)),
         ],
         compiler_params=params(),
         cost_estimate=cost(5, 1 << 22),
         name="finish",
-    )(block_lengths, order_values, radial, *[pieces[d] for d in range(8)], *[row_pieces[d] for d in range(8)])
+    )(info, radial, *[pieces[d] for d in range(8)], *[row_pieces[d] for d in range(8)])
 
 
 def solution(mesh):

time: 54.5 us -> 53 us (0.972)
  Pallas kernels: 12.1 us -> 8.64 us
  waiting for transfers between devices: 12.4 us -> 14.1 us
    all_to_all x1, waiting for transfers between devices: 2.23 us -> 13 us  [on_device(): lax.all_to_all(send, 'radial', split_axis=0, concat_axis=0, tiled=True)]
    ppermute x14, waiting for transfers between devices: 10.2 us -> 1.15 us  [swap(): return lax.ppermute(x, 'shell', [(i, i ^ d) for i in range(8)])]
    pallas_call x1, Pallas kernels: 5.94 us -> 3.86 us  [on_device(): pl.pallas_call(final_kernel, out_shape=shape((128, modes, 128), BF16), in...]
    pallas_call x1, Pallas kernels: 2.06 us -> 0.67 us  [on_device(): pl.pallas_call(radial_kernel, out_shape=shape((32, modes, 128), BF16), in...]
  transfers between devices with their start and end apart: 15 -> 15, of which waited for: 4 -> 3; matrix products, arithmetic and copies ran while one was open for 0% -> 0% of each run, Pallas kernels for 5% -> 2%
where the time goes in v5:
time: 53 us; the launch traced here: 52.8 us
  starting transfers between devices  29 us (55%)
  waiting for transfers between devices  14.1 us (27%)
  Pallas kernels  8.64 us (16%)
  local copies, waits for them, and re-layouts  0.74 us (1%)
    ppermute x14, starting transfers between devices, swap(): return lax.ppermute(x, 'shell', [(i, i ^ d) for i in range(8)])  16.9 us
    all_to_all x1, waiting for transfers between devices, on_device(): lax.all_to_all(send, 'radial', split_axis=0, concat_axis=0, tiled=True)  13 us
    all_to_all x1, starting transfers between devices, on_device(): lax.all_to_all(send, 'radial', split_axis=0, concat_axis=0, tiled=True)  12.2 us
    pallas_call x1, Pallas kernels, on_device(): pl.pallas_call(final_kernel, out_shape=shape((128, modes, 128), BF16), in...  3.86 us
    pallas_call x1, Pallas kernels, on_device(): pl.pallas_call(front_kernel, out_shape=[shape((32, 16 + modes, 128), BF16...  3.65 us
    ppermute x14, waiting for transfers between devices, swap(): return lax.ppermute(x, 'shell', [(i, i ^ d) for i in range(8)])  1.15 us
  transfers between devices with their start and end apart: 15, of which 3 were waited for; matrix products, arithmetic and copies ran while one was open for 0% of the time, Pallas kernels for 2%

profile of v5, /device:TPU:1, one launch (start us, length us, event | category | flops | bytes accessed | tf_op | source)
XLA Modules:
  0.0 52.8 jit_solution(14517554260323939216)
XLA Ops:
  0.0 3.6 %front.1 = (bf16[32,80,128]{2,1,0:T(8,128)(2,1)}, bf16[8,128,128]{2,1,0:T(8,128)(2,1)}, s32[40,128]{1,0:T(8,128)}) custom-call(s32[32]{0:T(128)} %lengths_hbm.1, s32[16]{0:T(128)} %cycle_hbm.1, s32[64]{0:T(128)} %order_hbm.1, f32[1,16,4096]{2,1,0:T(8,128)} %density_hbm.1, s32[1,16,4096]{2,1,0:T(8,128)} %footprint_hbm.1, bf16[64,2048]{1,0:T(8,128)(2,1)} %bitcast.3, ...), custom_call_target="tpu_custom_call" | custom-call | flops 2000000000 | bytes 2097152 | tf_op jit(solution)/shard_map/front/pallas_call | solution.py:259
  3.7 12.2 %all-to-all-start = ((bf16[32,80,128]{2,1,0:T(8,128)(2,1)}), bf16[32,80,128]{2,1,0:T(8,128)(2,1)S(1)}, u32[]{:S(2)}, u32[]{:S(2)}) async-start(bf16[32,80,128]{2,1,0:T(8,128)(2,1)} %get-tuple-element.14), calls=%async_computation | async-start | bytes 1310720 | tf_op jit(solution)/shard_map/all_to_all | solution.py:283
  15.9 2.6 %collective-permute-start.2 = (bf16[8,128,128]{2,1,0:T(8,128)(2,1)}, bf16[8,128,128]{2,1,0:T(8,128)(2,1)S(1)}, u32[]{:S(2)}, u32[]{:S(2)}) collective-permute-start(bf16[8,128,128]{2,1,0:T(8,128)(2,1)} %get-tuple-element.15.refs_8_), channel_id=1, source_target_pairs={{0,192},{32,224},{64,128},{96,160},{128,64},{160,96},{192,0},{224,... | collective-permute-start | bytes 786440 | tf_op jit(solution)/shard_map/ppermute | solution.py:257
  18.4 0.0 collective-permute-start.1
  18.4 1.4 %collective-permute-start = (bf16[8,128,128]{2,1,0:T(8,128)(2,1)}, bf16[8,128,128]{2,1,0:T(8,128)(2,1)S(1)}, u32[]{:S(2)}, u32[]{:S(2)}) collective-permute-start(bf16[8,128,128]{2,1,0:T(8,128)(2,1)} %get-tuple-element.15.refs_8_), channel_id=1, source_target_pairs={{0,128},{32,160},{64,192},{96,224},{128,0},{160,32},{192,64},{224,... | collective-permute-start | bytes 786440 | tf_op jit(solution)/shard_map/ppermute | solution.py:257
  19.8 1.8 %collective-permute-start.10 = (bf16[8,128,128]{2,1,0:T(8,128)(2,1)}, bf16[8,128,128]{2,1,0:T(8,128)(2,1)S(1)}, u32[]{:S(2)}, u32[]{:S(2)}) collective-permute-start(bf16[8,128,128]{2,1,0:T(8,128)(2,1)} %get-tuple-element.15.refs_8_), channel_id=1, source_target_pairs={{0,32},{32,0},{64,96},{96,64},{128,160},{160,128},{192,224},{224,1... | collective-permute-start | bytes 786440 | tf_op jit(solution)/shard_map/ppermute | solution.py:257
  21.6 13.0 %all-to-all-done.recv_ref = bf16[32,80,128]{2,1,0:T(8,128)(2,1)S(1)} async-done(((bf16[32,80,128]{2,1,0:T(8,128)(2,1)}), bf16[32,80,128]{2,1,0:T(8,128)(2,1)S(1)}, u32[]{:S(2)}, u32[]{:S(2)}) %all-to-all-start) | async-done | bytes 655392 | tf_op jit(solution)/shard_map/all_to_all | solution.py:283
  34.6 0.5 turn.1.refs_0_
  35.0 2.6 %collective-permute-start.8 = (bf16[512,128]{1,0:T(8,128)(2,1)S(1)}, bf16[512,128]{1,0:T(8,128)(2,1)S(1)}, u32[]{:S(2)}, u32[]{:S(2)}) collective-permute-start(bf16[512,128]{1,0:T(8,128)(2,1)S(1)} %turn.1.refs_0_), channel_id=1, source_target_pairs={{0,192},{32,224},{64,128},{96,160},{128,64},{160,96},{192,0},{224,... | collective-permute-start | bytes 393224 | tf_op jit(solution)/shard_map/ppermute | solution.py:257
  37.6 0.0 collective-permute-done.2.refs_14_
  37.6 0.5 collective-permute-start.6
  38.1 0.0 collective-permute-done.1.refs_10_
  38.1 0.3 collective-permute-start.4
  38.4 0.7 %copy-done.1 = s32[40,128]{1,0:T(8,128)S(1)} copy-done((s32[40,128]{1,0:T(8,128)S(1)}, s32[40,128]{1,0:T(8,128)}, u32[]{:S(2)}) %copy-start.1) | copy-done | bytes 20504
  39.1 0.7 %radial_rows.1.radial_ref = bf16[32,64,128]{2,1,0:T(8,128)(2,1)S(1)} custom-call(s32[40,128]{1,0:T(8,128)S(1)} %copy-done.1, bf16[32,80,128]{2,1,0:T(8,128)(2,1)S(1)} %all-to-all-done.recv_ref), custom_call_target="tpu_custom_call" | custom-call | flops 1500000000 | bytes 1048576 | tf_op jit(solution)/shard_map/radial_rows/pallas_call | solution.py:300
  39.8 0.0 collective-permute-done.refs_12_
  39.8 3.4 %collective-permute-start.3 = (bf16[512,128]{1,0:T(8,128)(2,1)S(1)}, bf16[512,128]{1,0:T(8,128)(2,1)S(1)}, u32[]{:S(2)}, u32[]{:S(2)}) collective-permute-start(bf16[512,128]{1,0:T(8,128)(2,1)S(1)} %turn.1.refs_0_), channel_id=1, source_target_pairs={{0,32},{32,0},{64,96},{96,64},{128,160},{160,128},{192,224},{224,1... | collective-permute-start | bytes 393224 | tf_op jit(solution)/shard_map/ppermute | solution.py:257
  43.2 0.0 collective-permute-done.10.refs_9_
  43.2 0.1 collective-permute-start.11
  43.3 0.0 collective-permute-done.8.refs_6_
  43.3 1.7 %collective-permute-start.9 = (bf16[512,128]{1,0:T(8,128)(2,1)S(1)}, bf16[512,128]{1,0:T(8,128)(2,1)S(1)}, u32[]{:S(2)}, u32[]{:S(2)}) collective-permute-start(bf16[512,128]{1,0:T(8,128)(2,1)S(1)} %collective-permute-done.8.refs_6_), channel_id=1, source_target_pairs={{0,32},{32,0},{64,96},{96,64},{128,160},{160,128},{192,224},{224,1... | collective-permute-start | bytes 393224 | tf_op jit(solution)/shard_map/ppermute | solution.py:257
  45.0 0.0 collective-permute-done.6.refs_4_
  45.0 1.8 %collective-permute-start.12 = (bf16[8,128,128]{2,1,0:T(8,128)(2,1)S(1)}, bf16[8,128,128]{2,1,0:T(8,128)(2,1)S(1)}, u32[]{:S(2)}, u32[]{:S(2)}) collective-permute-start(bf16[8,128,128]{2,1,0:T(8,128)(2,1)S(1)} %collective-permute-done.refs_12_), channel_id=1, source_target_pairs={{0,32},{32,0},{64,96},{96,64},{128,160},{160,128},{192,224},{224,1... | collective-permute-start | bytes 786440 | tf_op jit(solution)/shard_map/ppermute | solution.py:257
  46.8 0.0 collective-permute-done.4.refs_2_
  46.8 0.0 collective-permute-start.13
  46.8 0.0 collective-permute-done.3.refs_1_
  46.8 0.5 collective-permute-start.7
  47.3 0.3 collective-permute-start.5
  47.6 0.9 %collective-permute-done.7.refs_5_ = bf16[512,128]{1,0:T(8,128)(2,1)S(1)} collective-permute-done((bf16[512,128]{1,0:T(8,128)(2,1)S(1)}, bf16[512,128]{1,0:T(8,128)(2,1)S(1)}, u32[]{:S(2)}, u32[]{:S(2)}) %collective-permute-start.7) | collective-permute-done | bytes 131104 | tf_op jit(solution)/shard_map/ppermute | solution.py:257
  48.5 0.2 collective-permute-done.5.refs_3_
  48.7 0.0 collective-permute-done.13.refs_15_
  48.8 3.9 %finish.1 = bf16[128,64,128]{2,1,0:T(8,128)(2,1)} custom-call(s32[40,128]{1,0:T(8,128)S(1)} %copy-done.2, bf16[32,64,128]{2,1,0:T(8,128)(2,1)S(1)} %radial_rows.1.radial_ref, bf16[512,128]{1,0:T(8,128)(2,1)S(1)} %turn.1.refs_0_, bf16[512,128]{1,0:T(8,128)(2,1)S(1)} %collective-permute-done.3.refs_1_, bf16[512,128]{1,0:T(8,128)(2,1)S(1)} %collective-permute-done.4.refs_2_, ...), custom_call_target="tpu_custom_call" | custom-call | flops 2500000000 | bytes 4194304 | tf_op jit(solution)/shard_map/finish/pallas_call | solution.py:322
  (8 shorter events, 0.0 us)
Async XLA Ops:
  3.7 45.1 %copy-start = (bf16[8,128,128]{2,1,0:T(8,128)(2,1)S(1)}, bf16[8,128,128]{2,1,0:T(8,128)(2,1)}, u32[]{:S(2)}) copy-start(bf16[8,128,128]{2,1,0:T(8,128)(2,1)} %get-tuple-element.15.refs_8_) | copy-start | bytes 786436
  3.7 45.1 %copy-start.2 = (s32[40,128]{1,0:T(8,128)S(1)}, s32[40,128]{1,0:T(8,128)}, u32[]{:S(2)}) copy-start(s32[40,128]{1,0:T(8,128)} %get-tuple-element.13.info_ref) | copy-start | bytes 61444
  3.7 30.9 %all-to-all-start = ((bf16[32,80,128]{2,1,0:T(8,128)(2,1)}), bf16[32,80,128]{2,1,0:T(8,128)(2,1)S(1)}, u32[]{:S(2)}, u32[]{:S(2)}) async-start(bf16[32,80,128]{2,1,0:T(8,128)(2,1)} %get-tuple-element.14), calls=%async_computation | async-start | bytes 1310720 | tf_op jit(solution)/shard_map/all_to_all | solution.py:283
  15.9 21.7 %collective-permute-start.2 = (bf16[8,128,128]{2,1,0:T(8,128)(2,1)}, bf16[8,128,128]{2,1,0:T(8,128)(2,1)S(1)}, u32[]{:S(2)}, u32[]{:S(2)}) collective-permute-start(bf16[8,128,128]{2,1,0:T(8,128)(2,1)} %get-tuple-element.15.refs_8_), channel_id=1, source_target_pairs={{0,192},{32,224},{64,128},{96,160},{128,64},{160,96},{192,0},{224,... | collective-permute-start | bytes 786440 | tf_op jit(solution)/shard_map/ppermute | solution.py:257
  18.4 19.7 %collective-permute-start.1 = (bf16[8,128,128]{2,1,0:T(8,128)(2,1)}, bf16[8,128,128]{2,1,0:T(8,128)(2,1)S(1)}, u32[]{:S(2)}, u32[]{:S(2)}) collective-permute-start(bf16[8,128,128]{2,1,0:T(8,128)(2,1)} %get-tuple-element.15.refs_8_), channel_id=1, source_target_pairs={{0,64},{32,96},{64,0},{96,32},{128,192},{160,224},{192,128},{224,1... | collective-permute-start | bytes 786440 | tf_op jit(solution)/shard_map/ppermute | solution.py:257
  18.4 21.4 %collective-permute-start = (bf16[8,128,128]{2,1,0:T(8,128)(2,1)}, bf16[8,128,128]{2,1,0:T(8,128)(2,1)S(1)}, u32[]{:S(2)}, u32[]{:S(2)}) collective-permute-start(bf16[8,128,128]{2,1,0:T(8,128)(2,1)} %get-tuple-element.15.refs_8_), channel_id=1, source_target_pairs={{0,128},{32,160},{64,192},{96,224},{128,0},{160,32},{192,64},{224,... | collective-permute-start | bytes 786440 | tf_op jit(solution)/shard_map/ppermute | solution.py:257
  19.8 23.4 %collective-permute-start.10 = (bf16[8,128,128]{2,1,0:T(8,128)(2,1)}, bf16[8,128,128]{2,1,0:T(8,128)(2,1)S(1)}, u32[]{:S(2)}, u32[]{:S(2)}) collective-permute-start(bf16[8,128,128]{2,1,0:T(8,128)(2,1)} %get-tuple-element.15.refs_8_), channel_id=1, source_target_pairs={{0,32},{32,0},{64,96},{96,64},{128,160},{160,128},{192,224},{224,1... | collective-permute-start | bytes 786440 | tf_op jit(solution)/shard_map/ppermute | solution.py:257
  35.0 8.3 %collective-permute-start.8 = (bf16[512,128]{1,0:T(8,128)(2,1)S(1)}, bf16[512,128]{1,0:T(8,128)(2,1)S(1)}, u32[]{:S(2)}, u32[]{:S(2)}) collective-permute-start(bf16[512,128]{1,0:T(8,128)(2,1)S(1)} %turn.1.refs_0_), channel_id=1, source_target_pairs={{0,192},{32,224},{64,128},{96,160},{128,64},{160,96},{192,0},{224,... | collective-permute-start | bytes 393224 | tf_op jit(solution)/shard_map/ppermute | solution.py:257
  37.6 7.4 %collective-permute-start.6 = (bf16[512,128]{1,0:T(8,128)(2,1)S(1)}, bf16[512,128]{1,0:T(8,128)(2,1)S(1)}, u32[]{:S(2)}, u32[]{:S(2)}) collective-permute-start(bf16[512,128]{1,0:T(8,128)(2,1)S(1)} %turn.1.refs_0_), channel_id=1, source_target_pairs={{0,128},{32,160},{64,192},{96,224},{128,0},{160,32},{192,64},{224,... | collective-permute-start | bytes 393224 | tf_op jit(solution)/shard_map/ppermute | solution.py:257
  38.1 8.7 %collective-permute-start.4 = (bf16[512,128]{1,0:T(8,128)(2,1)S(1)}, bf16[512,128]{1,0:T(8,128)(2,1)S(1)}, u32[]{:S(2)}, u32[]{:S(2)}) collective-permute-start(bf16[512,128]{1,0:T(8,128)(2,1)S(1)} %turn.1.refs_0_), channel_id=1, source_target_pairs={{0,64},{32,96},{64,0},{96,32},{128,192},{160,224},{192,128},{224,1... | collective-permute-start | bytes 393224 | tf_op jit(solution)/shard_map/ppermute | solution.py:257
  38.4 0.7 %copy-start.1 = (s32[40,128]{1,0:T(8,128)S(1)}, s32[40,128]{1,0:T(8,128)}, u32[]{:S(2)}) copy-start(s32[40,128]{1,0:T(8,128)} %get-tuple-element.13.info_ref) | copy-start | bytes 61444
  39.8 7.0 %collective-permute-start.3 = (bf16[512,128]{1,0:T(8,128)(2,1)S(1)}, bf16[512,128]{1,0:T(8,128)(2,1)S(1)}, u32[]{:S(2)}, u32[]{:S(2)}) collective-permute-start(bf16[512,128]{1,0:T(8,128)(2,1)S(1)} %turn.1.refs_0_), channel_id=1, source_target_pairs={{0,32},{32,0},{64,96},{96,64},{128,160},{160,128},{192,224},{224,1... | collective-permute-start | bytes 393224 | tf_op jit(solution)/shard_map/ppermute | solution.py:257
  43.2 5.5 %collective-permute-start.11 = (bf16[8,128,128]{2,1,0:T(8,128)(2,1)S(1)}, bf16[8,128,128]{2,1,0:T(8,128)(2,1)S(1)}, u32[]{:S(2)}, u32[]{:S(2)}) collective-permute-start(bf16[8,128,128]{2,1,0:T(8,128)(2,1)S(1)} %collective-permute-done.1.refs_10_), channel_id=1, source_target_pairs={{0,32},{32,0},{64,96},{96,64},{128,160},{160,128},{192,224},{224,1... | collective-permute-start | bytes 786440 | tf_op jit(solution)/shard_map/ppermute | solution.py:257
  43.3 4.0 %collective-permute-start.9 = (bf16[512,128]{1,0:T(8,128)(2,1)S(1)}, bf16[512,128]{1,0:T(8,128)(2,1)S(1)}, u32[]{:S(2)}, u32[]{:S(2)}) collective-permute-start(bf16[512,128]{1,0:T(8,128)(2,1)S(1)} %collective-permute-done.8.refs_6_), channel_id=1, source_target_pairs={{0,32},{32,0},{64,96},{96,64},{128,160},{160,128},{192,224},{224,1... | collective-permute-start | bytes 393224 | tf_op jit(solution)/shard_map/ppermute | solution.py:257
  45.0 3.7 %collective-permute-start.12 = (bf16[8,128,128]{2,1,0:T(8,128)(2,1)S(1)}, bf16[8,128,128]{2,1,0:T(8,128)(2,1)S(1)}, u32[]{:S(2)}, u32[]{:S(2)}) collective-permute-start(bf16[8,128,128]{2,1,0:T(8,128)(2,1)S(1)} %collective-permute-done.refs_12_), channel_id=1, source_target_pairs={{0,32},{32,0},{64,96},{96,64},{128,160},{160,128},{192,224},{224,1... | collective-permute-start | bytes 786440 | tf_op jit(solution)/shard_map/ppermute | solution.py:257
  46.8 1.9 %collective-permute-start.13 = (bf16[8,128,128]{2,1,0:T(8,128)(2,1)S(1)}, bf16[8,128,128]{2,1,0:T(8,128)(2,1)S(1)}, u32[]{:S(2)}, u32[]{:S(2)}) collective-permute-start(bf16[8,128,128]{2,1,0:T(8,128)(2,1)S(1)} %collective-permute-done.2.refs_14_), channel_id=1, source_target_pairs={{0,32},{32,0},{64,96},{96,64},{128,160},{160,128},{192,224},{224,1... | collective-permute-start | bytes 786440 | tf_op jit(solution)/shard_map/ppermute | solution.py:257
  46.8 1.7 %collective-permute-start.7 = (bf16[512,128]{1,0:T(8,128)(2,1)S(1)}, bf16[512,128]{1,0:T(8,128)(2,1)S(1)}, u32[]{:S(2)}, u32[]{:S(2)}) collective-permute-start(bf16[512,128]{1,0:T(8,128)(2,1)S(1)} %collective-permute-done.6.refs_4_), channel_id=1, source_target_pairs={{0,32},{32,0},{64,96},{96,64},{128,160},{160,128},{192,224},{224,1... | collective-permute-start | bytes 393224 | tf_op jit(solution)/shard_map/ppermute | solution.py:257
  47.3 1.4 %collective-permute-start.5 = (bf16[512,128]{1,0:T(8,128)(2,1)S(1)}, bf16[512,128]{1,0:T(8,128)(2,1)S(1)}, u32[]{:S(2)}, u32[]{:S(2)}) collective-permute-start(bf16[512,128]{1,0:T(8,128)(2,1)S(1)} %collective-permute-done.4.refs_2_), channel_id=1, source_target_pairs={{0,32},{32,0},{64,96},{96,64},{128,160},{160,128},{192,224},{224,1... | collective-permute-start | bytes 393224 | tf_op jit(solution)/shard_map/ppermute | solution.py:257

commit v6 on v5

--- a/solution.py
+++ b/solution.py
@@ -28,6 +28,18 @@
 def split_start(start):
     base = pl.multiple_of((start >> 7) << 7, 128)
     return base, start - base
+
+
+def swap_tiles(blocks, width):
+    tile = lax.broadcasted_iota(jnp.int32, (width, 128), 1) >> 5
+    odd, upper = (tile & 1) == 1, tile >= 2
+    middle = []
+    for p in (0, 2):
+        middle.append(jnp.where(odd, pltpu.roll(blocks[p + 1], 32, 1), blocks[p]))
+        middle.append(jnp.where(odd, blocks[p + 1], pltpu.roll(blocks[p], 96, 1)))
+    low = [jnp.where(upper, pltpu.roll(middle[p + 2], 64, 1), middle[p]) for p in (0, 1)]
+    high = [jnp.where(upper, middle[p + 2], pltpu.roll(middle[p], 64, 1)) for p in (0, 1)]
+    return low + high
 
 
 def cos_sin(turns):
@@ -72,22 +84,17 @@
     for copy in windows:
         copy.start()
     copies[1].wait()
-    lane = lax.broadcasted_iota(jnp.int32, (modes, 128), 1)
-    tile = lax.broadcasted_iota(jnp.int32, (16, 128), 1) >> 5
+    lane_in_block = lax.broadcasted_iota(jnp.int32, (modes, 128), 1)
 
     def step(k, start):
         base, shift = split_start(start)
         after = pl.multiple_of(jnp.minimum(base + 128, deg - 128), 128)
-        block = jnp.where(lane >= shift, bessel_ref[:, pl.ds(base, 128)], bessel_ref[:, pl.ds(after, 128)])
-        for j in range(4):
-            row = block[16 * j : 16 * j + 16]
-            for i in range(4):
-                if i != j:
-                    row = jnp.where(tile == i, pltpu.roll(block[16 * i : 16 * i + 16], (32 * (i - j)) % 128, 1), row)
+        block = jnp.where(lane_in_block >= shift, bessel_ref[:, pl.ds(base, 128)], bessel_ref[:, pl.ds(after, 128)])
+        for j, row in enumerate(swap_tiles([block[16 * i : 16 * i + 16] for i in range(4)], 16)):
             block_ref[k, 16 * j : 16 * j + 16, :] = row
         return start + lengths_ref[k]
 
-    lax.fori_loop(0, block_ref.shape[0], step, jnp.int32(0), unroll=4)
+    lax.fori_loop(0, block_ref.shape[0], step, jnp.int32(0), unroll=16)
     outputs = [pltpu.make_async_copy(block_ref, send_hbm.at[:, pl.ds(16, modes), :], sems.at[8])]
     outputs[0].start()
 
@@ -153,16 +160,8 @@
 def turn_kernel(recv_ref, out_ref, wide_ref, turned_ref):
     for s in range(32):
         wide_ref[24 * s : 24 * s + 16, :] = recv_ref[s, :16].astype(F32)
-    tile = lax.broadcasted_iota(jnp.int32, (32, 128), 1) >> 5
     for a in range(4):
-        x = [wide_ref[pl.ds(4 * a + b, 32, stride=24), :] for b in range(4)]
-        pieces = []
-        for u in range(4):
-            piece = x[u]
-            for b in range(4):
-                if b != u:
-                    piece = jnp.where(tile == b, pltpu.roll(x[b], (32 * (b - u)) % 128, 1), piece)
-            pieces.append(piece)
+        pieces = swap_tiles([wide_ref[pl.ds(4 * a + b, 32, stride=24), :] for b in range(4)], 32)
         turned = jnp.transpose(jnp.concatenate(pieces, axis=0))
         for b in range(4):
             turned_ref[pl.ds(4 * a + b, 32, stride=24), :] = turned[32 * b : 32 * b + 32]
@@ -207,20 +206,15 @@
     slot = lax.broadcasted_iota(jnp.int32, (128, 128), 0)
     degree = base + slot + jnp.where(slot < shift, 128, 0)
     first_half = lane < 64
-    tile = lax.broadcasted_iota(jnp.int32, (32, 128), 1) >> 5
     for d in range(8):
         for i in range(4):
             pair = 4 * (mine ^ d) + i
             left = rows[d][2 * i : 2 * i + 2].reshape(256, 128)
             both = jnp.dot(left, four_ref[pair].reshape(128, 128), preferred_element_type=F32)
             value = jnp.where(first_half, both[:128], both[128:])
-            value = jnp.where(degree >= info_ref[pl.ds(pair, 1), :], value, 0.0)
-            for u in range(4):
-                packed = value[32 * u : 32 * u + 32]
-                for j in range(4):
-                    if j != u:
-                        packed = jnp.where(tile == j, pltpu.roll(value[32 * j : 32 * j + 32], (32 * (j - u)) % 128, 1), packed)
-                harmonic_ref[pl.ds(2 * pair + (u & 1) * 64 + (u >> 1), 32, stride=136), :] = packed
+            value = jnp.where(degree >= info_ref[pl.ds(pair, 1), :], value, 0.0).astype(BF16)
+            for u, packed in enumerate(swap_tiles([value[32 * j : 32 * j + 32] for j in range(4)], 32)):
+                harmonic_ref[pl.ds(2 * pair + (u & 1) * 64 + (u >> 1), 32, stride=136), :] = packed.astype(F32)
     group = lax.broadcasted_iota(jnp.int32, (64, 128), 1) >> 5
     zero = jnp.zeros((64, 128), BF16)
     for g in range(32):

time: 53 us -> 51.8 us (0.977)
  Pallas kernels: 8.64 us -> 7.47 us
    pallas_call x1, Pallas kernels: 3.86 us -> 2.95 us  [on_device(): pl.pallas_call(final_kernel, out_shape=shape((128, modes, 128), BF16), in...]
where the time goes in v6:
time: 51.8 us; the launch traced here: 51.5 us
  starting transfers between devices  29 us (56%)
  waiting for transfers between devices  14.3 us (28%)
  Pallas kernels  7.47 us (14%)
  local copies, waits for them, and re-layouts  0.74 us (1%)
    ppermute x14, starting transfers between devices, swap(): return lax.ppermute(x, 'shell', [(i, i ^ d) for i in range(8)])  16.7 us
    all_to_all x1, waiting for transfers between devices, on_device(): lax.all_to_all(send, 'radial', split_axis=0, concat_axis=0, tiled=True)  13 us
    all_to_all x1, starting transfers between devices, on_device(): lax.all_to_all(send, 'radial', split_axis=0, concat_axis=0, tiled=True)  12.3 us
    pallas_call x1, Pallas kernels, on_device(): pl.pallas_call(front_kernel, out_shape=[shape((32, 16 + modes, 128), BF16...  3.43 us
    pallas_call x1, Pallas kernels, on_device(): pl.pallas_call(final_kernel, out_shape=shape((128, modes, 128), BF16), in...  2.95 us
    ppermute x14, waiting for transfers between devices, swap(): return lax.ppermute(x, 'shell', [(i, i ^ d) for i in range(8)])  1.33 us
  transfers between devices with their start and end apart: 15, of which 3 were waited for; matrix products, arithmetic and copies ran while one was open for 0% of the time, Pallas kernels for 2%

profile of v6, /device:TPU:1, one launch (start us, length us, event | category | flops | bytes accessed | tf_op | source)
XLA Modules:
  0.0 51.5 jit_solution(3776396807763010852)
XLA Ops:
  0.0 3.4 %front.1 = (bf16[32,80,128]{2,1,0:T(8,128)(2,1)}, bf16[8,128,128]{2,1,0:T(8,128)(2,1)}, s32[40,128]{1,0:T(8,128)}) custom-call(s32[32]{0:T(128)} %lengths_hbm.1, s32[16]{0:T(128)} %cycle_hbm.1, s32[64]{0:T(128)} %order_hbm.1, f32[1,16,4096]{2,1,0:T(8,128)} %density_hbm.1, s32[1,16,4096]{2,1,0:T(8,128)} %footprint_hbm.1, bf16[64,2048]{1,0:T(8,128)(2,1)} %bitcast.3, ...), custom_call_target="tpu_custom_call" | custom-call | flops 2000000000 | bytes 2097152 | tf_op jit(solution)/shard_map/front/pallas_call | solution.py:253
  3.5 12.3 %all-to-all-start = ((bf16[32,80,128]{2,1,0:T(8,128)(2,1)}), bf16[32,80,128]{2,1,0:T(8,128)(2,1)S(1)}, u32[]{:S(2)}, u32[]{:S(2)}) async-start(bf16[32,80,128]{2,1,0:T(8,128)(2,1)} %get-tuple-element.14), calls=%async_computation | async-start | bytes 1310720 | tf_op jit(solution)/shard_map/all_to_all | solution.py:277
  15.7 2.6 %collective-permute-start.2 = (bf16[8,128,128]{2,1,0:T(8,128)(2,1)}, bf16[8,128,128]{2,1,0:T(8,128)(2,1)S(1)}, u32[]{:S(2)}, u32[]{:S(2)}) collective-permute-start(bf16[8,128,128]{2,1,0:T(8,128)(2,1)} %get-tuple-element.15.refs_8_), channel_id=1, source_target_pairs={{0,192},{32,224},{64,128},{96,160},{128,64},{160,96},{192,0},{224,... | collective-permute-start | bytes 786440 | tf_op jit(solution)/shard_map/ppermute | solution.py:251
  18.3 0.0 collective-permute-start.1
  18.3 1.4 %collective-permute-start = (bf16[8,128,128]{2,1,0:T(8,128)(2,1)}, bf16[8,128,128]{2,1,0:T(8,128)(2,1)S(1)}, u32[]{:S(2)}, u32[]{:S(2)}) collective-permute-start(bf16[8,128,128]{2,1,0:T(8,128)(2,1)} %get-tuple-element.15.refs_8_), channel_id=1, source_target_pairs={{0,128},{32,160},{64,192},{96,224},{128,0},{160,32},{192,64},{224,... | collective-permute-start | bytes 786440 | tf_op jit(solution)/shard_map/ppermute | solution.py:251
  19.7 1.8 %collective-permute-start.10 = (bf16[8,128,128]{2,1,0:T(8,128)(2,1)}, bf16[8,128,128]{2,1,0:T(8,128)(2,1)S(1)}, u32[]{:S(2)}, u32[]{:S(2)}) collective-permute-start(bf16[8,128,128]{2,1,0:T(8,128)(2,1)} %get-tuple-element.15.refs_8_), channel_id=1, source_target_pairs={{0,32},{32,0},{64,96},{96,64},{128,160},{160,128},{192,224},{224,1... | collective-permute-start | bytes 786440 | tf_op jit(solution)/shard_map/ppermute | solution.py:251
  21.5 13.0 %all-to-all-done.recv_ref = bf16[32,80,128]{2,1,0:T(8,128)(2,1)S(1)} async-done(((bf16[32,80,128]{2,1,0:T(8,128)(2,1)}), bf16[32,80,128]{2,1,0:T(8,128)(2,1)S(1)}, u32[]{:S(2)}, u32[]{:S(2)}) %all-to-all-start) | async-done | bytes 655392 | tf_op jit(solution)/shard_map/all_to_all | solution.py:277
  34.4 0.4 turn.1.refs_0_
  34.9 2.6 %collective-permute-start.8 = (bf16[512,128]{1,0:T(8,128)(2,1)S(1)}, bf16[512,128]{1,0:T(8,128)(2,1)S(1)}, u32[]{:S(2)}, u32[]{:S(2)}) collective-permute-start(bf16[512,128]{1,0:T(8,128)(2,1)S(1)} %turn.1.refs_0_), channel_id=1, source_target_pairs={{0,192},{32,224},{64,128},{96,160},{128,64},{160,96},{192,0},{224,... | collective-permute-start | bytes 393224 | tf_op jit(solution)/shard_map/ppermute | solution.py:251
  37.4 0.0 collective-permute-done.2.refs_14_
  37.4 0.5 %collective-permute-start.6 = (bf16[512,128]{1,0:T(8,128)(2,1)S(1)}, bf16[512,128]{1,0:T(8,128)(2,1)S(1)}, u32[]{:S(2)}, u32[]{:S(2)}) collective-permute-start(bf16[512,128]{1,0:T(8,128)(2,1)S(1)} %turn.1.refs_0_), channel_id=1, source_target_pairs={{0,128},{32,160},{64,192},{96,224},{128,0},{160,32},{192,64},{224,... | collective-permute-start | bytes 393224 | tf_op jit(solution)/shard_map/ppermute | solution.py:251
  38.0 0.0 collective-permute-done.1.refs_10_
  38.0 0.3 collective-permute-start.4
  38.2 0.7 %copy-done.1 = s32[40,128]{1,0:T(8,128)S(1)} copy-done((s32[40,128]{1,0:T(8,128)S(1)}, s32[40,128]{1,0:T(8,128)}, u32[]{:S(2)}) %copy-start.1) | copy-done | bytes 20504
  38.9 0.7 %radial_rows.1.radial_ref = bf16[32,64,128]{2,1,0:T(8,128)(2,1)S(1)} custom-call(s32[40,128]{1,0:T(8,128)S(1)} %copy-done.1, bf16[32,80,128]{2,1,0:T(8,128)(2,1)S(1)} %all-to-all-done.recv_ref), custom_call_target="tpu_custom_call" | custom-call | flops 1500000000 | bytes 1048576 | tf_op jit(solution)/shard_map/radial_rows/pallas_call | solution.py:294
  39.6 0.0 collective-permute-done.refs_12_
  39.6 3.4 %collective-permute-start.3 = (bf16[512,128]{1,0:T(8,128)(2,1)S(1)}, bf16[512,128]{1,0:T(8,128)(2,1)S(1)}, u32[]{:S(2)}, u32[]{:S(2)}) collective-permute-start(bf16[512,128]{1,0:T(8,128)(2,1)S(1)} %turn.1.refs_0_), channel_id=1, source_target_pairs={{0,32},{32,0},{64,96},{96,64},{128,160},{160,128},{192,224},{224,1... | collective-permute-start | bytes 393224 | tf_op jit(solution)/shard_map/ppermute | solution.py:251
  43.0 0.0 collective-permute-done.10.refs_9_
  43.0 0.1 collective-permute-start.11
  43.1 0.0 collective-permute-done.8.refs_6_
  43.1 1.7 %collective-permute-start.9 = (bf16[512,128]{1,0:T(8,128)(2,1)S(1)}, bf16[512,128]{1,0:T(8,128)(2,1)S(1)}, u32[]{:S(2)}, u32[]{:S(2)}) collective-permute-start(bf16[512,128]{1,0:T(8,128)(2,1)S(1)} %collective-permute-done.8.refs_6_), channel_id=1, source_target_pairs={{0,32},{32,0},{64,96},{96,64},{128,160},{160,128},{192,224},{224,1... | collective-permute-start | bytes 393224 | tf_op jit(solution)/shard_map/ppermute | solution.py:251
  44.9 0.0 collective-permute-done.6.refs_4_
  44.9 1.8 %collective-permute-start.12 = (bf16[8,128,128]{2,1,0:T(8,128)(2,1)S(1)}, bf16[8,128,128]{2,1,0:T(8,128)(2,1)S(1)}, u32[]{:S(2)}, u32[]{:S(2)}) collective-permute-start(bf16[8,128,128]{2,1,0:T(8,128)(2,1)S(1)} %collective-permute-done.refs_12_), channel_id=1, source_target_pairs={{0,32},{32,0},{64,96},{96,64},{128,160},{160,128},{192,224},{224,1... | collective-permute-start | bytes 786440 | tf_op jit(solution)/shard_map/ppermute | solution.py:251
  46.7 0.0 collective-permute-done.4.refs_2_
  46.7 0.0 collective-permute-start.13
  46.7 0.5 collective-permute-start.7
  47.2 0.0 collective-permute-done.9.refs_7_
  47.2 0.1 collective-permute-start.5
  47.3 1.1 %collective-permute-done.7.refs_5_ = bf16[512,128]{1,0:T(8,128)(2,1)S(1)} collective-permute-done((bf16[512,128]{1,0:T(8,128)(2,1)S(1)}, bf16[512,128]{1,0:T(8,128)(2,1)S(1)}, u32[]{:S(2)}, u32[]{:S(2)}) %collective-permute-start.7) | collective-permute-done | bytes 131104 | tf_op jit(solution)/shard_map/ppermute | solution.py:251
  48.4 0.2 collective-permute-done.5.refs_3_
  48.6 0.0 collective-permute-done.11.refs_11_
  48.6 2.9 %finish.1 = bf16[128,64,128]{2,1,0:T(8,128)(2,1)} custom-call(s32[40,128]{1,0:T(8,128)S(1)} %copy-done.2, bf16[32,64,128]{2,1,0:T(8,128)(2,1)S(1)} %radial_rows.1.radial_ref, bf16[512,128]{1,0:T(8,128)(2,1)S(1)} %turn.1.refs_0_, bf16[512,128]{1,0:T(8,128)(2,1)S(1)} %collective-permute-done.3.refs_1_, bf16[512,128]{1,0:T(8,128)(2,1)S(1)} %collective-permute-done.4.refs_2_, ...), custom_call_target="tpu_custom_call" | custom-call | flops 2500000000 | bytes 4194304 | tf_op jit(solution)/shard_map/finish/pallas_call | solution.py:316
  (8 shorter events, 0.0 us)
Async XLA Ops:
  3.4 45.1 %copy-start = (bf16[8,128,128]{2,1,0:T(8,128)(2,1)S(1)}, bf16[8,128,128]{2,1,0:T(8,128)(2,1)}, u32[]{:S(2)}) copy-start(bf16[8,128,128]{2,1,0:T(8,128)(2,1)} %get-tuple-element.15.refs_8_) | copy-start | bytes 786436
  3.4 45.1 %copy-start.2 = (s32[40,128]{1,0:T(8,128)S(1)}, s32[40,128]{1,0:T(8,128)}, u32[]{:S(2)}) copy-start(s32[40,128]{1,0:T(8,128)} %get-tuple-element.13.info_ref) | copy-start | bytes 61444
  3.5 31.0 %all-to-all-start = ((bf16[32,80,128]{2,1,0:T(8,128)(2,1)}), bf16[32,80,128]{2,1,0:T(8,128)(2,1)S(1)}, u32[]{:S(2)}, u32[]{:S(2)}) async-start(bf16[32,80,128]{2,1,0:T(8,128)(2,1)} %get-tuple-element.14), calls=%async_computation | async-start | bytes 1310720 | tf_op jit(solution)/shard_map/all_to_all | solution.py:277
  15.7 21.7 %collective-permute-start.2 = (bf16[8,128,128]{2,1,0:T(8,128)(2,1)}, bf16[8,128,128]{2,1,0:T(8,128)(2,1)S(1)}, u32[]{:S(2)}, u32[]{:S(2)}) collective-permute-start(bf16[8,128,128]{2,1,0:T(8,128)(2,1)} %get-tuple-element.15.refs_8_), channel_id=1, source_target_pairs={{0,192},{32,224},{64,128},{96,160},{128,64},{160,96},{192,0},{224,... | collective-permute-start | bytes 786440 | tf_op jit(solution)/shard_map/ppermute | solution.py:251
  18.3 19.7 %collective-permute-start.1 = (bf16[8,128,128]{2,1,0:T(8,128)(2,1)}, bf16[8,128,128]{2,1,0:T(8,128)(2,1)S(1)}, u32[]{:S(2)}, u32[]{:S(2)}) collective-permute-start(bf16[8,128,128]{2,1,0:T(8,128)(2,1)} %get-tuple-element.15.refs_8_), channel_id=1, source_target_pairs={{0,64},{32,96},{64,0},{96,32},{128,192},{160,224},{192,128},{224,1... | collective-permute-start | bytes 786440 | tf_op jit(solution)/shard_map/ppermute | solution.py:251
  18.3 21.3 %collective-permute-start = (bf16[8,128,128]{2,1,0:T(8,128)(2,1)}, bf16[8,128,128]{2,1,0:T(8,128)(2,1)S(1)}, u32[]{:S(2)}, u32[]{:S(2)}) collective-permute-start(bf16[8,128,128]{2,1,0:T(8,128)(2,1)} %get-tuple-element.15.refs_8_), channel_id=1, source_target_pairs={{0,128},{32,160},{64,192},{96,224},{128,0},{160,32},{192,64},{224,... | collective-permute-start | bytes 786440 | tf_op jit(solution)/shard_map/ppermute | solution.py:251
  19.7 23.3 %collective-permute-start.10 = (bf16[8,128,128]{2,1,0:T(8,128)(2,1)}, bf16[8,128,128]{2,1,0:T(8,128)(2,1)S(1)}, u32[]{:S(2)}, u32[]{:S(2)}) collective-permute-start(bf16[8,128,128]{2,1,0:T(8,128)(2,1)} %get-tuple-element.15.refs_8_), channel_id=1, source_target_pairs={{0,32},{32,0},{64,96},{96,64},{128,160},{160,128},{192,224},{224,1... | collective-permute-start | bytes 786440 | tf_op jit(solution)/shard_map/ppermute | solution.py:251
  34.9 8.3 %collective-permute-start.8 = (bf16[512,128]{1,0:T(8,128)(2,1)S(1)}, bf16[512,128]{1,0:T(8,128)(2,1)S(1)}, u32[]{:S(2)}, u32[]{:S(2)}) collective-permute-start(bf16[512,128]{1,0:T(8,128)(2,1)S(1)} %turn.1.refs_0_), channel_id=1, source_target_pairs={{0,192},{32,224},{64,128},{96,160},{128,64},{160,96},{192,0},{224,... | collective-permute-start | bytes 393224 | tf_op jit(solution)/shard_map/ppermute | solution.py:251
  37.4 7.4 %collective-permute-start.6 = (bf16[512,128]{1,0:T(8,128)(2,1)S(1)}, bf16[512,128]{1,0:T(8,128)(2,1)S(1)}, u32[]{:S(2)}, u32[]{:S(2)}) collective-permute-start(bf16[512,128]{1,0:T(8,128)(2,1)S(1)} %turn.1.refs_0_), channel_id=1, source_target_pairs={{0,128},{32,160},{64,192},{96,224},{128,0},{160,32},{192,64},{224,... | collective-permute-start | bytes 393224 | tf_op jit(solution)/shard_map/ppermute | solution.py:251
  38.0 8.7 %collective-permute-start.4 = (bf16[512,128]{1,0:T(8,128)(2,1)S(1)}, bf16[512,128]{1,0:T(8,128)(2,1)S(1)}, u32[]{:S(2)}, u32[]{:S(2)}) collective-permute-start(bf16[512,128]{1,0:T(8,128)(2,1)S(1)} %turn.1.refs_0_), channel_id=1, source_target_pairs={{0,64},{32,96},{64,0},{96,32},{128,192},{160,224},{192,128},{224,1... | collective-permute-start | bytes 393224 | tf_op jit(solution)/shard_map/ppermute | solution.py:251
  38.2 0.7 %copy-start.1 = (s32[40,128]{1,0:T(8,128)S(1)}, s32[40,128]{1,0:T(8,128)}, u32[]{:S(2)}) copy-start(s32[40,128]{1,0:T(8,128)} %get-tuple-element.13.info_ref) | copy-start | bytes 61444
  39.6 7.0 %collective-permute-start.3 = (bf16[512,128]{1,0:T(8,128)(2,1)S(1)}, bf16[512,128]{1,0:T(8,128)(2,1)S(1)}, u32[]{:S(2)}, u32[]{:S(2)}) collective-permute-start(bf16[512,128]{1,0:T(8,128)(2,1)S(1)} %turn.1.refs_0_), channel_id=1, source_target_pairs={{0,32},{32,0},{64,96},{96,64},{128,160},{160,128},{192,224},{224,1... | collective-permute-start | bytes 393224 | tf_op jit(solution)/shard_map/ppermute | solution.py:251
  43.0 5.5 %collective-permute-start.11 = (bf16[8,128,128]{2,1,0:T(8,128)(2,1)S(1)}, bf16[8,128,128]{2,1,0:T(8,128)(2,1)S(1)}, u32[]{:S(2)}, u32[]{:S(2)}) collective-permute-start(bf16[8,128,128]{2,1,0:T(8,128)(2,1)S(1)} %collective-permute-done.1.refs_10_), channel_id=1, source_target_pairs={{0,32},{32,0},{64,96},{96,64},{128,160},{160,128},{192,224},{224,1... | collective-permute-start | bytes 786440 | tf_op jit(solution)/shard_map/ppermute | solution.py:251
  43.1 4.0 %collective-permute-start.9 = (bf16[512,128]{1,0:T(8,128)(2,1)S(1)}, bf16[512,128]{1,0:T(8,128)(2,1)S(1)}, u32[]{:S(2)}, u32[]{:S(2)}) collective-permute-start(bf16[512,128]{1,0:T(8,128)(2,1)S(1)} %collective-permute-done.8.refs_6_), channel_id=1, source_target_pairs={{0,32},{32,0},{64,96},{96,64},{128,160},{160,128},{192,224},{224,1... | collective-permute-start | bytes 393224 | tf_op jit(solution)/shard_map/ppermute | solution.py:251
  44.9 3.7 %collective-permute-start.12 = (bf16[8,128,128]{2,1,0:T(8,128)(2,1)S(1)}, bf16[8,128,128]{2,1,0:T(8,128)(2,1)S(1)}, u32[]{:S(2)}, u32[]{:S(2)}) collective-permute-start(bf16[8,128,128]{2,1,0:T(8,128)(2,1)S(1)} %collective-permute-done.refs_12_), channel_id=1, source_target_pairs={{0,32},{32,0},{64,96},{96,64},{128,160},{160,128},{192,224},{224,1... | collective-permute-start | bytes 786440 | tf_op jit(solution)/shard_map/ppermute | solution.py:251
  46.7 1.9 %collective-permute-start.13 = (bf16[8,128,128]{2,1,0:T(8,128)(2,1)S(1)}, bf16[8,128,128]{2,1,0:T(8,128)(2,1)S(1)}, u32[]{:S(2)}, u32[]{:S(2)}) collective-permute-start(bf16[8,128,128]{2,1,0:T(8,128)(2,1)S(1)} %collective-permute-done.2.refs_14_), channel_id=1, source_target_pairs={{0,32},{32,0},{64,96},{96,64},{128,160},{160,128},{192,224},{224,1... | collective-permute-start | bytes 786440 | tf_op jit(solution)/shard_map/ppermute | solution.py:251
  46.7 1.7 %collective-permute-start.7 = (bf16[512,128]{1,0:T(8,128)(2,1)S(1)}, bf16[512,128]{1,0:T(8,128)(2,1)S(1)}, u32[]{:S(2)}, u32[]{:S(2)}) collective-permute-start(bf16[512,128]{1,0:T(8,128)(2,1)S(1)} %collective-permute-done.6.refs_4_), channel_id=1, source_target_pairs={{0,32},{32,0},{64,96},{96,64},{128,160},{160,128},{192,224},{224,1... | collective-permute-start | bytes 393224 | tf_op jit(solution)/shard_map/ppermute | solution.py:251
  47.2 1.4 %collective-permute-start.5 = (bf16[512,128]{1,0:T(8,128)(2,1)S(1)}, bf16[512,128]{1,0:T(8,128)(2,1)S(1)}, u32[]{:S(2)}, u32[]{:S(2)}) collective-permute-start(bf16[512,128]{1,0:T(8,128)(2,1)S(1)} %collective-permute-done.4.refs_2_), channel_id=1, source_target_pairs={{0,32},{32,0},{64,96},{96,64},{128,160},{160,128},{192,224},{224,1... | collective-permute-start | bytes 393224 | tf_op jit(solution)/shard_map/ppermute | solution.py:251

commit v7 on v6

--- a/solution.py
+++ b/solution.py
@@ -279,6 +279,8 @@
     row_pieces = {0: leg_rows, 1: swap(leg_rows, 1)}
     for d in (4, 2, 6):
         row_pieces[d] = swap(leg_rows, d)
+    for d in (4, 2, 6):
+        row_pieces[d + 1] = swap(row_pieces[d], 1)
 
     four = pl.pallas_call(
         turn_kernel,
@@ -305,11 +307,8 @@
     pieces = {0: four}
     for d in (2, 6, 4):
         pieces[d] = swap(four, d)
-    own, radial, *moved = lax.optimization_barrier((four, radial, *[row_pieces[d] for d in (4, 2, 6)]))
+    own, radial = lax.optimization_barrier((four, radial))
     pieces[1] = swap(own, 1)
-    for d, piece in zip((4, 2, 6), moved):
-        row_pieces[d] = piece
-        row_pieces[d + 1] = swap(piece, 1)
     for d in (2, 6, 4):
         pieces[d + 1] = swap(pieces[d], 1)
 

time: 51.8 us -> 51.2 us (0.988)
  waiting for transfers between devices: 14.3 us -> 12.4 us
  starting transfers between devices: 29 us -> 30.2 us
    all_to_all x1, waiting for transfers between devices: 13 us -> 2.23 us  [on_device(): lax.all_to_all(send, 'radial', split_axis=0, concat_axis=0, tiled=True)]
    ppermute x14, waiting for transfers between devices: 1.33 us -> 10.2 us  [swap(): return lax.ppermute(x, 'shell', [(i, i ^ d) for i in range(8)])]
    ppermute x14, starting transfers between devices: 16.7 us -> 18 us  [swap(): return lax.ppermute(x, 'shell', [(i, i ^ d) for i in range(8)])]
  transfers between devices with their start and end apart: 15 -> 15, of which waited for: 3 -> 4; matrix products, arithmetic and copies ran while one was open for 0% -> 0% of each run, Pallas kernels for 2% -> 2%
where the time goes in v7:
time: 51.2 us; the launch traced here: 50.9 us
  starting transfers between devices  30.2 us (59%)
  waiting for transfers between devices  12.4 us (24%)
  Pallas kernels  7.47 us (15%)
  local copies, waits for them, and re-layouts  0.73 us (1%)
    ppermute x14, starting transfers between devices, swap(): return lax.ppermute(x, 'shell', [(i, i ^ d) for i in range(8)])  18 us
    all_to_all x1, starting transfers between devices, on_device(): lax.all_to_all(send, 'radial', split_axis=0, concat_axis=0, tiled=True)  12.3 us
    ppermute x14, waiting for transfers between devices, swap(): return lax.ppermute(x, 'shell', [(i, i ^ d) for i in range(8)])  10.2 us
    pallas_call x1, Pallas kernels, on_device(): pl.pallas_call(front_kernel, out_shape=[shape((32, 16 + modes, 128), BF16...  3.43 us
    pallas_call x1, Pallas kernels, on_device(): pl.pallas_call(final_kernel, out_shape=shape((128, modes, 128), BF16), in...  2.94 us
    all_to_all x1, waiting for transfers between devices, on_device(): lax.all_to_all(send, 'radial', split_axis=0, concat_axis=0, tiled=True)  2.23 us
  transfers between devices with their start and end apart: 15, of which 4 were waited for; matrix products, arithmetic and copies ran while one was open for 0% of the time, Pallas kernels for 2%

profile of v7, /device:TPU:1, one launch (start us, length us, event | category | flops | bytes accessed | tf_op | source)
XLA Modules:
  0.0 50.9 jit_solution(15493613118073263826)
XLA Ops:
  0.0 3.4 %front.1 = (bf16[32,80,128]{2,1,0:T(8,128)(2,1)}, bf16[8,128,128]{2,1,0:T(8,128)(2,1)}, s32[40,128]{1,0:T(8,128)}) custom-call(s32[32]{0:T(128)} %lengths_hbm.1, s32[16]{0:T(128)} %cycle_hbm.1, s32[64]{0:T(128)} %order_hbm.1, f32[1,16,4096]{2,1,0:T(8,128)} %density_hbm.1, s32[1,16,4096]{2,1,0:T(8,128)} %footprint_hbm.1, bf16[64,2048]{1,0:T(8,128)(2,1)} %bitcast.3, ...), custom_call_target="tpu_custom_call" | custom-call | flops 2000000000 | bytes 2097152 | tf_op jit(solution)/shard_map/front/pallas_call | solution.py:253
  3.4 12.3 %all-to-all-start = ((bf16[32,80,128]{2,1,0:T(8,128)(2,1)}), bf16[32,80,128]{2,1,0:T(8,128)(2,1)S(1)}, u32[]{:S(2)}, u32[]{:S(2)}) async-start(bf16[32,80,128]{2,1,0:T(8,128)(2,1)} %get-tuple-element.11), calls=%async_computation | async-start | bytes 1310720 | tf_op jit(solution)/shard_map/all_to_all | solution.py:277
  15.7 2.6 %collective-permute-start.12 = (bf16[8,128,128]{2,1,0:T(8,128)(2,1)}, bf16[8,128,128]{2,1,0:T(8,128)(2,1)S(1)}, u32[]{:S(2)}, u32[]{:S(2)}) collective-permute-start(bf16[8,128,128]{2,1,0:T(8,128)(2,1)} %get-tuple-element.14.refs_8_), channel_id=1, source_target_pairs={{0,192},{32,224},{64,128},{96,160},{128,64},{160,96},{192,0},{224,... | collective-permute-start | bytes 786440 | tf_op jit(solution)/shard_map/ppermute | solution.py:251
  18.3 0.5 %collective-permute-start.10 = (bf16[8,128,128]{2,1,0:T(8,128)(2,1)}, bf16[8,128,128]{2,1,0:T(8,128)(2,1)S(1)}, u32[]{:S(2)}, u32[]{:S(2)}) collective-permute-start(bf16[8,128,128]{2,1,0:T(8,128)(2,1)} %get-tuple-element.14.refs_8_), channel_id=1, source_target_pairs={{0,128},{32,160},{64,192},{96,224},{128,0},{160,32},{192,64},{224,... | collective-permute-start | bytes 786440 | tf_op jit(solution)/shard_map/ppermute | solution.py:251
  18.8 0.3 collective-permute-start.8
  19.1 1.8 %collective-permute-start.7 = (bf16[8,128,128]{2,1,0:T(8,128)(2,1)}, bf16[8,128,128]{2,1,0:T(8,128)(2,1)S(1)}, u32[]{:S(2)}, u32[]{:S(2)}) collective-permute-start(bf16[8,128,128]{2,1,0:T(8,128)(2,1)} %get-tuple-element.14.refs_8_), channel_id=1, source_target_pairs={{0,32},{32,0},{64,96},{96,64},{128,160},{160,128},{192,224},{224,1... | collective-permute-start | bytes 786440 | tf_op jit(solution)/shard_map/ppermute | solution.py:251
  20.9 8.8 %collective-permute-done.12.refs_14_ = bf16[8,128,128]{2,1,0:T(8,128)(2,1)S(1)} collective-permute-done((bf16[8,128,128]{2,1,0:T(8,128)(2,1)}, bf16[8,128,128]{2,1,0:T(8,128)(2,1)S(1)}, u32[]{:S(2)}, u32[]{:S(2)}) %collective-permute-start.12) | collective-permute-done | bytes 262176 | tf_op jit(solution)/shard_map/ppermute | solution.py:251
  29.7 1.9 %collective-permute-start.13 = (bf16[8,128,128]{2,1,0:T(8,128)(2,1)S(1)}, bf16[8,128,128]{2,1,0:T(8,128)(2,1)S(1)}, u32[]{:S(2)}, u32[]{:S(2)}) collective-permute-start(bf16[8,128,128]{2,1,0:T(8,128)(2,1)S(1)} %collective-permute-done.12.refs_14_), channel_id=1, source_target_pairs={{0,32},{32,0},{64,96},{96,64},{128,160},{160,128},{192,224},{224,1... | collective-permute-start | bytes 786440 | tf_op jit(solution)/shard_map/ppermute | solution.py:251
  31.6 0.0 collective-permute-done.10.refs_12_
  31.6 0.0 collective-permute-start.11
  31.6 0.0 collective-permute-done.8.refs_10_
  31.6 0.6 %collective-permute-start.9 = (bf16[8,128,128]{2,1,0:T(8,128)(2,1)S(1)}, bf16[8,128,128]{2,1,0:T(8,128)(2,1)S(1)}, u32[]{:S(2)}, u32[]{:S(2)}) collective-permute-start(bf16[8,128,128]{2,1,0:T(8,128)(2,1)S(1)} %collective-permute-done.8.refs_10_), channel_id=1, source_target_pairs={{0,32},{32,0},{64,96},{96,64},{128,160},{160,128},{192,224},{224,1... | collective-permute-start | bytes 786440 | tf_op jit(solution)/shard_map/ppermute | solution.py:251
  32.2 2.2 %all-to-all-done.recv_ref = bf16[32,80,128]{2,1,0:T(8,128)(2,1)S(1)} async-done(((bf16[32,80,128]{2,1,0:T(8,128)(2,1)}), bf16[32,80,128]{2,1,0:T(8,128)(2,1)S(1)}, u32[]{:S(2)}, u32[]{:S(2)}) %all-to-all-start) | async-done | bytes 655392 | tf_op jit(solution)/shard_map/all_to_all | solution.py:277
  34.4 0.4 turn.1.refs_0_
  34.9 2.6 %collective-permute-start.5 = (bf16[512,128]{1,0:T(8,128)(2,1)S(1)}, bf16[512,128]{1,0:T(8,128)(2,1)S(1)}, u32[]{:S(2)}, u32[]{:S(2)}) collective-permute-start(bf16[512,128]{1,0:T(8,128)(2,1)S(1)} %turn.1.refs_0_), channel_id=1, source_target_pairs={{0,192},{32,224},{64,128},{96,160},{128,64},{160,96},{192,0},{224,... | collective-permute-start | bytes 393224 | tf_op jit(solution)/shard_map/ppermute | solution.py:251
  37.4 0.0 collective-permute-done.7.refs_9_
  37.4 0.5 %collective-permute-start.3 = (bf16[512,128]{1,0:T(8,128)(2,1)S(1)}, bf16[512,128]{1,0:T(8,128)(2,1)S(1)}, u32[]{:S(2)}, u32[]{:S(2)}) collective-permute-start(bf16[512,128]{1,0:T(8,128)(2,1)S(1)} %turn.1.refs_0_), channel_id=1, source_target_pairs={{0,128},{32,160},{64,192},{96,224},{128,0},{160,32},{192,64},{224,... | collective-permute-start | bytes 393224 | tf_op jit(solution)/shard_map/ppermute | solution.py:251
  38.0 0.0 collective-permute-done.13.refs_15_
  38.0 0.3 collective-permute-start.1
  38.2 0.7 %copy-done.1 = s32[40,128]{1,0:T(8,128)S(1)} copy-done((s32[40,128]{1,0:T(8,128)S(1)}, s32[40,128]{1,0:T(8,128)}, u32[]{:S(2)}) %copy-start.1) | copy-done | bytes 20504
  38.9 0.7 %radial_rows.1.radial_ref = bf16[32,64,128]{2,1,0:T(8,128)(2,1)S(1)} custom-call(s32[40,128]{1,0:T(8,128)S(1)} %copy-done.1, bf16[32,80,128]{2,1,0:T(8,128)(2,1)S(1)} %all-to-all-done.recv_ref), custom_call_target="tpu_custom_call" | custom-call | flops 1500000000 | bytes 1048576 | tf_op jit(solution)/shard_map/radial_rows/pallas_call | solution.py:296
  39.6 0.0 collective-permute-done.11.refs_13_
  39.6 3.4 %collective-permute-start = (bf16[512,128]{1,0:T(8,128)(2,1)S(1)}, bf16[512,128]{1,0:T(8,128)(2,1)S(1)}, u32[]{:S(2)}, u32[]{:S(2)}) collective-permute-start(bf16[512,128]{1,0:T(8,128)(2,1)S(1)} %turn.1.refs_0_), channel_id=1, source_target_pairs={{0,32},{32,0},{64,96},{96,64},{128,160},{160,128},{192,224},{224,1... | collective-permute-start | bytes 393224 | tf_op jit(solution)/shard_map/ppermute | solution.py:251
  43.0 1.8 %collective-permute-start.6 = (bf16[512,128]{1,0:T(8,128)(2,1)S(1)}, bf16[512,128]{1,0:T(8,128)(2,1)S(1)}, u32[]{:S(2)}, u32[]{:S(2)}) collective-permute-start(bf16[512,128]{1,0:T(8,128)(2,1)S(1)} %collective-permute-done.5.refs_6_), channel_id=1, source_target_pairs={{0,32},{32,0},{64,96},{96,64},{128,160},{160,128},{192,224},{224,1... | collective-permute-start | bytes 393224 | tf_op jit(solution)/shard_map/ppermute | solution.py:251
  44.8 0.0 collective-permute-done.3.refs_4_
  44.9 1.8 %collective-permute-start.4 = (bf16[512,128]{1,0:T(8,128)(2,1)S(1)}, bf16[512,128]{1,0:T(8,128)(2,1)S(1)}, u32[]{:S(2)}, u32[]{:S(2)}) collective-permute-start(bf16[512,128]{1,0:T(8,128)(2,1)S(1)} %collective-permute-done.3.refs_4_), channel_id=1, source_target_pairs={{0,32},{32,0},{64,96},{96,64},{128,160},{160,128},{192,224},{224,1... | collective-permute-start | bytes 393224 | tf_op jit(solution)/shard_map/ppermute | solution.py:251
  46.6 0.0 collective-permute-done.1.refs_2_
  46.6 0.0 collective-permute-start.2
  46.6 0.0 collective-permute-done.9.refs_11_
  46.7 1.0 %collective-permute-done.4.refs_5_ = bf16[512,128]{1,0:T(8,128)(2,1)S(1)} collective-permute-done((bf16[512,128]{1,0:T(8,128)(2,1)S(1)}, bf16[512,128]{1,0:T(8,128)(2,1)S(1)}, u32[]{:S(2)}, u32[]{:S(2)}) %collective-permute-start.4) | collective-permute-done | bytes 131104 | tf_op jit(solution)/shard_map/ppermute | solution.py:251
  47.6 0.4 collective-permute-done.2.refs_3_
  48.0 2.9 %finish.1 = bf16[128,64,128]{2,1,0:T(8,128)(2,1)} custom-call(s32[40,128]{1,0:T(8,128)S(1)} %copy-done.1, bf16[32,64,128]{2,1,0:T(8,128)(2,1)S(1)} %radial_rows.1.radial_ref, bf16[512,128]{1,0:T(8,128)(2,1)S(1)} %turn.1.refs_0_, bf16[512,128]{1,0:T(8,128)(2,1)S(1)} %collective-permute-done.refs_1_, bf16[512,128]{1,0:T(8,128)(2,1)S(1)} %collective-permute-done.1.refs_2_, ...), custom_call_target="tpu_custom_call" | custom-call | flops 2500000000 | bytes 4194304 | tf_op jit(solution)/shard_map/finish/pallas_call | solution.py:315
  (6 shorter events, 0.0 us)
Async XLA Ops:
  3.4 44.6 %copy-start = (bf16[8,128,128]{2,1,0:T(8,128)(2,1)S(1)}, bf16[8,128,128]{2,1,0:T(8,128)(2,1)}, u32[]{:S(2)}) copy-start(bf16[8,128,128]{2,1,0:T(8,128)(2,1)} %get-tuple-element.14.refs_8_) | copy-start | bytes 786436
  3.4 31.0 %all-to-all-start = ((bf16[32,80,128]{2,1,0:T(8,128)(2,1)}), bf16[32,80,128]{2,1,0:T(8,128)(2,1)S(1)}, u32[]{:S(2)}, u32[]{:S(2)}) async-start(bf16[32,80,128]{2,1,0:T(8,128)(2,1)} %get-tuple-element.11), calls=%async_computation | async-start | bytes 1310720 | tf_op jit(solution)/shard_map/all_to_all | solution.py:277
  15.7 14.0 %collective-permute-start.12 = (bf16[8,128,128]{2,1,0:T(8,128)(2,1)}, bf16[8,128,128]{2,1,0:T(8,128)(2,1)S(1)}, u32[]{:S(2)}, u32[]{:S(2)}) collective-permute-start(bf16[8,128,128]{2,1,0:T(8,128)(2,1)} %get-tuple-element.14.refs_8_), channel_id=1, source_target_pairs={{0,192},{32,224},{64,128},{96,160},{128,64},{160,96},{192,0},{224,... | collective-permute-start | bytes 786440 | tf_op jit(solution)/shard_map/ppermute | solution.py:251
  18.3 13.3 %collective-permute-start.10 = (bf16[8,128,128]{2,1,0:T(8,128)(2,1)}, bf16[8,128,128]{2,1,0:T(8,128)(2,1)S(1)}, u32[]{:S(2)}, u32[]{:S(2)}) collective-permute-start(bf16[8,128,128]{2,1,0:T(8,128)(2,1)} %get-tuple-element.14.refs_8_), channel_id=1, source_target_pairs={{0,128},{32,160},{64,192},{96,224},{128,0},{160,32},{192,64},{224,... | collective-permute-start | bytes 786440 | tf_op jit(solution)/shard_map/ppermute | solution.py:251
  18.8 12.8 %collective-permute-start.8 = (bf16[8,128,128]{2,1,0:T(8,128)(2,1)}, bf16[8,128,128]{2,1,0:T(8,128)(2,1)S(1)}, u32[]{:S(2)}, u32[]{:S(2)}) collective-permute-start(bf16[8,128,128]{2,1,0:T(8,128)(2,1)} %get-tuple-element.14.refs_8_), channel_id=1, source_target_pairs={{0,64},{32,96},{64,0},{96,32},{128,192},{160,224},{192,128},{224,1... | collective-permute-start | bytes 786440 | tf_op jit(solution)/shard_map/ppermute | solution.py:251
  19.1 18.4 %collective-permute-start.7 = (bf16[8,128,128]{2,1,0:T(8,128)(2,1)}, bf16[8,128,128]{2,1,0:T(8,128)(2,1)S(1)}, u32[]{:S(2)}, u32[]{:S(2)}) collective-permute-start(bf16[8,128,128]{2,1,0:T(8,128)(2,1)} %get-tuple-element.14.refs_8_), channel_id=1, source_target_pairs={{0,32},{32,0},{64,96},{96,64},{128,160},{160,128},{192,224},{224,1... | collective-permute-start | bytes 786440 | tf_op jit(solution)/shard_map/ppermute | solution.py:251
  29.7 8.3 %collective-permute-start.13 = (bf16[8,128,128]{2,1,0:T(8,128)(2,1)S(1)}, bf16[8,128,128]{2,1,0:T(8,128)(2,1)S(1)}, u32[]{:S(2)}, u32[]{:S(2)}) collective-permute-start(bf16[8,128,128]{2,1,0:T(8,128)(2,1)S(1)} %collective-permute-done.12.refs_14_), channel_id=1, source_target_pairs={{0,32},{32,0},{64,96},{96,64},{128,160},{160,128},{192,224},{224,1... | collective-permute-start | bytes 786440 | tf_op jit(solution)/shard_map/ppermute | solution.py:251
  31.6 8.0 %collective-permute-start.11 = (bf16[8,128,128]{2,1,0:T(8,128)(2,1)S(1)}, bf16[8,128,128]{2,1,0:T(8,128)(2,1)S(1)}, u32[]{:S(2)}, u32[]{:S(2)}) collective-permute-start(bf16[8,128,128]{2,1,0:T(8,128)(2,1)S(1)} %collective-permute-done.10.refs_12_), channel_id=1, source_target_pairs={{0,32},{32,0},{64,96},{96,64},{128,160},{160,128},{192,224},{224,1... | collective-permute-start | bytes 786440 | tf_op jit(solution)/shard_map/ppermute | solution.py:251
  31.6 15.1 %collective-permute-start.9 = (bf16[8,128,128]{2,1,0:T(8,128)(2,1)S(1)}, bf16[8,128,128]{2,1,0:T(8,128)(2,1)S(1)}, u32[]{:S(2)}, u32[]{:S(2)}) collective-permute-start(bf16[8,128,128]{2,1,0:T(8,128)(2,1)S(1)} %collective-permute-done.8.refs_10_), channel_id=1, source_target_pairs={{0,32},{32,0},{64,96},{96,64},{128,160},{160,128},{192,224},{224,1... | collective-permute-start | bytes 786440 | tf_op jit(solution)/shard_map/ppermute | solution.py:251
  34.9 8.2 %collective-permute-start.5 = (bf16[512,128]{1,0:T(8,128)(2,1)S(1)}, bf16[512,128]{1,0:T(8,128)(2,1)S(1)}, u32[]{:S(2)}, u32[]{:S(2)}) collective-permute-start(bf16[512,128]{1,0:T(8,128)(2,1)S(1)} %turn.1.refs_0_), channel_id=1, source_target_pairs={{0,192},{32,224},{64,128},{96,160},{128,64},{160,96},{192,0},{224,... | collective-permute-start | bytes 393224 | tf_op jit(solution)/shard_map/ppermute | solution.py:251
  37.4 7.4 %collective-permute-start.3 = (bf16[512,128]{1,0:T(8,128)(2,1)S(1)}, bf16[512,128]{1,0:T(8,128)(2,1)S(1)}, u32[]{:S(2)}, u32[]{:S(2)}) collective-permute-start(bf16[512,128]{1,0:T(8,128)(2,1)S(1)} %turn.1.refs_0_), channel_id=1, source_target_pairs={{0,128},{32,160},{64,192},{96,224},{128,0},{160,32},{192,64},{224,... | collective-permute-start | bytes 393224 | tf_op jit(solution)/shard_map/ppermute | solution.py:251
  38.0 8.7 %collective-permute-start.1 = (bf16[512,128]{1,0:T(8,128)(2,1)S(1)}, bf16[512,128]{1,0:T(8,128)(2,1)S(1)}, u32[]{:S(2)}, u32[]{:S(2)}) collective-permute-start(bf16[512,128]{1,0:T(8,128)(2,1)S(1)} %turn.1.refs_0_), channel_id=1, source_target_pairs={{0,64},{32,96},{64,0},{96,32},{128,192},{160,224},{192,128},{224,1... | collective-permute-start | bytes 393224 | tf_op jit(solution)/shard_map/ppermute | solution.py:251
  38.2 0.7 %copy-start.1 = (s32[40,128]{1,0:T(8,128)S(1)}, s32[40,128]{1,0:T(8,128)}, u32[]{:S(2)}) copy-start(s32[40,128]{1,0:T(8,128)} %get-tuple-element.10.info_ref) | copy-start | bytes 61444
  39.6 7.0 %collective-permute-start = (bf16[512,128]{1,0:T(8,128)(2,1)S(1)}, bf16[512,128]{1,0:T(8,128)(2,1)S(1)}, u32[]{:S(2)}, u32[]{:S(2)}) collective-permute-start(bf16[512,128]{1,0:T(8,128)(2,1)S(1)} %turn.1.refs_0_), channel_id=1, source_target_pairs={{0,32},{32,0},{64,96},{96,64},{128,160},{160,128},{192,224},{224,1... | collective-permute-start | bytes 393224 | tf_op jit(solution)/shard_map/ppermute | solution.py:251
  43.0 3.7 %collective-permute-start.6 = (bf16[512,128]{1,0:T(8,128)(2,1)S(1)}, bf16[512,128]{1,0:T(8,128)(2,1)S(1)}, u32[]{:S(2)}, u32[]{:S(2)}) collective-permute-start(bf16[512,128]{1,0:T(8,128)(2,1)S(1)} %collective-permute-done.5.refs_6_), channel_id=1, source_target_pairs={{0,32},{32,0},{64,96},{96,64},{128,160},{160,128},{192,224},{224,1... | collective-permute-start | bytes 393224 | tf_op jit(solution)/shard_map/ppermute | solution.py:251
  44.9 2.8 %collective-permute-start.4 = (bf16[512,128]{1,0:T(8,128)(2,1)S(1)}, bf16[512,128]{1,0:T(8,128)(2,1)S(1)}, u32[]{:S(2)}, u32[]{:S(2)}) collective-permute-start(bf16[512,128]{1,0:T(8,128)(2,1)S(1)} %collective-permute-done.3.refs_4_), channel_id=1, source_target_pairs={{0,32},{32,0},{64,96},{96,64},{128,160},{160,128},{192,224},{224,1... | collective-permute-start | bytes 393224 | tf_op jit(solution)/shard_map/ppermute | solution.py:251
  46.6 1.3 %collective-permute-start.2 = (bf16[512,128]{1,0:T(8,128)(2,1)S(1)}, bf16[512,128]{1,0:T(8,128)(2,1)S(1)}, u32[]{:S(2)}, u32[]{:S(2)}) collective-permute-start(bf16[512,128]{1,0:T(8,128)(2,1)S(1)} %collective-permute-done.1.refs_2_), channel_id=1, source_target_pairs={{0,32},{32,0},{64,96},{96,64},{128,160},{160,128},{192,224},{224,1... | collective-permute-start | bytes 393224 | tf_op jit(solution)/shard_map/ppermute | solution.py:251

commit v8 on v7

--- a/solution.py
+++ b/solution.py
@@ -222,23 +222,23 @@
         left = jnp.concatenate([jnp.where(group == j, radial_ref[g], zero) for j in range(4)], axis=0)
         result = lax.dot_general(left, right, (((1,), (1,)), ((), ())), preferred_element_type=F32)
         block_ref[:, g] = result.reshape(4, 64, 128).astype(BF16)
-        if g % 8 == 7:
+        if g % 4 == 3:
             for j in range(4):
-                first = g - 7
-                sem = sems.at[4 * (g // 8) + j]
+                first = g - 3
+                sem = sems.at[4 * (g // 4) + j]
                 row = (32 * j + first - start) & 127
 
-                @pl.when(row <= 120)
+                @pl.when(row <= 124)
                 def _(j=j, first=first, sem=sem, row=row):
-                    pltpu.make_async_copy(block_ref.at[j, pl.ds(first, 8)], out_ref.at[pl.ds(row, 8)], sem).start()
-
-                @pl.when(row > 120)
+                    pltpu.make_async_copy(block_ref.at[j, pl.ds(first, 4)], out_ref.at[pl.ds(row, 4)], sem).start()
+
+                @pl.when(row > 124)
                 def _(j=j, first=first, sem=sem, row=row):
-                    for i in range(8):
+                    for i in range(4):
                         pltpu.make_async_copy(block_ref.at[j, first + i], out_ref.at[(row + i) & 127], sem).start()
 
-    for i in range(16):
-        pltpu.make_async_copy(block_ref.at[0, pl.ds(0, 8)], out_ref.at[pl.ds(0, 8)], sems.at[i]).wait()
+    for i in range(32):
+        pltpu.make_async_copy(block_ref.at[0, pl.ds(0, 4)], out_ref.at[pl.ds(0, 4)], sems.at[i]).wait()
 
 
 def on_device(density, footprint, cycle_index, order_values, block_lengths, legendre, bessel):
@@ -277,9 +277,9 @@
     recv = lax.all_to_all(send, "radial", split_axis=0, concat_axis=0, tiled=True)
 
     row_pieces = {0: leg_rows, 1: swap(leg_rows, 1)}
-    for d in (4, 2, 6):
+    for d in (6, 2, 4):
         row_pieces[d] = swap(leg_rows, d)
-    for d in (4, 2, 6):
+    for d in (4, 6, 2):
         row_pieces[d + 1] = swap(row_pieces[d], 1)
 
     four = pl.pallas_call(
@@ -305,11 +305,11 @@
     )(info, recv)
 
     pieces = {0: four}
-    for d in (2, 6, 4):
+    for d in (6, 2, 4):
         pieces[d] = swap(four, d)
     own, radial = lax.optimization_barrier((four, radial))
     pieces[1] = swap(own, 1)
-    for d in (2, 6, 4):
+    for d in (4, 6, 2):
         pieces[d + 1] = swap(pieces[d], 1)
 
     return pl.pallas_call(
@@ -321,7 +321,7 @@
             pltpu.VMEM((32, 8, 16, 128), BF16),
             pltpu.VMEM((32 * 136, 128), F32),
             pltpu.VMEM((4, 32, modes, 128), BF16),
-            dma((16,)),
+            dma((32,)),
         ],
         compiler_params=params(),
         cost_estimate=cost(5, 1 << 22),

time: 51.2 us -> 51.2 us (level)
  no operation moved by 1% of the time
where the time goes in v8:
time: 51.2 us; the launch traced here: 50.9 us
  starting transfers between devices  30.2 us (59%)
  waiting for transfers between devices  12.4 us (24%)
  Pallas kernels  7.48 us (15%)
  local copies, waits for them, and re-layouts  0.73 us (1%)
    ppermute x14, starting transfers between devices, swap(): return lax.ppermute(x, 'shell', [(i, i ^ d) for i in range(8)])  18 us
    all_to_all x1, starting transfers between devices, on_device(): lax.all_to_all(send, 'radial', split_axis=0, concat_axis=0, tiled=True)  12.3 us
    ppermute x14, waiting for transfers between devices, swap(): return lax.ppermute(x, 'shell', [(i, i ^ d) for i in range(8)])  10.2 us
    pallas_call x1, Pallas kernels, on_device(): pl.pallas_call(front_kernel, out_shape=[shape((32, 16 + modes, 128), BF16...  3.43 us
    pallas_call x1, Pallas kernels, on_device(): pl.pallas_call(final_kernel, out_shape=shape((128, modes, 128), BF16), in...  2.95 us
    all_to_all x1, waiting for transfers between devices, on_device(): lax.all_to_all(send, 'radial', split_axis=0, concat_axis=0, tiled=True)  2.23 us
  transfers between devices with their start and end apart: 15, of which 4 were waited for; matrix products, arithmetic and copies ran while one was open for 0% of the time, Pallas kernels for 2%

profile of v8, /device:TPU:1, one launch (start us, length us, event | category | flops | bytes accessed | tf_op | source)
XLA Modules:
  0.0 50.9 jit_solution(10922327942701767968)
XLA Ops:
  0.0 3.4 %front.1 = (bf16[32,80,128]{2,1,0:T(8,128)(2,1)}, bf16[8,128,128]{2,1,0:T(8,128)(2,1)}, s32[40,128]{1,0:T(8,128)}) custom-call(s32[32]{0:T(128)} %lengths_hbm.1, s32[16]{0:T(128)} %cycle_hbm.1, s32[64]{0:T(128)} %order_hbm.1, f32[1,16,4096]{2,1,0:T(8,128)} %density_hbm.1, s32[1,16,4096]{2,1,0:T(8,128)} %footprint_hbm.1, bf16[64,2048]{1,0:T(8,128)(2,1)} %bitcast.3, ...), custom_call_target="tpu_custom_call" | custom-call | flops 2000000000 | bytes 2097152 | tf_op jit(solution)/shard_map/front/pallas_call | solution.py:253
  3.4 12.3 %all-to-all-start = ((bf16[32,80,128]{2,1,0:T(8,128)(2,1)}), bf16[32,80,128]{2,1,0:T(8,128)(2,1)S(1)}, u32[]{:S(2)}, u32[]{:S(2)}) async-start(bf16[32,80,128]{2,1,0:T(8,128)(2,1)} %get-tuple-element.11), calls=%async_computation | async-start | bytes 1310720 | tf_op jit(solution)/shard_map/all_to_all | solution.py:277
  15.7 2.6 %collective-permute-start.12 = (bf16[8,128,128]{2,1,0:T(8,128)(2,1)}, bf16[8,128,128]{2,1,0:T(8,128)(2,1)S(1)}, u32[]{:S(2)}, u32[]{:S(2)}) collective-permute-start(bf16[8,128,128]{2,1,0:T(8,128)(2,1)} %get-tuple-element.14.refs_8_), channel_id=1, source_target_pairs={{0,192},{32,224},{64,128},{96,160},{128,64},{160,96},{192,0},{224,... | collective-permute-start | bytes 786440 | tf_op jit(solution)/shard_map/ppermute | solution.py:251
  18.3 0.5 %collective-permute-start.10 = (bf16[8,128,128]{2,1,0:T(8,128)(2,1)}, bf16[8,128,128]{2,1,0:T(8,128)(2,1)S(1)}, u32[]{:S(2)}, u32[]{:S(2)}) collective-permute-start(bf16[8,128,128]{2,1,0:T(8,128)(2,1)} %get-tuple-element.14.refs_8_), channel_id=1, source_target_pairs={{0,128},{32,160},{64,192},{96,224},{128,0},{160,32},{192,64},{224,... | collective-permute-start | bytes 786440 | tf_op jit(solution)/shard_map/ppermute | solution.py:251
  18.8 0.3 collective-permute-start.8
  19.1 1.8 %collective-permute-start.7 = (bf16[8,128,128]{2,1,0:T(8,128)(2,1)}, bf16[8,128,128]{2,1,0:T(8,128)(2,1)S(1)}, u32[]{:S(2)}, u32[]{:S(2)}) collective-permute-start(bf16[8,128,128]{2,1,0:T(8,128)(2,1)} %get-tuple-element.14.refs_8_), channel_id=1, source_target_pairs={{0,32},{32,0},{64,96},{96,64},{128,160},{160,128},{192,224},{224,1... | collective-permute-start | bytes 786440 | tf_op jit(solution)/shard_map/ppermute | solution.py:251
  20.9 8.8 %collective-permute-done.12.refs_14_ = bf16[8,128,128]{2,1,0:T(8,128)(2,1)S(1)} collective-permute-done((bf16[8,128,128]{2,1,0:T(8,128)(2,1)}, bf16[8,128,128]{2,1,0:T(8,128)(2,1)S(1)}, u32[]{:S(2)}, u32[]{:S(2)}) %collective-permute-start.12) | collective-permute-done | bytes 262176 | tf_op jit(solution)/shard_map/ppermute | solution.py:251
  29.7 1.9 %collective-permute-start.13 = (bf16[8,128,128]{2,1,0:T(8,128)(2,1)S(1)}, bf16[8,128,128]{2,1,0:T(8,128)(2,1)S(1)}, u32[]{:S(2)}, u32[]{:S(2)}) collective-permute-start(bf16[8,128,128]{2,1,0:T(8,128)(2,1)S(1)} %collective-permute-done.12.refs_14_), channel_id=1, source_target_pairs={{0,32},{32,0},{64,96},{96,64},{128,160},{160,128},{192,224},{224,1... | collective-permute-start | bytes 786440 | tf_op jit(solution)/shard_map/ppermute | solution.py:251
  31.6 0.0 collective-permute-done.10.refs_12_
  31.6 0.0 collective-permute-start.11
  31.6 0.0 collective-permute-done.8.refs_10_
  31.6 0.6 %collective-permute-start.9 = (bf16[8,128,128]{2,1,0:T(8,128)(2,1)S(1)}, bf16[8,128,128]{2,1,0:T(8,128)(2,1)S(1)}, u32[]{:S(2)}, u32[]{:S(2)}) collective-permute-start(bf16[8,128,128]{2,1,0:T(8,128)(2,1)S(1)} %collective-permute-done.8.refs_10_), channel_id=1, source_target_pairs={{0,32},{32,0},{64,96},{96,64},{128,160},{160,128},{192,224},{224,1... | collective-permute-start | bytes 786440 | tf_op jit(solution)/shard_map/ppermute | solution.py:251
  32.2 2.2 %all-to-all-done.recv_ref = bf16[32,80,128]{2,1,0:T(8,128)(2,1)S(1)} async-done(((bf16[32,80,128]{2,1,0:T(8,128)(2,1)}), bf16[32,80,128]{2,1,0:T(8,128)(2,1)S(1)}, u32[]{:S(2)}, u32[]{:S(2)}) %all-to-all-start) | async-done | bytes 655392 | tf_op jit(solution)/shard_map/all_to_all | solution.py:277
  34.4 0.4 turn.1.refs_0_
  34.9 2.6 %collective-permute-start.5 = (bf16[512,128]{1,0:T(8,128)(2,1)S(1)}, bf16[512,128]{1,0:T(8,128)(2,1)S(1)}, u32[]{:S(2)}, u32[]{:S(2)}) collective-permute-start(bf16[512,128]{1,0:T(8,128)(2,1)S(1)} %turn.1.refs_0_), channel_id=1, source_target_pairs={{0,192},{32,224},{64,128},{96,160},{128,64},{160,96},{192,0},{224,... | collective-permute-start | bytes 393224 | tf_op jit(solution)/shard_map/ppermute | solution.py:251
  37.4 0.0 collective-permute-done.7.refs_9_
  37.4 0.5 %collective-permute-start.3 = (bf16[512,128]{1,0:T(8,128)(2,1)S(1)}, bf16[512,128]{1,0:T(8,128)(2,1)S(1)}, u32[]{:S(2)}, u32[]{:S(2)}) collective-permute-start(bf16[512,128]{1,0:T(8,128)(2,1)S(1)} %turn.1.refs_0_), channel_id=1, source_target_pairs={{0,128},{32,160},{64,192},{96,224},{128,0},{160,32},{192,64},{224,... | collective-permute-start | bytes 393224 | tf_op jit(solution)/shard_map/ppermute | solution.py:251
  38.0 0.0 collective-permute-done.13.refs_15_
  38.0 0.3 collective-permute-start.1
  38.2 0.7 %copy-done.1 = s32[40,128]{1,0:T(8,128)S(1)} copy-done((s32[40,128]{1,0:T(8,128)S(1)}, s32[40,128]{1,0:T(8,128)}, u32[]{:S(2)}) %copy-start.1) | copy-done | bytes 20504
  38.9 0.7 %radial_rows.1.radial_ref = bf16[32,64,128]{2,1,0:T(8,128)(2,1)S(1)} custom-call(s32[40,128]{1,0:T(8,128)S(1)} %copy-done.1, bf16[32,80,128]{2,1,0:T(8,128)(2,1)S(1)} %all-to-all-done.recv_ref), custom_call_target="tpu_custom_call" | custom-call | flops 1500000000 | bytes 1048576 | tf_op jit(solution)/shard_map/radial_rows/pallas_call | solution.py:296
  39.6 0.0 collective-permute-done.11.refs_13_
  39.6 3.4 %collective-permute-start = (bf16[512,128]{1,0:T(8,128)(2,1)S(1)}, bf16[512,128]{1,0:T(8,128)(2,1)S(1)}, u32[]{:S(2)}, u32[]{:S(2)}) collective-permute-start(bf16[512,128]{1,0:T(8,128)(2,1)S(1)} %turn.1.refs_0_), channel_id=1, source_target_pairs={{0,32},{32,0},{64,96},{96,64},{128,160},{160,128},{192,224},{224,1... | collective-permute-start | bytes 393224 | tf_op jit(solution)/shard_map/ppermute | solution.py:251
  43.0 1.8 %collective-permute-start.6 = (bf16[512,128]{1,0:T(8,128)(2,1)S(1)}, bf16[512,128]{1,0:T(8,128)(2,1)S(1)}, u32[]{:S(2)}, u32[]{:S(2)}) collective-permute-start(bf16[512,128]{1,0:T(8,128)(2,1)S(1)} %collective-permute-done.5.refs_6_), channel_id=1, source_target_pairs={{0,32},{32,0},{64,96},{96,64},{128,160},{160,128},{192,224},{224,1... | collective-permute-start | bytes 393224 | tf_op jit(solution)/shard_map/ppermute | solution.py:251
  44.8 0.0 collective-permute-done.3.refs_4_
  44.9 1.8 %collective-permute-start.4 = (bf16[512,128]{1,0:T(8,128)(2,1)S(1)}, bf16[512,128]{1,0:T(8,128)(2,1)S(1)}, u32[]{:S(2)}, u32[]{:S(2)}) collective-permute-start(bf16[512,128]{1,0:T(8,128)(2,1)S(1)} %collective-permute-done.3.refs_4_), channel_id=1, source_target_pairs={{0,32},{32,0},{64,96},{96,64},{128,160},{160,128},{192,224},{224,1... | collective-permute-start | bytes 393224 | tf_op jit(solution)/shard_map/ppermute | solution.py:251
  46.6 0.0 collective-permute-done.1.refs_2_
  46.6 0.0 collective-permute-start.2
  46.6 0.0 collective-permute-done.9.refs_11_
  46.7 1.0 %collective-permute-done.4.refs_5_ = bf16[512,128]{1,0:T(8,128)(2,1)S(1)} collective-permute-done((bf16[512,128]{1,0:T(8,128)(2,1)S(1)}, bf16[512,128]{1,0:T(8,128)(2,1)S(1)}, u32[]{:S(2)}, u32[]{:S(2)}) %collective-permute-start.4) | collective-permute-done | bytes 131104 | tf_op jit(solution)/shard_map/ppermute | solution.py:251
  47.6 0.4 collective-permute-done.2.refs_3_
  48.0 3.0 %finish.1 = bf16[128,64,128]{2,1,0:T(8,128)(2,1)} custom-call(s32[40,128]{1,0:T(8,128)S(1)} %copy-done.1, bf16[32,64,128]{2,1,0:T(8,128)(2,1)S(1)} %radial_rows.1.radial_ref, bf16[512,128]{1,0:T(8,128)(2,1)S(1)} %turn.1.refs_0_, bf16[512,128]{1,0:T(8,128)(2,1)S(1)} %collective-permute-done.refs_1_, bf16[512,128]{1,0:T(8,128)(2,1)S(1)} %collective-permute-done.1.refs_2_, ...), custom_call_target="tpu_custom_call" | custom-call | flops 2500000000 | bytes 4194304 | tf_op jit(solution)/shard_map/finish/pallas_call | solution.py:315
  (6 shorter events, 0.0 us)
Async XLA Ops:
  3.4 44.6 %copy-start = (bf16[8,128,128]{2,1,0:T(8,128)(2,1)S(1)}, bf16[8,128,128]{2,1,0:T(8,128)(2,1)}, u32[]{:S(2)}) copy-start(bf16[8,128,128]{2,1,0:T(8,128)(2,1)} %get-tuple-element.14.refs_8_) | copy-start | bytes 786436
  3.4 31.0 %all-to-all-start = ((bf16[32,80,128]{2,1,0:T(8,128)(2,1)}), bf16[32,80,128]{2,1,0:T(8,128)(2,1)S(1)}, u32[]{:S(2)}, u32[]{:S(2)}) async-start(bf16[32,80,128]{2,1,0:T(8,128)(2,1)} %get-tuple-element.11), calls=%async_computation | async-start | bytes 1310720 | tf_op jit(solution)/shard_map/all_to_all | solution.py:277
  15.7 14.0 %collective-permute-start.12 = (bf16[8,128,128]{2,1,0:T(8,128)(2,1)}, bf16[8,128,128]{2,1,0:T(8,128)(2,1)S(1)}, u32[]{:S(2)}, u32[]{:S(2)}) collective-permute-start(bf16[8,128,128]{2,1,0:T(8,128)(2,1)} %get-tuple-element.14.refs_8_), channel_id=1, source_target_pairs={{0,192},{32,224},{64,128},{96,160},{128,64},{160,96},{192,0},{224,... | collective-permute-start | bytes 786440 | tf_op jit(solution)/shard_map/ppermute | solution.py:251
  18.3 13.3 %collective-permute-start.10 = (bf16[8,128,128]{2,1,0:T(8,128)(2,1)}, bf16[8,128,128]{2,1,0:T(8,128)(2,1)S(1)}, u32[]{:S(2)}, u32[]{:S(2)}) collective-permute-start(bf16[8,128,128]{2,1,0:T(8,128)(2,1)} %get-tuple-element.14.refs_8_), channel_id=1, source_target_pairs={{0,128},{32,160},{64,192},{96,224},{128,0},{160,32},{192,64},{224,... | collective-permute-start | bytes 786440 | tf_op jit(solution)/shard_map/ppermute | solution.py:251
  18.8 12.8 %collective-permute-start.8 = (bf16[8,128,128]{2,1,0:T(8,128)(2,1)}, bf16[8,128,128]{2,1,0:T(8,128)(2,1)S(1)}, u32[]{:S(2)}, u32[]{:S(2)}) collective-permute-start(bf16[8,128,128]{2,1,0:T(8,128)(2,1)} %get-tuple-element.14.refs_8_), channel_id=1, source_target_pairs={{0,64},{32,96},{64,0},{96,32},{128,192},{160,224},{192,128},{224,1... | collective-permute-start | bytes 786440 | tf_op jit(solution)/shard_map/ppermute | solution.py:251
  19.1 18.4 %collective-permute-start.7 = (bf16[8,128,128]{2,1,0:T(8,128)(2,1)}, bf16[8,128,128]{2,1,0:T(8,128)(2,1)S(1)}, u32[]{:S(2)}, u32[]{:S(2)}) collective-permute-start(bf16[8,128,128]{2,1,0:T(8,128)(2,1)} %get-tuple-element.14.refs_8_), channel_id=1, source_target_pairs={{0,32},{32,0},{64,96},{96,64},{128,160},{160,128},{192,224},{224,1... | collective-permute-start | bytes 786440 | tf_op jit(solution)/shard_map/ppermute | solution.py:251
  29.7 8.3 %collective-permute-start.13 = (bf16[8,128,128]{2,1,0:T(8,128)(2,1)S(1)}, bf16[8,128,128]{2,1,0:T(8,128)(2,1)S(1)}, u32[]{:S(2)}, u32[]{:S(2)}) collective-permute-start(bf16[8,128,128]{2,1,0:T(8,128)(2,1)S(1)} %collective-permute-done.12.refs_14_), channel_id=1, source_target_pairs={{0,32},{32,0},{64,96},{96,64},{128,160},{160,128},{192,224},{224,1... | collective-permute-start | bytes 786440 | tf_op jit(solution)/shard_map/ppermute | solution.py:251
  31.6 8.0 %collective-permute-start.11 = (bf16[8,128,128]{2,1,0:T(8,128)(2,1)S(1)}, bf16[8,128,128]{2,1,0:T(8,128)(2,1)S(1)}, u32[]{:S(2)}, u32[]{:S(2)}) collective-permute-start(bf16[8,128,128]{2,1,0:T(8,128)(2,1)S(1)} %collective-permute-done.10.refs_12_), channel_id=1, source_target_pairs={{0,32},{32,0},{64,96},{96,64},{128,160},{160,128},{192,224},{224,1... | collective-permute-start | bytes 786440 | tf_op jit(solution)/shard_map/ppermute | solution.py:251
  31.6 15.1 %collective-permute-start.9 = (bf16[8,128,128]{2,1,0:T(8,128)(2,1)S(1)}, bf16[8,128,128]{2,1,0:T(8,128)(2,1)S(1)}, u32[]{:S(2)}, u32[]{:S(2)}) collective-permute-start(bf16[8,128,128]{2,1,0:T(8,128)(2,1)S(1)} %collective-permute-done.8.refs_10_), channel_id=1, source_target_pairs={{0,32},{32,0},{64,96},{96,64},{128,160},{160,128},{192,224},{224,1... | collective-permute-start | bytes 786440 | tf_op jit(solution)/shard_map/ppermute | solution.py:251
  34.9 8.2 %collective-permute-start.5 = (bf16[512,128]{1,0:T(8,128)(2,1)S(1)}, bf16[512,128]{1,0:T(8,128)(2,1)S(1)}, u32[]{:S(2)}, u32[]{:S(2)}) collective-permute-start(bf16[512,128]{1,0:T(8,128)(2,1)S(1)} %turn.1.refs_0_), channel_id=1, source_target_pairs={{0,192},{32,224},{64,128},{96,160},{128,64},{160,96},{192,0},{224,... | collective-permute-start | bytes 393224 | tf_op jit(solution)/shard_map/ppermute | solution.py:251
  37.4 7.4 %collective-permute-start.3 = (bf16[512,128]{1,0:T(8,128)(2,1)S(1)}, bf16[512,128]{1,0:T(8,128)(2,1)S(1)}, u32[]{:S(2)}, u32[]{:S(2)}) collective-permute-start(bf16[512,128]{1,0:T(8,128)(2,1)S(1)} %turn.1.refs_0_), channel_id=1, source_target_pairs={{0,128},{32,160},{64,192},{96,224},{128,0},{160,32},{192,64},{224,... | collective-permute-start | bytes 393224 | tf_op jit(solution)/shard_map/ppermute | solution.py:251
  38.0 8.7 %collective-permute-start.1 = (bf16[512,128]{1,0:T(8,128)(2,1)S(1)}, bf16[512,128]{1,0:T(8,128)(2,1)S(1)}, u32[]{:S(2)}, u32[]{:S(2)}) collective-permute-start(bf16[512,128]{1,0:T(8,128)(2,1)S(1)} %turn.1.refs_0_), channel_id=1, source_target_pairs={{0,64},{32,96},{64,0},{96,32},{128,192},{160,224},{192,128},{224,1... | collective-permute-start | bytes 393224 | tf_op jit(solution)/shard_map/ppermute | solution.py:251
  38.2 0.7 %copy-start.1 = (s32[40,128]{1,0:T(8,128)S(1)}, s32[40,128]{1,0:T(8,128)}, u32[]{:S(2)}) copy-start(s32[40,128]{1,0:T(8,128)} %get-tuple-element.10.info_ref) | copy-start | bytes 61444
  39.6 7.0 %collective-permute-start = (bf16[512,128]{1,0:T(8,128)(2,1)S(1)}, bf16[512,128]{1,0:T(8,128)(2,1)S(1)}, u32[]{:S(2)}, u32[]{:S(2)}) collective-permute-start(bf16[512,128]{1,0:T(8,128)(2,1)S(1)} %turn.1.refs_0_), channel_id=1, source_target_pairs={{0,32},{32,0},{64,96},{96,64},{128,160},{160,128},{192,224},{224,1... | collective-permute-start | bytes 393224 | tf_op jit(solution)/shard_map/ppermute | solution.py:251
  43.0 3.7 %collective-permute-start.6 = (bf16[512,128]{1,0:T(8,128)(2,1)S(1)}, bf16[512,128]{1,0:T(8,128)(2,1)S(1)}, u32[]{:S(2)}, u32[]{:S(2)}) collective-permute-start(bf16[512,128]{1,0:T(8,128)(2,1)S(1)} %collective-permute-done.5.refs_6_), channel_id=1, source_target_pairs={{0,32},{32,0},{64,96},{96,64},{128,160},{160,128},{192,224},{224,1... | collective-permute-start | bytes 393224 | tf_op jit(solution)/shard_map/ppermute | solution.py:251
  44.9 2.8 %collective-permute-start.4 = (bf16[512,128]{1,0:T(8,128)(2,1)S(1)}, bf16[512,128]{1,0:T(8,128)(2,1)S(1)}, u32[]{:S(2)}, u32[]{:S(2)}) collective-permute-start(bf16[512,128]{1,0:T(8,128)(2,1)S(1)} %collective-permute-done.3.refs_4_), channel_id=1, source_target_pairs={{0,32},{32,0},{64,96},{96,64},{128,160},{160,128},{192,224},{224,1... | collective-permute-start | bytes 393224 | tf_op jit(solution)/shard_map/ppermute | solution.py:251
  46.6 1.3 %collective-permute-start.2 = (bf16[512,128]{1,0:T(8,128)(2,1)S(1)}, bf16[512,128]{1,0:T(8,128)(2,1)S(1)}, u32[]{:S(2)}, u32[]{:S(2)}) collective-permute-start(bf16[512,128]{1,0:T(8,128)(2,1)S(1)} %collective-permute-done.1.refs_2_), channel_id=1, source_target_pairs={{0,32},{32,0},{64,96},{96,64},{128,160},{160,128},{192,224},{224,1... | collective-permute-start | bytes 393224 | tf_op jit(solution)/shard_map/ppermute | solution.py:251

commit v9 on v7

--- a/solution.py
+++ b/solution.py
@@ -173,17 +173,12 @@
     return lax.fori_loop(0, lax.axis_index("radial"), lambda k, total: total + lengths_ref[k], jnp.int32(0))
 
 
-def radial_kernel(info_ref, recv_ref, out_ref, wide_ref, turned_ref):
+def radial_kernel(recv_ref, out_ref, wide_ref, turned_ref):
     for s in range(32):
         wide_ref[72 * s : 72 * s + 64, :] = recv_ref[s, 16:].astype(F32)
-    lane = lax.broadcasted_iota(jnp.int32, (128, 128), 1)
-    row = lax.broadcasted_iota(jnp.int32, (128, 128), 0)
-    slot = 32 * (row >> 5) + (lane & 31)
-    keep = ((slot - info_ref[32:33]) & 127) < info_ref[33:34]
-
     def step(a, carry):
         x = jnp.concatenate([wide_ref[pl.ds(16 * j + a, 32, stride=72), :] for j in range(4)], axis=0)
-        turned = jnp.transpose(jnp.where(keep, x, 0.0))
+        turned = jnp.transpose(x)
         for m in range(4):
             turned_ref[pl.ds(16 * m + a, 32, stride=72), :] = turned[32 * m : 32 * m + 32]
         return carry
@@ -219,7 +214,9 @@
     zero = jnp.zeros((64, 128), BF16)
     for g in range(32):
         right = harmonic_ref[136 * g : 136 * g + 128, :].astype(BF16)
-        left = jnp.concatenate([jnp.where(group == j, radial_ref[g], zero) for j in range(4)], axis=0)
+        slot = 32 * group + g
+        filled = jnp.where(((slot - info_ref[32:33]) & 127) < info_ref[33:34], radial_ref[g], zero)
+        left = jnp.concatenate([jnp.where(group == j, filled, zero) for j in range(4)], axis=0)
         result = lax.dot_general(left, right, (((1,), (1,)), ((), ())), preferred_element_type=F32)
         block_ref[:, g] = result.reshape(4, 64, 128).astype(BF16)
         if g % 8 == 7:
@@ -296,13 +293,13 @@
     radial = pl.pallas_call(
         radial_kernel,
         out_shape=shape((32, modes, 128), BF16),
-        in_specs=[VMEM_SPEC] * 2,
+        in_specs=[VMEM_SPEC],
         out_specs=VMEM_SPEC,
         scratch_shapes=[pltpu.VMEM((32 * 72, 128), F32)] * 2,
         compiler_params=params(),
         cost_estimate=cost(3, 1 << 20),
         name="radial_rows",
-    )(info, recv)
+    )(recv)
 
     pieces = {0: four}
     for d in (2, 6, 4):

time: 51.2 us -> 51.2 us (level)
  starting transfers between devices: 30.2 us -> 31 us
  local copies, waits for them, and re-layouts: 0.73 us -> 0.01 us
    ppermute x14, starting transfers between devices: 18 us -> 18.7 us  [swap(): return lax.ppermute(x, 'shell', [(i, i ^ d) for i in range(8)])]
    unnamed x4, local copies, waits for them, and re-layouts: 0.73 us -> 0.01 us
where the time goes in v9:
time: 51.2 us; the launch traced here: 50.9 us
  starting transfers between devices  31 us (61%)
  waiting for transfers between devices  12.4 us (24%)
  Pallas kernels  7.45 us (15%)
    ppermute x14, starting transfers between devices, swap(): return lax.ppermute(x, 'shell', [(i, i ^ d) for i in range(8)])  18.7 us
    all_to_all x1, starting transfers between devices, on_device(): lax.all_to_all(send, 'radial', split_axis=0, concat_axis=0, tiled=True)  12.3 us
    ppermute x14, waiting for transfers between devices, swap(): return lax.ppermute(x, 'shell', [(i, i ^ d) for i in range(8)])  10.2 us
    pallas_call x1, Pallas kernels, on_device(): pl.pallas_call(front_kernel, out_shape=[shape((32, 16 + modes, 128), BF16...  3.43 us
    pallas_call x1, Pallas kernels, on_device(): pl.pallas_call(final_kernel, out_shape=shape((128, modes, 128), BF16), in...  2.93 us
    all_to_all x1, waiting for transfers between devices, on_device(): lax.all_to_all(send, 'radial', split_axis=0, concat_axis=0, tiled=True)  2.23 us
  transfers between devices with their start and end apart: 15, of which 4 were waited for; matrix products, arithmetic and copies ran while one was open for 0% of the time, Pallas kernels for 2%

profile of v9, /device:TPU:1, one launch (start us, length us, event | category | flops | bytes accessed | tf_op | source)
XLA Modules:
  0.0 50.9 jit_solution(5843442743325358703)
XLA Ops:
  0.0 3.4 %front.1 = (bf16[32,80,128]{2,1,0:T(8,128)(2,1)}, bf16[8,128,128]{2,1,0:T(8,128)(2,1)}, s32[40,128]{1,0:T(8,128)}) custom-call(s32[32]{0:T(128)} %lengths_hbm.1, s32[16]{0:T(128)} %cycle_hbm.1, s32[64]{0:T(128)} %order_hbm.1, f32[1,16,4096]{2,1,0:T(8,128)} %density_hbm.1, s32[1,16,4096]{2,1,0:T(8,128)} %footprint_hbm.1, bf16[64,2048]{1,0:T(8,128)(2,1)} %bitcast.3, ...), custom_call_target="tpu_custom_call" | custom-call | flops 2000000000 | bytes 2097152 | tf_op jit(solution)/shard_map/front/pallas_call | solution.py:250
  3.5 12.3 %all-to-all-start = ((bf16[32,80,128]{2,1,0:T(8,128)(2,1)}), bf16[32,80,128]{2,1,0:T(8,128)(2,1)S(1)}, u32[]{:S(2)}, u32[]{:S(2)}) async-start(bf16[32,80,128]{2,1,0:T(8,128)(2,1)} %get-tuple-element.11), calls=%async_computation | async-start | bytes 1310720 | tf_op jit(solution)/shard_map/all_to_all | solution.py:274
  15.7 2.6 %collective-permute-start.12 = (bf16[8,128,128]{2,1,0:T(8,128)(2,1)}, bf16[8,128,128]{2,1,0:T(8,128)(2,1)S(1)}, u32[]{:S(2)}, u32[]{:S(2)}) collective-permute-start(bf16[8,128,128]{2,1,0:T(8,128)(2,1)} %get-tuple-element.14.refs_8_), channel_id=1, source_target_pairs={{0,192},{32,224},{64,128},{96,160},{128,64},{160,96},{192,0},{224,... | collective-permute-start | bytes 786440 | tf_op jit(solution)/shard_map/ppermute | solution.py:248
  18.3 0.5 %collective-permute-start.10 = (bf16[8,128,128]{2,1,0:T(8,128)(2,1)}, bf16[8,128,128]{2,1,0:T(8,128)(2,1)S(1)}, u32[]{:S(2)}, u32[]{:S(2)}) collective-permute-start(bf16[8,128,128]{2,1,0:T(8,128)(2,1)} %get-tuple-element.14.refs_8_), channel_id=1, source_target_pairs={{0,128},{32,160},{64,192},{96,224},{128,0},{160,32},{192,64},{224,... | collective-permute-start | bytes 786440 | tf_op jit(solution)/shard_map/ppermute | solution.py:248
  18.8 0.3 collective-permute-start.8
  19.1 1.8 %collective-permute-start.7 = (bf16[8,128,128]{2,1,0:T(8,128)(2,1)}, bf16[8,128,128]{2,1,0:T(8,128)(2,1)S(1)}, u32[]{:S(2)}, u32[]{:S(2)}) collective-permute-start(bf16[8,128,128]{2,1,0:T(8,128)(2,1)} %get-tuple-element.14.refs_8_), channel_id=1, source_target_pairs={{0,32},{32,0},{64,96},{96,64},{128,160},{160,128},{192,224},{224,1... | collective-permute-start | bytes 786440 | tf_op jit(solution)/shard_map/ppermute | solution.py:248
  20.9 8.8 %collective-permute-done.12.refs_14_ = bf16[8,128,128]{2,1,0:T(8,128)(2,1)S(1)} collective-permute-done((bf16[8,128,128]{2,1,0:T(8,128)(2,1)}, bf16[8,128,128]{2,1,0:T(8,128)(2,1)S(1)}, u32[]{:S(2)}, u32[]{:S(2)}) %collective-permute-start.12) | collective-permute-done | bytes 262176 | tf_op jit(solution)/shard_map/ppermute | solution.py:248
  29.7 1.9 %collective-permute-start.13 = (bf16[8,128,128]{2,1,0:T(8,128)(2,1)S(1)}, bf16[8,128,128]{2,1,0:T(8,128)(2,1)S(1)}, u32[]{:S(2)}, u32[]{:S(2)}) collective-permute-start(bf16[8,128,128]{2,1,0:T(8,128)(2,1)S(1)} %collective-permute-done.12.refs_14_), channel_id=1, source_target_pairs={{0,32},{32,0},{64,96},{96,64},{128,160},{160,128},{192,224},{224,1... | collective-permute-start | bytes 786440 | tf_op jit(solution)/shard_map/ppermute | solution.py:248
  31.6 0.0 collective-permute-done.10.refs_12_
  31.6 0.0 collective-permute-start.11
  31.6 0.0 collective-permute-done.8.refs_10_
  31.6 0.6 %collective-permute-start.9 = (bf16[8,128,128]{2,1,0:T(8,128)(2,1)S(1)}, bf16[8,128,128]{2,1,0:T(8,128)(2,1)S(1)}, u32[]{:S(2)}, u32[]{:S(2)}) collective-permute-start(bf16[8,128,128]{2,1,0:T(8,128)(2,1)S(1)} %collective-permute-done.8.refs_10_), channel_id=1, source_target_pairs={{0,32},{32,0},{64,96},{96,64},{128,160},{160,128},{192,224},{224,1... | collective-permute-start | bytes 786440 | tf_op jit(solution)/shard_map/ppermute | solution.py:248
  32.2 2.2 %all-to-all-done.recv_ref = bf16[32,80,128]{2,1,0:T(8,128)(2,1)S(1)} async-done(((bf16[32,80,128]{2,1,0:T(8,128)(2,1)}), bf16[32,80,128]{2,1,0:T(8,128)(2,1)S(1)}, u32[]{:S(2)}, u32[]{:S(2)}) %all-to-all-start) | async-done | bytes 655392 | tf_op jit(solution)/shard_map/all_to_all | solution.py:274
  34.4 0.4 turn.1.refs_0_
  34.9 2.6 %collective-permute-start.5 = (bf16[512,128]{1,0:T(8,128)(2,1)S(1)}, bf16[512,128]{1,0:T(8,128)(2,1)S(1)}, u32[]{:S(2)}, u32[]{:S(2)}) collective-permute-start(bf16[512,128]{1,0:T(8,128)(2,1)S(1)} %turn.1.refs_0_), channel_id=1, source_target_pairs={{0,192},{32,224},{64,128},{96,160},{128,64},{160,96},{192,0},{224,... | collective-permute-start | bytes 393224 | tf_op jit(solution)/shard_map/ppermute | solution.py:248
  37.4 0.0 collective-permute-done.7.refs_9_
  37.4 0.5 %collective-permute-start.3 = (bf16[512,128]{1,0:T(8,128)(2,1)S(1)}, bf16[512,128]{1,0:T(8,128)(2,1)S(1)}, u32[]{:S(2)}, u32[]{:S(2)}) collective-permute-start(bf16[512,128]{1,0:T(8,128)(2,1)S(1)} %turn.1.refs_0_), channel_id=1, source_target_pairs={{0,128},{32,160},{64,192},{96,224},{128,0},{160,32},{192,64},{224,... | collective-permute-start | bytes 393224 | tf_op jit(solution)/shard_map/ppermute | solution.py:248
  38.0 0.0 collective-permute-done.13.refs_15_
  38.0 0.3 collective-permute-start.1
  38.2 0.7 %radial_rows.1.radial_ref = bf16[32,64,128]{2,1,0:T(8,128)(2,1)S(1)} custom-call(bf16[32,80,128]{2,1,0:T(8,128)(2,1)S(1)} %all-to-all-done.recv_ref), custom_call_target="tpu_custom_call" | custom-call | flops 1500000000 | bytes 1048576 | tf_op jit(solution)/shard_map/radial_rows/pallas_call | solution.py:293
  38.9 0.0 collective-permute-done.11.refs_13_
  38.9 3.4 %collective-permute-start = (bf16[512,128]{1,0:T(8,128)(2,1)S(1)}, bf16[512,128]{1,0:T(8,128)(2,1)S(1)}, u32[]{:S(2)}, u32[]{:S(2)}) collective-permute-start(bf16[512,128]{1,0:T(8,128)(2,1)S(1)} %turn.1.refs_0_), channel_id=1, source_target_pairs={{0,32},{32,0},{64,96},{96,64},{128,160},{160,128},{192,224},{224,1... | collective-permute-start | bytes 393224 | tf_op jit(solution)/shard_map/ppermute | solution.py:248
  42.3 2.6 %collective-permute-start.6 = (bf16[512,128]{1,0:T(8,128)(2,1)S(1)}, bf16[512,128]{1,0:T(8,128)(2,1)S(1)}, u32[]{:S(2)}, u32[]{:S(2)}) collective-permute-start(bf16[512,128]{1,0:T(8,128)(2,1)S(1)} %collective-permute-done.5.refs_6_), channel_id=1, source_target_pairs={{0,32},{32,0},{64,96},{96,64},{128,160},{160,128},{192,224},{224,1... | collective-permute-start | bytes 393224 | tf_op jit(solution)/shard_map/ppermute | solution.py:248
  44.9 0.0 collective-permute-done.3.refs_4_
  44.9 1.8 %collective-permute-start.4 = (bf16[512,128]{1,0:T(8,128)(2,1)S(1)}, bf16[512,128]{1,0:T(8,128)(2,1)S(1)}, u32[]{:S(2)}, u32[]{:S(2)}) collective-permute-start(bf16[512,128]{1,0:T(8,128)(2,1)S(1)} %collective-permute-done.3.refs_4_), channel_id=1, source_target_pairs={{0,32},{32,0},{64,96},{96,64},{128,160},{160,128},{192,224},{224,1... | collective-permute-start | bytes 393224 | tf_op jit(solution)/shard_map/ppermute | solution.py:248
  46.7 0.0 collective-permute-done.1.refs_2_
  46.7 0.0 collective-permute-start.2
  46.7 0.0 collective-permute-done.9.refs_11_
  46.7 0.0 collective-permute-done.refs_1_
  46.7 1.0 %collective-permute-done.4.refs_5_ = bf16[512,128]{1,0:T(8,128)(2,1)S(1)} collective-permute-done((bf16[512,128]{1,0:T(8,128)(2,1)S(1)}, bf16[512,128]{1,0:T(8,128)(2,1)S(1)}, u32[]{:S(2)}, u32[]{:S(2)}) %collective-permute-start.4) | collective-permute-done | bytes 131104 | tf_op jit(solution)/shard_map/ppermute | solution.py:248
  47.6 0.4 collective-permute-done.2.refs_3_
  48.0 2.9 %finish.1 = bf16[128,64,128]{2,1,0:T(8,128)(2,1)} custom-call(s32[40,128]{1,0:T(8,128)S(1)} %copy-done.1, bf16[32,64,128]{2,1,0:T(8,128)(2,1)S(1)} %radial_rows.1.radial_ref, bf16[512,128]{1,0:T(8,128)(2,1)S(1)} %turn.1.refs_0_, bf16[512,128]{1,0:T(8,128)(2,1)S(1)} %collective-permute-done.refs_1_, bf16[512,128]{1,0:T(8,128)(2,1)S(1)} %collective-permute-done.1.refs_2_, ...), custom_call_target="tpu_custom_call" | custom-call | flops 2500000000 | bytes 4194304 | tf_op jit(solution)/shard_map/finish/pallas_call | solution.py:312
  (6 shorter events, 0.0 us)
Async XLA Ops:
  3.4 44.6 %copy-start = (bf16[8,128,128]{2,1,0:T(8,128)(2,1)S(1)}, bf16[8,128,128]{2,1,0:T(8,128)(2,1)}, u32[]{:S(2)}) copy-start(bf16[8,128,128]{2,1,0:T(8,128)(2,1)} %get-tuple-element.14.refs_8_) | copy-start | bytes 786436
  3.4 44.6 %copy-start.1 = (s32[40,128]{1,0:T(8,128)S(1)}, s32[40,128]{1,0:T(8,128)}, u32[]{:S(2)}) copy-start(s32[40,128]{1,0:T(8,128)} %get-tuple-element.10.info_ref) | copy-start | bytes 61444
  3.5 31.0 %all-to-all-start = ((bf16[32,80,128]{2,1,0:T(8,128)(2,1)}), bf16[32,80,128]{2,1,0:T(8,128)(2,1)S(1)}, u32[]{:S(2)}, u32[]{:S(2)}) async-start(bf16[32,80,128]{2,1,0:T(8,128)(2,1)} %get-tuple-element.11), calls=%async_computation | async-start | bytes 1310720 | tf_op jit(solution)/shard_map/all_to_all | solution.py:274
  15.7 14.0 %collective-permute-start.12 = (bf16[8,128,128]{2,1,0:T(8,128)(2,1)}, bf16[8,128,128]{2,1,0:T(8,128)(2,1)S(1)}, u32[]{:S(2)}, u32[]{:S(2)}) collective-permute-start(bf16[8,128,128]{2,1,0:T(8,128)(2,1)} %get-tuple-element.14.refs_8_), channel_id=1, source_target_pairs={{0,192},{32,224},{64,128},{96,160},{128,64},{160,96},{192,0},{224,... | collective-permute-start | bytes 786440 | tf_op jit(solution)/shard_map/ppermute | solution.py:248
  18.3 13.3 %collective-permute-start.10 = (bf16[8,128,128]{2,1,0:T(8,128)(2,1)}, bf16[8,128,128]{2,1,0:T(8,128)(2,1)S(1)}, u32[]{:S(2)}, u32[]{:S(2)}) collective-permute-start(bf16[8,128,128]{2,1,0:T(8,128)(2,1)} %get-tuple-element.14.refs_8_), channel_id=1, source_target_pairs={{0,128},{32,160},{64,192},{96,224},{128,0},{160,32},{192,64},{224,... | collective-permute-start | bytes 786440 | tf_op jit(solution)/shard_map/ppermute | solution.py:248
  18.8 12.8 %collective-permute-start.8 = (bf16[8,128,128]{2,1,0:T(8,128)(2,1)}, bf16[8,128,128]{2,1,0:T(8,128)(2,1)S(1)}, u32[]{:S(2)}, u32[]{:S(2)}) collective-permute-start(bf16[8,128,128]{2,1,0:T(8,128)(2,1)} %get-tuple-element.14.refs_8_), channel_id=1, source_target_pairs={{0,64},{32,96},{64,0},{96,32},{128,192},{160,224},{192,128},{224,1... | collective-permute-start | bytes 786440 | tf_op jit(solution)/shard_map/ppermute | solution.py:248
  19.1 18.4 %collective-permute-start.7 = (bf16[8,128,128]{2,1,0:T(8,128)(2,1)}, bf16[8,128,128]{2,1,0:T(8,128)(2,1)S(1)}, u32[]{:S(2)}, u32[]{:S(2)}) collective-permute-start(bf16[8,128,128]{2,1,0:T(8,128)(2,1)} %get-tuple-element.14.refs_8_), channel_id=1, source_target_pairs={{0,32},{32,0},{64,96},{96,64},{128,160},{160,128},{192,224},{224,1... | collective-permute-start | bytes 786440 | tf_op jit(solution)/shard_map/ppermute | solution.py:248
  29.7 8.3 %collective-permute-start.13 = (bf16[8,128,128]{2,1,0:T(8,128)(2,1)S(1)}, bf16[8,128,128]{2,1,0:T(8,128)(2,1)S(1)}, u32[]{:S(2)}, u32[]{:S(2)}) collective-permute-start(bf16[8,128,128]{2,1,0:T(8,128)(2,1)S(1)} %collective-permute-done.12.refs_14_), channel_id=1, source_target_pairs={{0,32},{32,0},{64,96},{96,64},{128,160},{160,128},{192,224},{224,1... | collective-permute-start | bytes 786440 | tf_op jit(solution)/shard_map/ppermute | solution.py:248
  31.6 7.3 %collective-permute-start.11 = (bf16[8,128,128]{2,1,0:T(8,128)(2,1)S(1)}, bf16[8,128,128]{2,1,0:T(8,128)(2,1)S(1)}, u32[]{:S(2)}, u32[]{:S(2)}) collective-permute-start(bf16[8,128,128]{2,1,0:T(8,128)(2,1)S(1)} %collective-permute-done.10.refs_12_), channel_id=1, source_target_pairs={{0,32},{32,0},{64,96},{96,64},{128,160},{160,128},{192,224},{224,1... | collective-permute-start | bytes 786440 | tf_op jit(solution)/shard_map/ppermute | solution.py:248
  31.6 15.1 %collective-permute-start.9 = (bf16[8,128,128]{2,1,0:T(8,128)(2,1)S(1)}, bf16[8,128,128]{2,1,0:T(8,128)(2,1)S(1)}, u32[]{:S(2)}, u32[]{:S(2)}) collective-permute-start(bf16[8,128,128]{2,1,0:T(8,128)(2,1)S(1)} %collective-permute-done.8.refs_10_), channel_id=1, source_target_pairs={{0,32},{32,0},{64,96},{96,64},{128,160},{160,128},{192,224},{224,1... | collective-permute-start | bytes 786440 | tf_op jit(solution)/shard_map/ppermute | solution.py:248
  34.9 7.4 %collective-permute-start.5 = (bf16[512,128]{1,0:T(8,128)(2,1)S(1)}, bf16[512,128]{1,0:T(8,128)(2,1)S(1)}, u32[]{:S(2)}, u32[]{:S(2)}) collective-permute-start(bf16[512,128]{1,0:T(8,128)(2,1)S(1)} %turn.1.refs_0_), channel_id=1, source_target_pairs={{0,192},{32,224},{64,128},{96,160},{128,64},{160,96},{192,0},{224,... | collective-permute-start | bytes 393224 | tf_op jit(solution)/shard_map/ppermute | solution.py:248
  37.4 7.4 %collective-permute-start.3 = (bf16[512,128]{1,0:T(8,128)(2,1)S(1)}, bf16[512,128]{1,0:T(8,128)(2,1)S(1)}, u32[]{:S(2)}, u32[]{:S(2)}) collective-permute-start(bf16[512,128]{1,0:T(8,128)(2,1)S(1)} %turn.1.refs_0_), channel_id=1, source_target_pairs={{0,128},{32,160},{64,192},{96,224},{128,0},{160,32},{192,64},{224,... | collective-permute-start | bytes 393224 | tf_op jit(solution)/shard_map/ppermute | solution.py:248
  38.0 8.7 %collective-permute-start.1 = (bf16[512,128]{1,0:T(8,128)(2,1)S(1)}, bf16[512,128]{1,0:T(8,128)(2,1)S(1)}, u32[]{:S(2)}, u32[]{:S(2)}) collective-permute-start(bf16[512,128]{1,0:T(8,128)(2,1)S(1)} %turn.1.refs_0_), channel_id=1, source_target_pairs={{0,64},{32,96},{64,0},{96,32},{128,192},{160,224},{192,128},{224,1... | collective-permute-start | bytes 393224 | tf_op jit(solution)/shard_map/ppermute | solution.py:248
  38.9 7.8 %collective-permute-start = (bf16[512,128]{1,0:T(8,128)(2,1)S(1)}, bf16[512,128]{1,0:T(8,128)(2,1)S(1)}, u32[]{:S(2)}, u32[]{:S(2)}) collective-permute-start(bf16[512,128]{1,0:T(8,128)(2,1)S(1)} %turn.1.refs_0_), channel_id=1, source_target_pairs={{0,32},{32,0},{64,96},{96,64},{128,160},{160,128},{192,224},{224,1... | collective-permute-start | bytes 393224 | tf_op jit(solution)/shard_map/ppermute | solution.py:248
  42.3 4.4 %collective-permute-start.6 = (bf16[512,128]{1,0:T(8,128)(2,1)S(1)}, bf16[512,128]{1,0:T(8,128)(2,1)S(1)}, u32[]{:S(2)}, u32[]{:S(2)}) collective-permute-start(bf16[512,128]{1,0:T(8,128)(2,1)S(1)} %collective-permute-done.5.refs_6_), channel_id=1, source_target_pairs={{0,32},{32,0},{64,96},{96,64},{128,160},{160,128},{192,224},{224,1... | collective-permute-start | bytes 393224 | tf_op jit(solution)/shard_map/ppermute | solution.py:248
  44.9 2.8 %collective-permute-start.4 = (bf16[512,128]{1,0:T(8,128)(2,1)S(1)}, bf16[512,128]{1,0:T(8,128)(2,1)S(1)}, u32[]{:S(2)}, u32[]{:S(2)}) collective-permute-start(bf16[512,128]{1,0:T(8,128)(2,1)S(1)} %collective-permute-done.3.refs_4_), channel_id=1, source_target_pairs={{0,32},{32,0},{64,96},{96,64},{128,160},{160,128},{192,224},{224,1... | collective-permute-start | bytes 393224 | tf_op jit(solution)/shard_map/ppermute | solution.py:248
  46.7 1.3 %collective-permute-start.2 = (bf16[512,128]{1,0:T(8,128)(2,1)S(1)}, bf16[512,128]{1,0:T(8,128)(2,1)S(1)}, u32[]{:S(2)}, u32[]{:S(2)}) collective-permute-start(bf16[512,128]{1,0:T(8,128)(2,1)S(1)} %collective-permute-done.1.refs_2_), channel_id=1, source_target_pairs={{0,32},{32,0},{64,96},{96,64},{128,160},{160,128},{192,224},{224,1... | collective-permute-start | bytes 393224 | tf_op jit(solution)/shard_map/ppermute | solution.py:248
